TPU v7x, 128 devices: a whole 4x4x4 slice. The times are simulated.
128 devices in a mesh: rows: 16 (over y, z), feat: 8 (over x, core).
Axes of the slice: x: 4, y: 4, z: 4, core: 2. Of those that a mesh axis runs over, the one named last changes fastest.
Arguments:
- features: float32 [65536, 8192], P('rows', 'feat'), may hold values from -0.0234375 to 0.0234375
- targets: float32 [32, 65536], P(None, 'rows'), may hold values from -6 to 6
- counts: int32 [16], P('rows'), may hold values from 1 to 4096, as said below
- ranks: int32 [65536], P('rows'), may hold values from 1 to 65536
Outputs:
- solution: float32 [32, 8192], P(None, 'feat')
- residual: float32 [32, 8192], P(None, 'feat')
Inputs may be any that keep to these rules, and one draw needn't show every extreme that they name: `counts`: one shard in every draw holds all 4096 slots live.
All inputs are finite; a program needn't handle non-finite values.
Results may differ from a plain program's by a relative error of at most 0.0003.
Values sent between devices are 32-bit elements; how exact they have to be, the bound alone decides.
No kernel may reach another device: no remote copies, remote signals or barrier semaphores. Data moves between devices by JAX's collectives and lax.ppermute only.
A program may use at most 64 MiB of HBM per device.

v0:
```python
import jax
import jax.numpy as jnp
from jax import lax
from jax.sharding import PartitionSpec as P

ITERS = 2


prio_power = 0.7
weight_power = 0.5
ridge_shift = 0.5


def spd_solve(matrix, rhs_block):
    matrix = 0.5 * (matrix + matrix.T)
    lower = jnp.linalg.cholesky(matrix)
    return jax.scipy.linalg.cho_solve((lower, True), rhs_block)


def row_gram(left, right):
    return lax.dot_general(left, right, (((1,), (1,)), ((), ())), precision=lax.Precision.HIGHEST)


def local(features, targets, counts, ranks):
    highest = lax.Precision.HIGHEST
    slots = features.shape[0]
    row_index = jnp.arange(slots, dtype=jnp.int32)
    live_row = row_index < counts[0]
    raw_prio = ranks.astype(jnp.float32) ** (-prio_power)
    priority = jnp.where(live_row, raw_prio, 0.0)
    total_prio, live_total = lax.psum((jnp.sum(priority), counts[0].astype(jnp.float32)), "rows")
    weights = jnp.where(live_row, (live_total * raw_prio / total_prio) ** (-weight_power), 0.0)
    rhs_field = lax.psum(jnp.dot(targets * weights[None, :], features, precision=highest), "rows")
    gram_now = lax.psum(row_gram(rhs_field, rhs_field), "feat")
    full_direction = rhs_field
    residual = rhs_field
    direction = residual
    solution = jnp.zeros_like(residual)
    for iteration in range(ITERS):
        partial_img = row_gram(full_direction, features)
        images = lax.psum(partial_img, "feat")
        weighted = images * weights[None, :]
        partial_back = jnp.dot(weighted, features, precision=highest)
        backward = lax.psum(partial_back, "rows") + ridge_shift * direction
        curvature = lax.psum(row_gram(direction, backward), "feat")
        step_size = spd_solve(curvature, gram_now)
        solution = solution + jnp.dot(step_size.T, direction, precision=highest)
        residual = residual - jnp.dot(step_size.T, backward, precision=highest)
        if iteration + 1 < ITERS:
            gram_new = lax.psum(row_gram(residual, residual), "feat")
            conj_coef = spd_solve(gram_now, gram_new)
            direction = residual + jnp.dot(conj_coef.T, direction, precision=highest)
            full_direction = direction
            gram_now = gram_new
    return (solution, residual)


def solution(mesh):
    placed = (P("rows", "feat"), P(None, "rows"), P("rows"), P("rows"))
    return jax.shard_map(
        local,
        mesh=mesh,
        in_specs=placed,
        out_specs=(P(None, "feat"), P(None, "feat")),
        check_vma=False,
    )
```

profile of v0, /device:TPU:0, one launch (start us, length us, event | category | flops | bytes accessed | tf_op | source)
XLA Modules:
  0.0 603.0 jit_solution(4634478987522612169)
XLA Ops:
  7.9 1.3 select_reduce_fusion.3
  9.2 42.7 %all-reduce = (f32[]{:T(128)}, f32[]{:T(128)}) all-reduce(f32[]{:T(128)} %select_reduce_fusion.3, f32[]{:T(128)S(6)} %convert_element_type.6), channel_id=1, replica_groups=mesh['rows'=16,'feat'=8] {'rows'}, use_global_device_ids=true, to_apply=%region_2.3 | all-reduce | flops 2 | bytes 16 | tf_op jit(solution)/shard_map/psum | solution.py:31
  51.9 2.1 power_select_fusion
  54.0 13.8 %fusion.4 = f32[32,1024]{1,0:T(8,128)} fusion(f32[4096,1024]{1,0:T(8,128)} %param.7, f32[32,4096]{1,0:T(8,128)} %param.8, f32[4096]{0:T(1024)S(1)} %power_select_fusion), kind=kOutput, calls=%fused_computation.8 | convolution fusion | flops 1610743808 | bytes 17448960 | tf_op jit(solution)/shard_map/dot_general | solution.py:33
  67.9 78.8 %all-reduce.8.cloned.1.call-done = f32[32,1024]{1,0:T(8,128)} async-done(((f32[32,1024]{1,0:T(8,128)}), f32[32,1024]{1,0:T(8,128)}) %all-reduce.8.cloned.1.call-update) | async-done | bytes 131088 | tf_op jit(solution)/shard_map/psum | solution.py:33
  146.7 21.2 %fusion.40 = f32[32,4096]{1,0:T(8,128)} fusion(f32[32,1024]{1,0:T(8,128)} %all-reduce.8.cloned.1.call-done, f32[4096,1024]{1,0:T(8,128)} %param.7), kind=kOutput, calls=%fused_computation.67 | convolution fusion | flops 1610612736 | bytes 17432576 | tf_op jit(solution)/shard_map/dot_general | solution.py:21
  168.2 59.8 %all-reduce.10.cloned.1.call-done = f32[32,4096]{1,0:T(8,128)} async-done(((f32[32,4096]{1,0:T(8,128)}), f32[32,4096]{1,0:T(8,128)}) %all-reduce.10.cloned.1.call-update) | async-done | bytes 524304 | tf_op jit(solution)/shard_map/psum | solution.py:41
  228.0 13.8 %fusion.2 = f32[32,1024]{1,0:T(8,128)} fusion(f32[4096,1024]{1,0:T(8,128)} %param.7, f32[32,4096]{1,0:T(8,128)} %all-reduce.10.cloned.1.call-done, f32[4096]{0:T(1024)S(1)} %power_select_fusion), kind=kOutput, calls=%fused_computation.6 | convolution fusion | flops 1610743808 | bytes 17448960 | tf_op jit(solution)/shard_map/dot_general | solution.py:43
  242.1 81.5 %all-reduce.12.cloned.1.call-done = f32[32,1024]{1,0:T(8,128)} async-done(((f32[32,1024]{1,0:T(8,128)}), f32[32,1024]{1,0:T(8,128)}) %all-reduce.12.cloned.1.call-update) | async-done | bytes 131088 | tf_op jit(solution)/shard_map/psum | solution.py:44
  323.6 1.2 fusion.9
  324.8 24.0 %all-reduce.1 = (f32[32,32]{1,0:T(8,128)S(1)}, f32[32,32]{1,0:T(8,128)S(1)}) all-reduce(f32[32,32]{1,0:T(8,128)S(1)} %fusion.41, f32[32,32]{1,0:T(8,128)S(1)} %fusion.9), channel_id=1, replica_groups=mesh['rows'=16,'feat'=8] {'feat'}, use_global_device_ids=true, to_apply=%region_9.11 | all-reduce | flops 2048 | bytes 16384 | tf_op jit(solution)/shard_map/psum | solution.py:34
  349.0 2.9 cholesky.70
  352.0 0.6 compare_reduce_fusion.1
  352.6 0.7 fusion.16
  353.3 2.4 custom-call.10
  355.8 2.9 cholesky.59
  359.4 0.7 fusion.15
  360.1 2.4 custom-call.9
  362.9 1.2 convolution_subtract_fusion.1
  364.4 23.8 %psum.84 = f32[32,32]{1,0:T(8,128)S(1)} all-reduce(f32[32,32]{1,0:T(8,128)S(1)} %fusion.43), channel_id=1, replica_groups=mesh['rows'=16,'feat'=8] {'feat'}, use_global_device_ids=true, to_apply=%region_10.13 | all-reduce | flops 1024 | bytes 8192 | tf_op jit(solution)/shard_map/psum | solution.py:50
  388.9 19.3 %fusion.44 = f32[32,4096]{1,0:T(8,128)} fusion(f32[32,1024]{1,0:T(8,128)S(1)} %convolution_add_fusion.1, f32[4096,1024]{1,0:T(8,128)} %param.7), kind=kOutput, calls=%fused_computation.71 | convolution fusion | flops 1610612736 | bytes 17432576 | tf_op jit(solution)/shard_map/dot_general | solution.py:21
  408.2 57.3 %all-reduce.14.cloned.1.call-done = f32[32,4096]{1,0:T(8,128)} async-done(((f32[32,4096]{1,0:T(8,128)}), f32[32,4096]{1,0:T(8,128)}) %all-reduce.14.cloned.1.call-update) | async-done | bytes 524304 | tf_op jit(solution)/shard_map/psum | solution.py:41
  465.5 13.8 %fusion = f32[32,1024]{1,0:T(8,128)} fusion(f32[4096,1024]{1,0:T(8,128)} %param.7, f32[32,4096]{1,0:T(8,128)} %all-reduce.14.cloned.1.call-done, f32[4096]{0:T(1024)S(1)} %power_select_fusion), kind=kOutput, calls=%fused_computation.4 | convolution fusion | flops 1610743808 | bytes 17448960 | tf_op jit(solution)/shard_map/dot_general | solution.py:43
  479.6 81.5 %all-reduce.16.cloned.1.call-done = f32[32,1024]{1,0:T(8,128)} async-done(((f32[32,1024]{1,0:T(8,128)}), f32[32,1024]{1,0:T(8,128)}) %all-reduce.16.cloned.1.call-update) | async-done | bytes 131088 | tf_op jit(solution)/shard_map/psum | solution.py:44
  561.2 1.2 fusion.10
  562.3 24.0 %psum.87 = f32[32,32]{1,0:T(8,128)S(1)} all-reduce(f32[32,32]{1,0:T(8,128)S(1)} %fusion.10), channel_id=1, replica_groups=mesh['rows'=16,'feat'=8] {'feat'}, use_global_device_ids=true, to_apply=%region_13.16 | all-reduce | flops 1024 | bytes 8192 | tf_op jit(solution)/shard_map/psum | solution.py:45
  586.5 2.9 cholesky.81
  589.4 0.6 compare_reduce_fusion
  590.1 0.7 fusion.17
  590.7 2.4 custom-call.11
  593.6 1.0 convolution_add_fusion
  594.6 1.9 convolution_subtract_fusion
  (37 shorter events, 3.9 us)
Async XLA Ops:
  7.2 139.5 %all-reduce.8.cloned.1.call-start = ((), (), s32[]{:S(2)}) async-start(), calls=%async_computation | async-start | bytes 262144 | tf_op jit(solution)/shard_map/psum | solution.py:33
  67.9 160.1 %all-reduce.10.cloned.1.call-start = ((), (), s32[]{:S(2)}) async-start(), calls=%async_computation.1 | async-start | bytes 1048576 | tf_op jit(solution)/shard_map/psum | solution.py:41
  146.7 95.2 %copy-start = (f32[32,1024]{1,0:T(8,128)S(1)}, f32[32,1024]{1,0:T(8,128)}, u32[]{:S(2)}) copy-start(f32[32,1024]{1,0:T(8,128)} %all-reduce.8.cloned.1.call-done) | copy-start | bytes 393220
  168.0 155.7 %all-reduce.12.cloned.1.call-start = ((), (), s32[]{:S(2)}) async-start(), calls=%async_computation.2 | async-start | bytes 262144 | tf_op jit(solution)/shard_map/psum | solution.py:44
  241.8 223.7 %all-reduce.14.cloned.1.call-start = ((), (), s32[]{:S(2)}) async-start(), calls=%async_computation.3 | async-start | bytes 1048576 | tf_op jit(solution)/shard_map/psum | solution.py:41
  408.2 153.0 %all-reduce.16.cloned.1.call-start = ((), (), s32[]{:S(2)}) async-start(), calls=%async_computation.4 | async-start | bytes 262144 | tf_op jit(solution)/shard_map/psum | solution.py:44
Sparse Core Ops, SparseCore 0:
  68.0 78.6 all-reduce.7
  168.1 59.8 all-reduce.9
  241.9 81.6 all-reduce.11
  408.3 57.1 all-reduce.13
  479.4 81.6 all-reduce.15
where the time goes:
time: 603 us
  waiting for transfers between devices  359 us (60%)
  blocking collectives  115 us (19%)
  matrix products  90.5 us (15%)
  other arithmetic  23.5 us (4%)
  between operations  14.6 us (2%)
    psum x2, waiting for transfers between devices, local(): backward = lax.psum(partial_back, 'rows') + ridge_shift * direction  163 us
    psum x2, waiting for transfers between devices, local(): images = lax.psum(partial_img, 'feat')  117 us
    psum x1, waiting for transfers between devices, local(): lax.psum(jnp.dot(targets * weights[None, :], features, precision=highest)...  78.8 us
    dot_general x6, matrix products, row_gram(): lax.dot_general(left, right, (((1,), (1,)), ((), ())), precision=lax.Prec...  43.3 us
    psum x1, blocking collectives, local(): lax.psum((jnp.sum(priority), counts[0].astype(jnp.float32)), 'rows')  42.7 us
    dot_general x2, matrix products, local(): partial_back = jnp.dot(weighted, features, precision=highest)  27.6 us
    psum x1, blocking collectives, local(): gram_now = lax.psum(row_gram(rhs_field, rhs_field), 'feat')  24 us
    psum x1, blocking collectives, local(): curvature = lax.psum(row_gram(direction, backward), 'feat')  24 us
  transfers between devices with their start and end apart: 5, of which 5 were waited for; matrix products, arithmetic and copies ran while one was open for 0% of the time, Pallas kernels for 0%

commit v1 on v0

v1 whole, which is shorter than its diff:
```python
import functools

import jax
import jax.numpy as jnp
from jax import lax
from jax.experimental import pallas as pl
from jax.experimental.pallas import tpu as pltpu
from jax.sharding import PartitionSpec as P


K = 32
HALF = K // 2
EXTRA = 128
XCHIPS = 4
CHUNK = 512
BUFFERS = 4
prio_power = 0.7
weight_power = 0.5
ridge_shift = 0.5
f32, bf16 = jnp.float32, jnp.bfloat16
IN_VMEM = pl.BlockSpec(memory_space=pltpu.VMEM)
IN_SMEM = pl.BlockSpec(memory_space=pltpu.SMEM)
ANYWHERE = pl.BlockSpec(memory_space=pl.ANY)
ROWS_BY_ROWS = (((1,), (1,)), ((), ()))


def split(value):
    high = value.astype(bf16)
    return high, (value - high.astype(f32)).astype(bf16)


def exact(left, right):
    return jnp.dot(left, right, precision=lax.Precision.HIGHEST, preferred_element_type=f32)


def row_gram(left, right):
    return lax.dot_general(left, right, ROWS_BY_ROWS, precision=lax.Precision.HIGHEST, preferred_element_type=f32)


def solve_t(matrix, rhs_block):
    matrix = 0.5 * (matrix + matrix.T)
    table = jnp.concatenate([matrix, rhs_block], axis=1)
    row_id = lax.broadcasted_iota(jnp.int32, (K, 1), 0)
    for k in range(K):
        row = table[k : k + 1, :] / table[k : k + 1, k : k + 1]
        table = jnp.where(row_id == k, row, table - table[:, k : k + 1] * row)
    return table[:, K:].T


def merged(parts):
    a, b, c, d = (part[...] for part in parts)
    return (a + b) + (c + d)


def k1(count, ranks_any, targets_any, features, high, low, scale, out, buf, targets, ranks, pair, sem, in_sem):
    slots, width = features.shape
    steps = slots // CHUNK
    small = [
        pltpu.make_async_copy(ranks_any, ranks, in_sem.at[0]),
        pltpu.make_async_copy(targets_any, targets, in_sem.at[1]),
    ]
    copies = [
        pltpu.make_async_copy(features.at[pl.ds(c * CHUNK, CHUNK)], buf.at[c % BUFFERS], sem.at[c % BUFFERS])
        for c in range(steps)
    ]
    for copy in small:
        copy.start()
    for c in range(BUFFERS):
        copies[c].start()
    live = lax.broadcasted_iota(jnp.int32, (1, slots), 1) < count[0]
    small[0].wait()
    log_rank = jnp.log(ranks[...].astype(f32))
    scale_now = jnp.where(live, jnp.exp((prio_power * weight_power) * log_rank), 0.0)
    scale[...] = scale_now
    prio_sum = jnp.sum(jnp.where(live, jnp.exp(-prio_power * log_rank), 0.0))
    small[1].wait()
    high_t, low_t = split(targets[...] * scale_now)
    pair[0:K, :] = high_t
    pair[K : 2 * K, :] = low_t
    total = jnp.zeros((2 * K, width), f32)
    rest = jnp.zeros((K, width), f32)
    for c in range(steps):
        at = slice(c * CHUNK, (c + 1) * CHUNK)
        copies[c].wait()
        high_f, low_f = split(buf[c % BUFFERS])
        if c + BUFFERS < steps:
            copies[c + BUFFERS].start()
        high[at, :] = high_f
        low[at, :] = low_f
        total += jnp.dot(pair[:, at], high_f, preferred_element_type=f32)
        rest += jnp.dot(pair[0:K, at], low_f, preferred_element_type=f32)
    out[:, 0:width] = total[0:K] + total[K:] + rest
    row = lax.broadcasted_iota(jnp.int32, (K, EXTRA), 0)
    col = lax.broadcasted_iota(jnp.int32, (K, EXTRA), 1)
    tail = jnp.where(col == 0, prio_sum, jnp.where(col == 1, count[0].astype(f32), 0.0))
    out[:, width:] = jnp.where(row == 0, tail, 0.0)


def put_images(field, gram, high, low, mine, other):
    place = lax.axis_index("feat")
    x, first = place // 2, place % 2 == 0
    slots = high.shape[0]
    part = slots // XCHIPS
    high_v, low_v = split(field)
    pair = jnp.concatenate([high_v, low_v], axis=0)
    blank = jnp.zeros((K, EXTRA - gram.shape[1]), f32)
    gram = jnp.concatenate([gram, blank], axis=1)
    for c in range(XCHIPS):
        slot = x ^ c
        for piece in range(part // CHUNK):
            at = slice(c * part + piece * CHUNK, c * part + (piece + 1) * CHUNK)
            to = slice(piece * CHUNK, (piece + 1) * CHUNK)
            both = lax.dot_general(pair, high[at, :], ROWS_BY_ROWS, preferred_element_type=f32)
            rest = lax.dot_general(high_v, low[at, :], ROWS_BY_ROWS, preferred_element_type=f32)
            value = both[0:K] + both[K:] + rest
            mine[slot, :, to] = jnp.where(first, value[0:HALF], value[HALF:])
            other[slot, :, to] = jnp.where(first, value[HALF:], value[0:HALF])
        tail = gram if c == 0 else jnp.zeros_like(gram)
        mine[slot, :, part:] = jnp.where(first, tail[0:HALF], tail[HALF:])
        other[slot, :, part:] = jnp.where(first, tail[HALF:], tail[0:HALF])


def k2(p0, p1, p2, p3, high, low, field, norm, mine, other):
    width = high.shape[1]
    total = merged((p0, p1, p2, p3))
    factor = jnp.sqrt(total[0:1, width : width + 1] / total[0:1, width + 1 : width + 2])
    norm[...] = jnp.broadcast_to(factor, norm.shape)
    rhs_field = total[:, 0:width] * factor
    field[...] = rhs_field
    put_images(rhs_field, row_gram(rhs_field, rhs_field), high, low, mine, other)


def get_images(near, far):
    first = lax.axis_index("feat") % 2 == 0
    out = []
    for j, ref in enumerate(near):
        a, b = ref[...], far[j]
        out.append(jnp.concatenate([jnp.where(first, a, b), jnp.where(first, b, a)], axis=0))
    return out


def owned(chunks, part):
    x = lax.axis_index("feat") // 2
    tail = chunks[0][:, part:]
    for j in range(1, XCHIPS):
        tail = jnp.where(x == j, chunks[j][:, part:], tail)
    return tail


def back_project(images, scale, high, low, out):
    x = lax.axis_index("feat") // 2
    part, width = images[0].shape[1], high.shape[1]
    total = jnp.zeros((2 * K, width), f32)
    rest = jnp.zeros((K, width), f32)
    curve = jnp.zeros((2 * K, 2 * K), f32)
    for j in range(XCHIPS):
        base = pl.multiple_of((x ^ j) * part, part)
        weighted = images[j] * scale[:, pl.ds(base, part)]
        high_w, low_w = split(weighted)
        high_i, low_i = split(images[j])
        pair = jnp.concatenate([high_w, low_w], axis=0)
        curve += lax.dot_general(pair, jnp.concatenate([high_i, low_i], axis=0), ROWS_BY_ROWS, preferred_element_type=f32)
        for piece in range(part // CHUNK):
            at = pl.ds(pl.multiple_of(base + piece * CHUNK, CHUNK), CHUNK)
            to = slice(piece * CHUNK, (piece + 1) * CHUNK)
            total += jnp.dot(pair[:, to], high[at, :], preferred_element_type=f32)
            rest += jnp.dot(high_w[:, to], low[at, :], preferred_element_type=f32)
    out[:, 0:width] = total[0:K] + total[K:] + rest
    curve = curve[0:K, 0:K] + curve[0:K, K:] + curve[K:, 0:K]
    out[:, width:] = jnp.concatenate([curve, jnp.zeros((K, EXTRA - K), f32)], axis=1)


def k3(n0, n1, n2, n3, far, scale, high, low, out, kept, gram):
    part = kept.shape[2]
    chunks = get_images((n0, n1, n2, n3), far)
    gram[...] = owned(chunks, part)[:, 0:K]
    images = [chunk[:, 0:part] for chunk in chunks]
    for j in range(XCHIPS):
        kept[j] = images[j]
    back_project(images, scale, high, low, out)


def k4(z0, z1, z2, z3, field, norm, gram, high, low, residual, step, mine, other):
    width = high.shape[1]
    total = merged((z0, z1, z2, z3)) * norm[0:1, 0:1]
    backward = total[:, 0:width] + ridge_shift * field[...]
    curvature = total[:, width : width + K] + ridge_shift * gram[...]
    step_t = solve_t(curvature, gram[...])
    step[...] = step_t
    now = field[...] - exact(step_t, backward)
    residual[...] = now
    grams = jnp.concatenate([row_gram(now, now), row_gram(now, field[...])], axis=1)
    put_images(now, grams, high, low, mine, other)


def k5(n0, n1, n2, n3, far, kept, gram, scale, high, low, out, coef, grams):
    part = kept.shape[2]
    chunks = get_images((n0, n1, n2, n3), far)
    tail = owned(chunks, part)
    grams[...] = tail[:, 0 : 2 * K]
    coef_t = solve_t(gram[...], tail[:, 0:K])
    coef[...] = coef_t
    images = [chunk[:, 0:part] + exact(coef_t, kept[j]) for j, chunk in enumerate(chunks)]
    back_project(images, scale, high, low, out)


def k6(z0, z1, z2, z3, field, residual, norm, gram, grams, step, coef, solution_out, residual_out):
    width = field.shape[1]
    coef_t = coef[...]
    gram_new, cross = grams[:, 0:K], grams[:, K : 2 * K]
    mixed = row_gram(cross, coef_t)
    square = gram_new + mixed + mixed.T + row_gram(exact(coef_t, gram[...]), coef_t)
    total = merged((z0, z1, z2, z3)) * norm[0:1, 0:1]
    direction = residual[...] + exact(coef_t, field[...])
    backward = total[:, 0:width] + ridge_shift * direction
    curvature = total[:, width : width + K] + ridge_shift * square
    step_t = solve_t(curvature, gram_new)
    solution_out[...] = exact(step[...], field[...]) + exact(step_t, direction)
    residual_out[...] = residual[...] - exact(step_t, backward)


def call(kernel, outs, operands, specs=None, scratch=(), limit=24):
    return pl.pallas_call(
        kernel,
        out_shape=outs,
        in_specs=specs or [IN_VMEM] * len(operands),
        out_specs=[IN_VMEM] * len(outs),
        scratch_shapes=scratch,
        compiler_params=pltpu.CompilerParams(vmem_limit_bytes=limit << 20),
        name=kernel.__name__,
    )(*operands)


def exchange(value, axis, size, distance):
    return lax.ppermute(value, axis, [(i, i ^ distance) for i in range(size)])


def gather_rows(value):
    near = [value] + [exchange(value, "rows", 16, d) for d in (1, 2, 3)]
    value = (near[0] + near[1]) + (near[2] + near[3])
    return [value] + [exchange(value, "rows", 16, d) for d in (4, 8, 12)]


def sum_feat(mine, other):
    value = mine + exchange(other, "feat", 8, 1)
    got = [value[0]] + [exchange(value[j], "feat", 8, 2 * j) for j in (1, 2, 3)]
    value = (got[0] + got[1]) + (got[2] + got[3])
    near = [value] + [exchange(value, "feat", 8, 2 * j) for j in (1, 2, 3)]
    far = exchange(jnp.stack(near), "feat", 8, 1)
    return [*near, far]


def local(features, targets, counts, ranks):
    slots, width = features.shape
    part = slots // XCHIPS
    shape = jax.ShapeDtypeStruct
    summed = shape((K, width + EXTRA), f32)
    field_like, small = shape((K, width), f32), shape((K, K), f32)
    images_like = [shape((XCHIPS, HALF, part + EXTRA), f32)] * 2
    high, low, scale, out = call(
        k1,
        [pltpu.VMEM((slots, width), bf16), pltpu.VMEM((slots, width), bf16), shape((1, slots), f32), summed],
        (counts, ranks.reshape(1, slots), targets, features),
        [IN_SMEM, ANYWHERE, ANYWHERE, ANYWHERE],
        (
            pltpu.VMEM((BUFFERS, CHUNK, width), f32),
            pltpu.VMEM((K, slots), f32),
            pltpu.VMEM((1, slots), jnp.int32),
            pltpu.VMEM((2 * K, slots), bf16),
            pltpu.SemaphoreType.DMA((BUFFERS,)),
            pltpu.SemaphoreType.DMA((2,)),
        ),
    )
    parts = gather_rows(out)
    field, norm, mine, other = call(k2, [field_like, shape((8, 128), f32), *images_like], (*parts, high, low))
    parts = sum_feat(mine, other)
    out, kept, gram = call(
        k3, [summed, shape((XCHIPS, K, part), f32), small], (*parts, scale, high, low)
    )
    parts = gather_rows(out)
    residual, step, mine, other = call(
        k4, [field_like, small, *images_like], (*parts, field, norm, gram, high, low)
    )
    parts = sum_feat(mine, other)
    out, coef, grams = call(
        k5, [summed, small, shape((K, 2 * K), f32)], (*parts, kept, gram, scale, high, low)
    )
    parts = gather_rows(out)
    return tuple(
        call(k6, [field_like, field_like], (*parts, field, residual, norm, gram, grams, step, coef))
    )


def solution(mesh):
    placed = (P("rows", "feat"), P(None, "rows"), P("rows"), P("rows"))
    return jax.shard_map(
        local,
        mesh=mesh,
        in_specs=placed,
        out_specs=(P(None, "feat"), P(None, "feat")),
        check_vma=False,
    )
```

time: 603 us -> 141 us (0.23)
  waiting for transfers between devices: 359 us -> 60 us
  blocking collectives: 115 us -> 0 us
  matrix products: 90.5 us -> 0 us
  starting transfers between devices: 0.39 us -> 43.4 us
  Pallas kernels: 0 us -> 34 us
  other arithmetic: 23.5 us -> 0.24 us
  between operations: 14.6 us -> 1.44 us
    psum x5 -> x0, waiting for transfers between devices: 359 us -> none  [the longest x2 163 us: local(): backward = lax.psum(partial_back, 'rows') + ridge_shift * direction]
    psum x4 -> x0, blocking collectives: 115 us -> none  [the longest x1 42.7 us: local(): lax.psum((jnp.sum(priority), counts[0].astype(jnp.float32)), 'rows')]
    dot_general x14 -> x0, matrix products: 89.4 us -> none  [the longest x6 43.3 us: row_gram(): lax.dot_general(left, right, (((1,), (1,)), ((), ())), precision=lax.Prec...]
    ppermute x0 -> x34, waiting for transfers between devices: none -> 60 us  [exchange(): return lax.ppermute(value, axis, [(i, i ^ distance) for i in range(size)])]
    ppermute x0 -> x34, starting transfers between devices: none -> 43.4 us  [exchange(): return lax.ppermute(value, axis, [(i, i ^ distance) for i in range(size)])]
    pallas_call x0 -> x6, Pallas kernels: none -> 34 us  [call(): pl.pallas_call(kernel, out_shape=outs, in_specs=specs or [IN_VMEM] * len(...]
    another operation x15 -> x2, other arithmetic: 20.1 us -> 0.04 us  [sum_feat(): far = exchange(jnp.stack(near), 'feat', 8, 1)]
  transfers between devices with their start and end apart: 5 -> 34, of which waited for: 5 -> 24; matrix products, arithmetic and copies ran while one was open for 0% -> 0% of each run, Pallas kernels for 0% -> 0%
where the time goes in v1:
time: 141 us
  waiting for transfers between devices  60 us (43%)
  starting transfers between devices  43.4 us (31%)
  Pallas kernels  34 us (24%)
  local copies, waits for them, and re-layouts  1.79 us (1%)
  between operations  1.44 us (1%)
    ppermute x34, waiting for transfers between devices, exchange(): return lax.ppermute(value, axis, [(i, i ^ distance) for i in range(size)])  60 us
    ppermute x34, starting transfers between devices, exchange(): return lax.ppermute(value, axis, [(i, i ^ distance) for i in range(size)])  43.4 us
    pallas_call x6, Pallas kernels, call(): pl.pallas_call(kernel, out_shape=outs, in_specs=specs or [IN_VMEM] * len(...  34 us
  transfers between devices with their start and end apart: 34, of which 24 were waited for; matrix products, arithmetic and copies ran while one was open for 0% of the time, Pallas kernels for 0%

profile of v1, /device:TPU:0, one launch (start us, length us, event | category | flops | bytes accessed | tf_op | source)
XLA Modules:
  0.0 140.9 jit_solution(129927833618956925)
XLA Ops:
  3.0 6.8 %k1.1 = (bf16[4096,1024]{1,0:T(8,128)(2,1)S(1)}, bf16[4096,1024]{1,0:T(8,128)(2,1)S(1)}, f32[1,4096]{1,0:T(1,128)S(1)}, f32[32,1152]{1,0:T(8,128)S(1)}) custom-call(s32[1]{0:T(128)S(6)} %copy.6.count, s32[1,4096]{1,0:T(1,128)S(1)} %bitcast.41, f32[32,4096]{1,0:T(8,128)S(1)} %copy-done, f32[4096,1024]{1,0:T(8,128)} %features.1), custom_call_target="tpu_custom_call" | custom-call | tf_op jit(solution)/shard_map/k1/pallas_call | solution.py:223
  9.8 4.2 %collective-permute-start.2 = (f32[32,1152]{1,0:T(8,128)S(1)}, f32[32,1152]{1,0:T(8,128)S(1)}, u32[]{:S(2)}, u32[]{:S(2)}) collective-permute-start(f32[32,1152]{1,0:T(8,128)S(1)} %get-tuple-element.20), channel_id=1, source_target_pairs={{0,24},{8,16},{16,8},{24,0},{32,56},{40,48},{48,40},{56,32},{64,88... | collective-permute-start | bytes 442376 | tf_op jit(solution)/shard_map/ppermute | solution.py:235
  15.0 5.3 %collective-permute-done.2 = f32[32,1152]{1,0:T(8,128)S(1)} collective-permute-done((f32[32,1152]{1,0:T(8,128)S(1)}, f32[32,1152]{1,0:T(8,128)S(1)}, u32[]{:S(2)}, u32[]{:S(2)}) %collective-permute-start.2) | collective-permute-done | bytes 147488 | tf_op jit(solution)/shard_map/ppermute | solution.py:235
  20.3 2.0 %collective-permute-done.1 = f32[32,1152]{1,0:T(8,128)S(1)} collective-permute-done((f32[32,1152]{1,0:T(8,128)S(1)}, f32[32,1152]{1,0:T(8,128)S(1)}, u32[]{:S(2)}, u32[]{:S(2)}) %collective-permute-start.1) | collective-permute-done | bytes 147488 | tf_op jit(solution)/shard_map/ppermute | solution.py:235
  22.4 3.1 %collective-permute-start.5 = (f32[32,1152]{1,0:T(8,128)S(1)}, f32[32,1152]{1,0:T(8,128)S(1)}, u32[]{:S(2)}, u32[]{:S(2)}) collective-permute-start(f32[32,1152]{1,0:T(8,128)S(1)} %add_add_fusion.2.p0), channel_id=1, source_target_pairs={{0,96},{8,104},{16,112},{24,120},{32,64},{40,72},{48,80},{56,88},{... | collective-permute-start | bytes 442376 | tf_op jit(solution)/shard_map/ppermute | solution.py:235
  26.5 3.8 %collective-permute-done.5.p3 = f32[32,1152]{1,0:T(8,128)S(1)} collective-permute-done((f32[32,1152]{1,0:T(8,128)S(1)}, f32[32,1152]{1,0:T(8,128)S(1)}, u32[]{:S(2)}, u32[]{:S(2)}) %collective-permute-start.5) | collective-permute-done | bytes 147488 | tf_op jit(solution)/shard_map/ppermute | solution.py:235
  30.4 2.1 %collective-permute-done.4.p2 = f32[32,1152]{1,0:T(8,128)S(1)} collective-permute-done((f32[32,1152]{1,0:T(8,128)S(1)}, f32[32,1152]{1,0:T(8,128)S(1)}, u32[]{:S(2)}, u32[]{:S(2)}) %collective-permute-start.4) | collective-permute-done | bytes 147488 | tf_op jit(solution)/shard_map/ppermute | solution.py:235
  32.5 5.2 %k2.1 = (f32[32,1024]{1,0:T(8,128)S(1)}, f32[8,128]{1,0:T(8,128)S(1)}, f32[4,16,1152]{2,1,0:T(8,128)S(1)}, f32[4,16,1152]{2,1,0:T(8,128)S(1)}) custom-call(f32[32,1152]{1,0:T(8,128)S(1)} %add_add_fusion.2.p0, f32[32,1152]{1,0:T(8,128)S(1)} %collective-permute-done.3.p1, f32[32,1152]{1,0:T(8,128)S(1)} %collective-permute-done.4.p2, ...), custom_call_target="tpu_custom_call" | custom-call | tf_op jit(solution)/shard_map/k2/pallas_call | solution.py:223
  39.5 2.8 %collective-permute-start.9 = (f32[16,1152]{1,0:T(8,128)S(1)}, f32[16,1152]{1,0:T(8,128)S(1)}, u32[]{:S(2)}, u32[]{:S(2)}) collective-permute-start(f32[16,1152]{1,0:T(8,128)S(1)} %get-tuple-element.41), channel_id=1, source_target_pairs={{0,6},{1,7},{2,4},{3,5},{4,2},{5,3},{6,0},{7,1},{8,14},{9,15},{10,... | collective-permute-start | bytes 221192 | tf_op jit(solution)/shard_map/ppermute | solution.py:235
  43.6 2.0 %collective-permute-done.9 = f32[16,1152]{1,0:T(8,128)S(1)} collective-permute-done((f32[16,1152]{1,0:T(8,128)S(1)}, f32[16,1152]{1,0:T(8,128)S(1)}, u32[]{:S(2)}, u32[]{:S(2)}) %collective-permute-start.9) | collective-permute-done | bytes 73760 | tf_op jit(solution)/shard_map/ppermute | solution.py:235
  45.6 3.0 %collective-permute-done.8 = f32[16,1152]{1,0:T(8,128)S(1)} collective-permute-done((f32[16,1152]{1,0:T(8,128)S(1)}, f32[16,1152]{1,0:T(8,128)S(1)}, u32[]{:S(2)}, u32[]{:S(2)}) %collective-permute-start.8) | collective-permute-done | bytes 73760 | tf_op jit(solution)/shard_map/ppermute | solution.py:235
  51.1 1.7 %collective-permute-start.10 = (f32[16,1152]{1,0:T(8,128)S(1)}, f32[16,1152]{1,0:T(8,128)S(1)}, u32[]{:S(2)}, u32[]{:S(2)}) collective-permute-start(f32[16,1152]{1,0:T(8,128)S(1)} %fusion.3.n0), channel_id=1, source_target_pairs={{0,2},{1,3},{2,0},{3,1},{4,6},{5,7},{6,4},{7,5},{8,10},{9,11},{10,... | collective-permute-start | bytes 221192 | tf_op jit(solution)/shard_map/ppermute | solution.py:235
  52.8 1.6 %collective-permute-done.12.n3 = f32[16,1152]{1,0:T(8,128)S(1)} collective-permute-done((f32[16,1152]{1,0:T(8,128)S(1)}, f32[16,1152]{1,0:T(8,128)S(1)}, u32[]{:S(2)}, u32[]{:S(2)}) %collective-permute-start.12) | collective-permute-done | bytes 73760 | tf_op jit(solution)/shard_map/ppermute | solution.py:235
  57.8 3.0 %k3.1 = (f32[32,1152]{1,0:T(8,128)S(1)}, f32[4,32,1024]{2,1,0:T(8,128)S(1)}, f32[32,32]{1,0:T(8,128)S(1)}) custom-call(f32[16,1152]{1,0:T(8,128)S(1)} %fusion.3.n0, f32[16,1152]{1,0:T(8,128)S(1)} %collective-permute-done.10.n1, f32[16,1152]{1,0:T(8,128)S(1)} %collective-permute-done.11.n2, f32[16,1152]{1,0:T(8,128)S(1)} %collective-permute-done.12.n3, ...), custom_call_target="tpu_custom_call" | custom-call | tf_op jit(solution)/shard_map/k3/pallas_call | solution.py:223
  60.8 2.9 %collective-permute-start.16 = (f32[32,1152]{1,0:T(8,128)S(1)}, f32[32,1152]{1,0:T(8,128)S(1)}, u32[]{:S(2)}, u32[]{:S(2)}) collective-permute-start(f32[32,1152]{1,0:T(8,128)S(1)} %get-tuple-element.26), channel_id=1, source_target_pairs={{0,24},{8,16},{16,8},{24,0},{32,56},{40,48},{48,40},{56,32},{64,88... | collective-permute-start | bytes 442376 | tf_op jit(solution)/shard_map/ppermute | solution.py:235
  65.0 5.3 %collective-permute-done.16 = f32[32,1152]{1,0:T(8,128)S(1)} collective-permute-done((f32[32,1152]{1,0:T(8,128)S(1)}, f32[32,1152]{1,0:T(8,128)S(1)}, u32[]{:S(2)}, u32[]{:S(2)}) %collective-permute-start.16) | collective-permute-done | bytes 147488 | tf_op jit(solution)/shard_map/ppermute | solution.py:235
  70.3 1.7 %collective-permute-done.15 = f32[32,1152]{1,0:T(8,128)S(1)} collective-permute-done((f32[32,1152]{1,0:T(8,128)S(1)}, f32[32,1152]{1,0:T(8,128)S(1)}, u32[]{:S(2)}, u32[]{:S(2)}) %collective-permute-start.15) | collective-permute-done | bytes 147488 | tf_op jit(solution)/shard_map/ppermute | solution.py:235
  72.0 2.2 %collective-permute-start.19 = (f32[32,1152]{1,0:T(8,128)S(1)}, f32[32,1152]{1,0:T(8,128)S(1)}, u32[]{:S(2)}, u32[]{:S(2)}) collective-permute-start(f32[32,1152]{1,0:T(8,128)S(1)} %add_add_fusion.1.z0), channel_id=1, source_target_pairs={{0,96},{8,104},{16,112},{24,120},{32,64},{40,72},{48,80},{56,88},{... | collective-permute-start | bytes 442376 | tf_op jit(solution)/shard_map/ppermute | solution.py:235
  76.2 4.4 %collective-permute-done.19.z3 = f32[32,1152]{1,0:T(8,128)S(1)} collective-permute-done((f32[32,1152]{1,0:T(8,128)S(1)}, f32[32,1152]{1,0:T(8,128)S(1)}, u32[]{:S(2)}, u32[]{:S(2)}) %collective-permute-start.19) | collective-permute-done | bytes 147488 | tf_op jit(solution)/shard_map/ppermute | solution.py:235
  81.7 8.2 %k4.1 = (f32[32,1024]{1,0:T(8,128)S(1)}, f32[32,32]{1,0:T(8,128)S(1)}, f32[4,16,1152]{2,1,0:T(8,128)S(1)}, f32[4,16,1152]{2,1,0:T(8,128)S(1)}) custom-call(f32[32,1152]{1,0:T(8,128)S(1)} %add_add_fusion.1.z0, f32[32,1152]{1,0:T(8,128)S(1)} %collective-permute-done.17.z1, f32[32,1152]{1,0:T(8,128)S(1)} %collective-permute-done.18.z2, ...), custom_call_target="tpu_custom_call" | custom-call | tf_op jit(solution)/shard_map/k4/pallas_call | solution.py:223
  91.6 2.0 %collective-permute-start.23 = (f32[16,1152]{1,0:T(8,128)S(1)}, f32[16,1152]{1,0:T(8,128)S(1)}, u32[]{:S(2)}, u32[]{:S(2)}) collective-permute-start(f32[16,1152]{1,0:T(8,128)S(1)} %get-tuple-element.38), channel_id=1, source_target_pairs={{0,6},{1,7},{2,4},{3,5},{4,2},{5,3},{6,0},{7,1},{8,14},{9,15},{10,... | collective-permute-start | bytes 221192 | tf_op jit(solution)/shard_map/ppermute | solution.py:235
  97.2 2.7 %collective-permute-done.22 = f32[16,1152]{1,0:T(8,128)S(1)} collective-permute-done((f32[16,1152]{1,0:T(8,128)S(1)}, f32[16,1152]{1,0:T(8,128)S(1)}, u32[]{:S(2)}, u32[]{:S(2)}) %collective-permute-start.22) | collective-permute-done | bytes 73760 | tf_op jit(solution)/shard_map/ppermute | solution.py:235
  99.9 1.6 %collective-permute-start.26 = (f32[16,1152]{1,0:T(8,128)S(1)}, f32[16,1152]{1,0:T(8,128)S(1)}, u32[]{:S(2)}, u32[]{:S(2)}) collective-permute-start(f32[16,1152]{1,0:T(8,128)S(1)} %fusion.1.n0), channel_id=1, source_target_pairs={{0,6},{1,7},{2,4},{3,5},{4,2},{5,3},{6,0},{7,1},{8,14},{9,15},{10,... | collective-permute-start | bytes 221192 | tf_op jit(solution)/shard_map/ppermute | solution.py:235
  104.1 1.6 %collective-permute-done.26.n3 = f32[16,1152]{1,0:T(8,128)S(1)} collective-permute-done((f32[16,1152]{1,0:T(8,128)S(1)}, f32[16,1152]{1,0:T(8,128)S(1)}, u32[]{:S(2)}, u32[]{:S(2)}) %collective-permute-start.26) | collective-permute-done | bytes 73760 | tf_op jit(solution)/shard_map/ppermute | solution.py:235
  105.7 1.7 %collective-permute-done.25.n2 = f32[16,1152]{1,0:T(8,128)S(1)} collective-permute-done((f32[16,1152]{1,0:T(8,128)S(1)}, f32[16,1152]{1,0:T(8,128)S(1)}, u32[]{:S(2)}, u32[]{:S(2)}) %collective-permute-start.25) | collective-permute-done | bytes 73760 | tf_op jit(solution)/shard_map/ppermute | solution.py:235
  109.3 6.4 %k5.1 = (f32[32,1152]{1,0:T(8,128)S(1)}, f32[32,32]{1,0:T(8,128)S(1)}, f32[32,64]{1,0:T(8,128)S(1)}) custom-call(f32[16,1152]{1,0:T(8,128)S(1)} %fusion.1.n0, f32[16,1152]{1,0:T(8,128)S(1)} %collective-permute-done.24.n1, f32[16,1152]{1,0:T(8,128)S(1)} %collective-permute-done.25.n2, f32[16,1152]{1,0:T(8,128)S(1)} %collective-permute-done.26.n3, ...), custom_call_target="tpu_custom_call" | custom-call | tf_op jit(solution)/shard_map/k5/pallas_call | solution.py:223
  115.7 2.9 %collective-permute-start.30 = (f32[32,1152]{1,0:T(8,128)S(1)}, f32[32,1152]{1,0:T(8,128)S(1)}, u32[]{:S(2)}, u32[]{:S(2)}) collective-permute-start(f32[32,1152]{1,0:T(8,128)S(1)} %get-tuple-element.33), channel_id=1, source_target_pairs={{0,24},{8,16},{16,8},{24,0},{32,56},{40,48},{48,40},{56,32},{64,88... | collective-permute-start | bytes 442376 | tf_op jit(solution)/shard_map/ppermute | solution.py:235
  119.9 5.3 %collective-permute-done.30 = f32[32,1152]{1,0:T(8,128)S(1)} collective-permute-done((f32[32,1152]{1,0:T(8,128)S(1)}, f32[32,1152]{1,0:T(8,128)S(1)}, u32[]{:S(2)}, u32[]{:S(2)}) %collective-permute-start.30) | collective-permute-done | bytes 147488 | tf_op jit(solution)/shard_map/ppermute | solution.py:235
  125.2 1.6 %collective-permute-done.29 = f32[32,1152]{1,0:T(8,128)S(1)} collective-permute-done((f32[32,1152]{1,0:T(8,128)S(1)}, f32[32,1152]{1,0:T(8,128)S(1)}, u32[]{:S(2)}, u32[]{:S(2)}) %collective-permute-start.29) | collective-permute-done | bytes 147488 | tf_op jit(solution)/shard_map/ppermute | solution.py:235
  126.9 2.2 %collective-permute-start.33 = (f32[32,1152]{1,0:T(8,128)S(1)}, f32[32,1152]{1,0:T(8,128)S(1)}, u32[]{:S(2)}, u32[]{:S(2)}) collective-permute-start(f32[32,1152]{1,0:T(8,128)S(1)} %add_add_fusion.z0), channel_id=1, source_target_pairs={{0,96},{8,104},{16,112},{24,120},{32,64},{40,72},{48,80},{56,88},{... | collective-permute-start | bytes 442376 | tf_op jit(solution)/shard_map/ppermute | solution.py:235
  131.1 4.5 %collective-permute-done.33.z3 = f32[32,1152]{1,0:T(8,128)S(1)} collective-permute-done((f32[32,1152]{1,0:T(8,128)S(1)}, f32[32,1152]{1,0:T(8,128)S(1)}, u32[]{:S(2)}, u32[]{:S(2)}) %collective-permute-start.33) | collective-permute-done | bytes 147488 | tf_op jit(solution)/shard_map/ppermute | solution.py:235
  136.6 4.4 %k6.1 = (f32[32,1024]{1,0:T(8,128)}, f32[32,1024]{1,0:T(8,128)}) custom-call(f32[32,1152]{1,0:T(8,128)S(1)} %add_add_fusion.z0, f32[32,1152]{1,0:T(8,128)S(1)} %collective-permute-done.31.z1, f32[32,1152]{1,0:T(8,128)S(1)} %collective-permute-done.32.z2, f32[32,1152]{1,0:T(8,128)S(1)} %collective-permute-done.33.z3, f32[32,1024]{1,0:T(8,128)S(1)} %get-tuple-element.27.field, ...), custom_call_target="tpu_custom_call" | custom-call | tf_op jit(solution)/shard_map/k6/pallas_call | solution.py:223
  (57 shorter events, 31.0 us)
Async XLA Ops:
  9.8 10.5 %collective-permute-start.2 = (f32[32,1152]{1,0:T(8,128)S(1)}, f32[32,1152]{1,0:T(8,128)S(1)}, u32[]{:S(2)}, u32[]{:S(2)}) collective-permute-start(f32[32,1152]{1,0:T(8,128)S(1)} %get-tuple-element.20), channel_id=1, source_target_pairs={{0,24},{8,16},{16,8},{24,0},{32,56},{40,48},{48,40},{56,32},{64,88... | collective-permute-start | bytes 442376 | tf_op jit(solution)/shard_map/ppermute | solution.py:235
  14.0 8.3 %collective-permute-start.1 = (f32[32,1152]{1,0:T(8,128)S(1)}, f32[32,1152]{1,0:T(8,128)S(1)}, u32[]{:S(2)}, u32[]{:S(2)}) collective-permute-start(f32[32,1152]{1,0:T(8,128)S(1)} %get-tuple-element.20), channel_id=1, source_target_pairs={{0,16},{8,24},{16,0},{24,8},{32,48},{40,56},{48,32},{56,40},{64,80... | collective-permute-start | bytes 442376 | tf_op jit(solution)/shard_map/ppermute | solution.py:235
  14.0 8.3 %collective-permute-start = (f32[32,1152]{1,0:T(8,128)S(1)}, f32[32,1152]{1,0:T(8,128)S(1)}, u32[]{:S(2)}, u32[]{:S(2)}) collective-permute-start(f32[32,1152]{1,0:T(8,128)S(1)} %get-tuple-element.20), channel_id=1, source_target_pairs={{0,8},{8,0},{16,24},{24,16},{32,40},{40,32},{48,56},{56,48},{64,72... | collective-permute-start | bytes 442376 | tf_op jit(solution)/shard_map/ppermute | solution.py:235
  22.4 8.0 %collective-permute-start.5 = (f32[32,1152]{1,0:T(8,128)S(1)}, f32[32,1152]{1,0:T(8,128)S(1)}, u32[]{:S(2)}, u32[]{:S(2)}) collective-permute-start(f32[32,1152]{1,0:T(8,128)S(1)} %add_add_fusion.2.p0), channel_id=1, source_target_pairs={{0,96},{8,104},{16,112},{24,120},{32,64},{40,72},{48,80},{56,88},{... | collective-permute-start | bytes 442376 | tf_op jit(solution)/shard_map/ppermute | solution.py:235
  25.4 7.0 %collective-permute-start.4 = (f32[32,1152]{1,0:T(8,128)S(1)}, f32[32,1152]{1,0:T(8,128)S(1)}, u32[]{:S(2)}, u32[]{:S(2)}) collective-permute-start(f32[32,1152]{1,0:T(8,128)S(1)} %add_add_fusion.2.p0), channel_id=1, source_target_pairs={{0,64},{8,72},{16,80},{24,88},{32,96},{40,104},{48,112},{56,120},{... | collective-permute-start | bytes 442376 | tf_op jit(solution)/shard_map/ppermute | solution.py:235
  26.1 6.4 %collective-permute-start.3 = (f32[32,1152]{1,0:T(8,128)S(1)}, f32[32,1152]{1,0:T(8,128)S(1)}, u32[]{:S(2)}, u32[]{:S(2)}) collective-permute-start(f32[32,1152]{1,0:T(8,128)S(1)} %add_add_fusion.2.p0), channel_id=1, source_target_pairs={{0,32},{8,40},{16,48},{24,56},{32,0},{40,8},{48,16},{56,24},{64,96... | collective-permute-start | bytes 442376 | tf_op jit(solution)/shard_map/ppermute | solution.py:235
  39.5 6.2 %collective-permute-start.9 = (f32[16,1152]{1,0:T(8,128)S(1)}, f32[16,1152]{1,0:T(8,128)S(1)}, u32[]{:S(2)}, u32[]{:S(2)}) collective-permute-start(f32[16,1152]{1,0:T(8,128)S(1)} %get-tuple-element.41), channel_id=1, source_target_pairs={{0,6},{1,7},{2,4},{3,5},{4,2},{5,3},{6,0},{7,1},{8,14},{9,15},{10,... | collective-permute-start | bytes 221192 | tf_op jit(solution)/shard_map/ppermute | solution.py:235
  42.3 6.3 %collective-permute-start.8 = (f32[16,1152]{1,0:T(8,128)S(1)}, f32[16,1152]{1,0:T(8,128)S(1)}, u32[]{:S(2)}, u32[]{:S(2)}) collective-permute-start(f32[16,1152]{1,0:T(8,128)S(1)} %get-tuple-element.42), channel_id=1, source_target_pairs={{0,4},{1,5},{2,6},{3,7},{4,0},{5,1},{6,2},{7,3},{8,12},{9,13},{10,... | collective-permute-start | bytes 221192 | tf_op jit(solution)/shard_map/ppermute | solution.py:235
  43.1 5.5 %collective-permute-start.7 = (f32[16,1152]{1,0:T(8,128)S(1)}, f32[16,1152]{1,0:T(8,128)S(1)}, u32[]{:S(2)}, u32[]{:S(2)}) collective-permute-start(f32[16,1152]{1,0:T(8,128)S(1)} %get-tuple-element.43), channel_id=1, source_target_pairs={{0,2},{1,3},{2,0},{3,1},{4,6},{5,7},{6,4},{7,5},{8,10},{9,11},{10,... | collective-permute-start | bytes 221192 | tf_op jit(solution)/shard_map/ppermute | solution.py:235
  48.6 5.8 %collective-permute-start.12 = (f32[16,1152]{1,0:T(8,128)S(1)}, f32[16,1152]{1,0:T(8,128)S(1)}, u32[]{:S(2)}, u32[]{:S(2)}) collective-permute-start(f32[16,1152]{1,0:T(8,128)S(1)} %fusion.3.n0), channel_id=1, source_target_pairs={{0,6},{1,7},{2,4},{3,5},{4,2},{5,3},{6,0},{7,1},{8,14},{9,15},{10,... | collective-permute-start | bytes 221192 | tf_op jit(solution)/shard_map/ppermute | solution.py:235
  50.1 5.9 %collective-permute-start.11 = (f32[16,1152]{1,0:T(8,128)S(1)}, f32[16,1152]{1,0:T(8,128)S(1)}, u32[]{:S(2)}, u32[]{:S(2)}) collective-permute-start(f32[16,1152]{1,0:T(8,128)S(1)} %fusion.3.n0), channel_id=1, source_target_pairs={{0,4},{1,5},{2,6},{3,7},{4,0},{5,1},{6,2},{7,3},{8,12},{9,13},{10,... | collective-permute-start | bytes 221192 | tf_op jit(solution)/shard_map/ppermute | solution.py:235
  51.1 4.8 %collective-permute-start.10 = (f32[16,1152]{1,0:T(8,128)S(1)}, f32[16,1152]{1,0:T(8,128)S(1)}, u32[]{:S(2)}, u32[]{:S(2)}) collective-permute-start(f32[16,1152]{1,0:T(8,128)S(1)} %fusion.3.n0), channel_id=1, source_target_pairs={{0,2},{1,3},{2,0},{3,1},{4,6},{5,7},{6,4},{7,5},{8,10},{9,11},{10,... | collective-permute-start | bytes 221192 | tf_op jit(solution)/shard_map/ppermute | solution.py:235
  56.0 1.8 %collective-permute-start.13 = (f32[4,16,1152]{2,1,0:T(8,128)S(1)}, f32[4,16,1152]{2,1,0:T(8,128)S(1)}, u32[]{:S(2)}, u32[]{:S(2)}) collective-permute-start(f32[4,16,1152]{2,1,0:T(8,128)S(1)} %pad_maximum_fusion), channel_id=1, source_target_pairs={{0,1},{1,0},{2,3},{3,2},{4,5},{5,4},{6,7},{7,6},{8,9},{9,8},{10,11... | collective-permute-start | bytes 884744 | tf_op jit(solution)/shard_map/ppermute | solution.py:235
  60.8 9.5 %collective-permute-start.16 = (f32[32,1152]{1,0:T(8,128)S(1)}, f32[32,1152]{1,0:T(8,128)S(1)}, u32[]{:S(2)}, u32[]{:S(2)}) collective-permute-start(f32[32,1152]{1,0:T(8,128)S(1)} %get-tuple-element.26), channel_id=1, source_target_pairs={{0,24},{8,16},{16,8},{24,0},{32,56},{40,48},{48,40},{56,32},{64,88... | collective-permute-start | bytes 442376 | tf_op jit(solution)/shard_map/ppermute | solution.py:235
  63.8 8.2 %collective-permute-start.15 = (f32[32,1152]{1,0:T(8,128)S(1)}, f32[32,1152]{1,0:T(8,128)S(1)}, u32[]{:S(2)}, u32[]{:S(2)}) collective-permute-start(f32[32,1152]{1,0:T(8,128)S(1)} %get-tuple-element.26), channel_id=1, source_target_pairs={{0,16},{8,24},{16,0},{24,8},{32,48},{40,56},{48,32},{56,40},{64,80... | collective-permute-start | bytes 442376 | tf_op jit(solution)/shard_map/ppermute | solution.py:235
  64.0 8.0 %collective-permute-start.14 = (f32[32,1152]{1,0:T(8,128)S(1)}, f32[32,1152]{1,0:T(8,128)S(1)}, u32[]{:S(2)}, u32[]{:S(2)}) collective-permute-start(f32[32,1152]{1,0:T(8,128)S(1)} %get-tuple-element.26), channel_id=1, source_target_pairs={{0,8},{8,0},{16,24},{24,16},{32,40},{40,32},{48,56},{56,48},{64,72... | collective-permute-start | bytes 442376 | tf_op jit(solution)/shard_map/ppermute | solution.py:235
  72.0 8.6 %collective-permute-start.19 = (f32[32,1152]{1,0:T(8,128)S(1)}, f32[32,1152]{1,0:T(8,128)S(1)}, u32[]{:S(2)}, u32[]{:S(2)}) collective-permute-start(f32[32,1152]{1,0:T(8,128)S(1)} %add_add_fusion.1.z0), channel_id=1, source_target_pairs={{0,96},{8,104},{16,112},{24,120},{32,64},{40,72},{48,80},{56,88},{... | collective-permute-start | bytes 442376 | tf_op jit(solution)/shard_map/ppermute | solution.py:235
  74.3 7.4 %collective-permute-start.18 = (f32[32,1152]{1,0:T(8,128)S(1)}, f32[32,1152]{1,0:T(8,128)S(1)}, u32[]{:S(2)}, u32[]{:S(2)}) collective-permute-start(f32[32,1152]{1,0:T(8,128)S(1)} %add_add_fusion.1.z0), channel_id=1, source_target_pairs={{0,64},{8,72},{16,80},{24,88},{32,96},{40,104},{48,112},{56,120},{... | collective-permute-start | bytes 442376 | tf_op jit(solution)/shard_map/ppermute | solution.py:235
  74.8 6.8 %collective-permute-start.17 = (f32[32,1152]{1,0:T(8,128)S(1)}, f32[32,1152]{1,0:T(8,128)S(1)}, u32[]{:S(2)}, u32[]{:S(2)}) collective-permute-start(f32[32,1152]{1,0:T(8,128)S(1)} %add_add_fusion.1.z0), channel_id=1, source_target_pairs={{0,32},{8,40},{16,48},{24,56},{32,0},{40,8},{48,16},{56,24},{64,96... | collective-permute-start | bytes 442376 | tf_op jit(solution)/shard_map/ppermute | solution.py:235
  91.6 5.6 %collective-permute-start.23 = (f32[16,1152]{1,0:T(8,128)S(1)}, f32[16,1152]{1,0:T(8,128)S(1)}, u32[]{:S(2)}, u32[]{:S(2)}) collective-permute-start(f32[16,1152]{1,0:T(8,128)S(1)} %get-tuple-element.38), channel_id=1, source_target_pairs={{0,6},{1,7},{2,4},{3,5},{4,2},{5,3},{6,0},{7,1},{8,14},{9,15},{10,... | collective-permute-start | bytes 221192 | tf_op jit(solution)/shard_map/ppermute | solution.py:235
  93.6 6.3 %collective-permute-start.22 = (f32[16,1152]{1,0:T(8,128)S(1)}, f32[16,1152]{1,0:T(8,128)S(1)}, u32[]{:S(2)}, u32[]{:S(2)}) collective-permute-start(f32[16,1152]{1,0:T(8,128)S(1)} %get-tuple-element.39), channel_id=1, source_target_pairs={{0,4},{1,5},{2,6},{3,7},{4,0},{5,1},{6,2},{7,3},{8,12},{9,13},{10,... | collective-permute-start | bytes 221192 | tf_op jit(solution)/shard_map/ppermute | solution.py:235
  95.0 4.9 %collective-permute-start.21 = (f32[16,1152]{1,0:T(8,128)S(1)}, f32[16,1152]{1,0:T(8,128)S(1)}, u32[]{:S(2)}, u32[]{:S(2)}) collective-permute-start(f32[16,1152]{1,0:T(8,128)S(1)} %get-tuple-element.40), channel_id=1, source_target_pairs={{0,2},{1,3},{2,0},{3,1},{4,6},{5,7},{6,4},{7,5},{8,10},{9,11},{10,... | collective-permute-start | bytes 221192 | tf_op jit(solution)/shard_map/ppermute | solution.py:235
  99.9 5.8 %collective-permute-start.26 = (f32[16,1152]{1,0:T(8,128)S(1)}, f32[16,1152]{1,0:T(8,128)S(1)}, u32[]{:S(2)}, u32[]{:S(2)}) collective-permute-start(f32[16,1152]{1,0:T(8,128)S(1)} %fusion.1.n0), channel_id=1, source_target_pairs={{0,6},{1,7},{2,4},{3,5},{4,2},{5,3},{6,0},{7,1},{8,14},{9,15},{10,... | collective-permute-start | bytes 221192 | tf_op jit(solution)/shard_map/ppermute | solution.py:235
  101.5 5.9 %collective-permute-start.25 = (f32[16,1152]{1,0:T(8,128)S(1)}, f32[16,1152]{1,0:T(8,128)S(1)}, u32[]{:S(2)}, u32[]{:S(2)}) collective-permute-start(f32[16,1152]{1,0:T(8,128)S(1)} %fusion.1.n0), channel_id=1, source_target_pairs={{0,4},{1,5},{2,6},{3,7},{4,0},{5,1},{6,2},{7,3},{8,12},{9,13},{10,... | collective-permute-start | bytes 221192 | tf_op jit(solution)/shard_map/ppermute | solution.py:235
  102.8 4.6 %collective-permute-start.24 = (f32[16,1152]{1,0:T(8,128)S(1)}, f32[16,1152]{1,0:T(8,128)S(1)}, u32[]{:S(2)}, u32[]{:S(2)}) collective-permute-start(f32[16,1152]{1,0:T(8,128)S(1)} %fusion.1.n0), channel_id=1, source_target_pairs={{0,2},{1,3},{2,0},{3,1},{4,6},{5,7},{6,4},{7,5},{8,10},{9,11},{10,... | collective-permute-start | bytes 221192 | tf_op jit(solution)/shard_map/ppermute | solution.py:235
  107.4 1.9 %collective-permute-start.27 = (f32[4,16,1152]{2,1,0:T(8,128)S(1)}, f32[4,16,1152]{2,1,0:T(8,128)S(1)}, u32[]{:S(2)}, u32[]{:S(2)}) collective-permute-start(f32[4,16,1152]{2,1,0:T(8,128)S(1)} %pad_maximum_fusion.1), channel_id=1, source_target_pairs={{0,1},{1,0},{2,3},{3,2},{4,5},{5,4},{6,7},{7,6},{8,9},{9,8},{10,11... | collective-permute-start | bytes 884744 | tf_op jit(solution)/shard_map/ppermute | solution.py:235
  115.7 9.5 %collective-permute-start.30 = (f32[32,1152]{1,0:T(8,128)S(1)}, f32[32,1152]{1,0:T(8,128)S(1)}, u32[]{:S(2)}, u32[]{:S(2)}) collective-permute-start(f32[32,1152]{1,0:T(8,128)S(1)} %get-tuple-element.33), channel_id=1, source_target_pairs={{0,24},{8,16},{16,8},{24,0},{32,56},{40,48},{48,40},{56,32},{64,88... | collective-permute-start | bytes 442376 | tf_op jit(solution)/shard_map/ppermute | solution.py:235
  118.6 8.2 %collective-permute-start.29 = (f32[32,1152]{1,0:T(8,128)S(1)}, f32[32,1152]{1,0:T(8,128)S(1)}, u32[]{:S(2)}, u32[]{:S(2)}) collective-permute-start(f32[32,1152]{1,0:T(8,128)S(1)} %get-tuple-element.33), channel_id=1, source_target_pairs={{0,16},{8,24},{16,0},{24,8},{32,48},{40,56},{48,32},{56,40},{64,80... | collective-permute-start | bytes 442376 | tf_op jit(solution)/shard_map/ppermute | solution.py:235
  118.9 8.0 %collective-permute-start.28 = (f32[32,1152]{1,0:T(8,128)S(1)}, f32[32,1152]{1,0:T(8,128)S(1)}, u32[]{:S(2)}, u32[]{:S(2)}) collective-permute-start(f32[32,1152]{1,0:T(8,128)S(1)} %get-tuple-element.33), channel_id=1, source_target_pairs={{0,8},{8,0},{16,24},{24,16},{32,40},{40,32},{48,56},{56,48},{64,72... | collective-permute-start | bytes 442376 | tf_op jit(solution)/shard_map/ppermute | solution.py:235
  126.9 8.7 %collective-permute-start.33 = (f32[32,1152]{1,0:T(8,128)S(1)}, f32[32,1152]{1,0:T(8,128)S(1)}, u32[]{:S(2)}, u32[]{:S(2)}) collective-permute-start(f32[32,1152]{1,0:T(8,128)S(1)} %add_add_fusion.z0), channel_id=1, source_target_pairs={{0,96},{8,104},{16,112},{24,120},{32,64},{40,72},{48,80},{56,88},{... | collective-permute-start | bytes 442376 | tf_op jit(solution)/shard_map/ppermute | solution.py:235
  129.1 7.4 %collective-permute-start.32 = (f32[32,1152]{1,0:T(8,128)S(1)}, f32[32,1152]{1,0:T(8,128)S(1)}, u32[]{:S(2)}, u32[]{:S(2)}) collective-permute-start(f32[32,1152]{1,0:T(8,128)S(1)} %add_add_fusion.z0), channel_id=1, source_target_pairs={{0,64},{8,72},{16,80},{24,88},{32,96},{40,104},{48,112},{56,120},{... | collective-permute-start | bytes 442376 | tf_op jit(solution)/shard_map/ppermute | solution.py:235
  129.6 6.9 %collective-permute-start.31 = (f32[32,1152]{1,0:T(8,128)S(1)}, f32[32,1152]{1,0:T(8,128)S(1)}, u32[]{:S(2)}, u32[]{:S(2)}) collective-permute-start(f32[32,1152]{1,0:T(8,128)S(1)} %add_add_fusion.z0), channel_id=1, source_target_pairs={{0,32},{8,40},{16,48},{24,56},{32,0},{40,8},{48,16},{56,24},{64,96... | collective-permute-start | bytes 442376 | tf_op jit(solution)/shard_map/ppermute | solution.py:235
  (4 other events, 5.0 us)

commit v2 on v1

v2 whole, which is shorter than its diff:
```python
import jax
import jax.numpy as jnp
from jax import lax
from jax.experimental import pallas as pl
from jax.experimental.pallas import tpu as pltpu
from jax.sharding import PartitionSpec as P


K = 32
HALF = K // 2
LANES = 128
TILE = 8
XCHIPS = 4
DISTANCES = (0, 1, 3, 2)
CHUNK = 512
BUFFERS = 4
prio_power = 0.7
weight_power = 0.5
ridge_shift = 0.5
f32, bf16 = jnp.float32, jnp.bfloat16
IN_VMEM = pl.BlockSpec(memory_space=pltpu.VMEM)
IN_SMEM = pl.BlockSpec(memory_space=pltpu.SMEM)
IN_HBM = pl.BlockSpec(memory_space=pltpu.HBM)
ROWS_BY_ROWS = (((1,), (1,)), ((), ()))


def split(value):
    high = value.astype(bf16)
    return high, (value - high.astype(f32)).astype(bf16)


def exact(left, right):
    return jnp.dot(left, right, precision=lax.Precision.HIGHEST, preferred_element_type=f32)


def row_gram(left, right):
    return lax.dot_general(left, right, ROWS_BY_ROWS, precision=lax.Precision.HIGHEST, preferred_element_type=f32)


def solve_t(matrix, rhs_block):
    block = 4
    matrix = 0.5 * (matrix + matrix.T)
    table = jnp.concatenate([matrix, rhs_block], axis=1)
    row_id = lax.broadcasted_iota(jnp.int32, table.shape, 0)
    for k in range(0, K, block):
        columns = [jnp.broadcast_to(table[:, k + j : k + j + 1], table.shape) for j in range(block)]
        rows = [table[k + i : k + i + 1, :] for i in range(block)]
        pivot = [[column[k + i : k + i + 1, :] for column in columns] for i in range(block)]
        for p in range(block):
            inverse = 1.0 / pivot[p][p]
            rows[p] = rows[p] * inverse
            pivot[p] = [value * inverse for value in pivot[p]]
            for i in range(block):
                if i != p:
                    factor = pivot[i][p]
                    rows[i] = rows[i] - factor * rows[p]
                    pivot[i] = [value - factor * over for value, over in zip(pivot[i], pivot[p])]
        for j in range(block):
            table = table - columns[j] * rows[j]
        for i in range(block):
            table = jnp.where(row_id == k + i, rows[i], table)
    return table[:, K:].T


def merged(parts):
    a, b, c, d = (part[...] for part in parts)
    return (a + b) + (c + d)


def pack(square):
    return jnp.concatenate([square[i : i + TILE] for i in range(0, K, TILE)], axis=1)


def unpack(tile):
    return jnp.concatenate([tile[:, i : i + K] for i in range(0, LANES, K)], axis=0)


def put_blocks(out, value, tile):
    blocks = value.shape[1] // LANES
    for j in range(blocks):
        out[j * K : (j + 1) * K, :] = value[:, j * LANES : (j + 1) * LANES]
    out[blocks * K :, :] = tile


def get_blocks(stacked):
    blocks = stacked.shape[0] // K
    value = jnp.concatenate([stacked[j * K : (j + 1) * K] for j in range(blocks)], axis=1)
    return value, stacked[blocks * K :]


def k1(count, ranks_hbm, targets_hbm, features, high, low, scale, out, buf, targets, ranks, pair, sem, in_sem):
    slots, width = features.shape
    steps = slots // CHUNK
    small = [
        pltpu.make_async_copy(ranks_hbm, ranks, in_sem.at[0]),
        pltpu.make_async_copy(targets_hbm, targets, in_sem.at[1]),
    ]
    copies = [
        pltpu.make_async_copy(features.at[pl.ds(c * CHUNK, CHUNK)], buf.at[c % BUFFERS], sem.at[c % BUFFERS])
        for c in range(steps)
    ]
    for copy in small:
        copy.start()
    for c in range(BUFFERS):
        copies[c].start()
    live = lax.broadcasted_iota(jnp.int32, (1, slots), 1) < count[0]
    small[0].wait()
    log_rank = jnp.log(ranks[...].astype(f32))
    scale_now = jnp.where(live, jnp.exp((prio_power * weight_power) * log_rank), 0.0)
    scale[...] = scale_now
    prio_sum = jnp.sum(jnp.where(live, jnp.exp(-prio_power * log_rank), 0.0))
    small[1].wait()
    high_t, low_t = split(targets[...] * scale_now)
    pair[0:K, :] = high_t
    pair[K : 2 * K, :] = low_t
    total = jnp.zeros((2 * K, width), f32)
    rest = jnp.zeros((K, width), f32)
    for c in range(steps):
        at = slice(c * CHUNK, (c + 1) * CHUNK)
        copies[c].wait()
        high_f, low_f = split(buf[c % BUFFERS])
        if c + BUFFERS < steps:
            copies[c + BUFFERS].start()
        high[at, :] = high_f
        low[at, :] = low_f
        total += jnp.dot(pair[:, at], high_f, preferred_element_type=f32)
        rest += jnp.dot(pair[0:K, at], low_f, preferred_element_type=f32)
    row = lax.broadcasted_iota(jnp.int32, (TILE, LANES), 0)
    col = lax.broadcasted_iota(jnp.int32, (TILE, LANES), 1)
    tail = jnp.where(col == 0, prio_sum, jnp.where(col == 1, count[0].astype(f32), 0.0))
    put_blocks(out, total[0:K] + total[K:] + rest, jnp.where(row == 0, tail, 0.0))


def put_images(field, tiles, high, low, mine, other):
    place = lax.axis_index("feat")
    x, first = place // 2, place % 2 == 0
    part = high.shape[0] // XCHIPS
    high_v, low_v = split(field)
    pair = jnp.concatenate([high_v, low_v], axis=0)
    for c in range(XCHIPS):
        slot = x ^ c
        for piece in range(0, part, CHUNK):
            at = slice(c * part + piece, c * part + piece + CHUNK)
            both = lax.dot_general(pair, high[at, :], ROWS_BY_ROWS, preferred_element_type=f32)
            rest = lax.dot_general(high_v, low[at, :], ROWS_BY_ROWS, preferred_element_type=f32)
            value = both[0:K] + both[K:] + rest
            here = jnp.where(first, value[0:HALF], value[HALF:])
            there = jnp.where(first, value[HALF:], value[0:HALF])
            for j in range(0, CHUNK, LANES):
                to = (piece + j) // LANES * HALF
                mine[slot, to : to + HALF, :] = here[:, j : j + LANES]
                other[slot, to : to + HALF, :] = there[:, j : j + LANES]
        mine[slot, part // LANES * HALF :, :] = tiles
        other[slot, part // LANES * HALF :, :] = tiles


def k2(p0, p1, p2, p3, high, low, field, norm, mine, other):
    total, tile = get_blocks(merged((p0, p1, p2, p3)))
    factor = jnp.sqrt(tile[0:1, 0:1] / tile[0:1, 1:2])
    norm[...] = jnp.broadcast_to(factor, norm.shape)
    rhs_field = total * factor
    field[...] = rhs_field
    put_images(rhs_field, pack(row_gram(rhs_field, rhs_field)), high, low, mine, other)


def get_images(near, far, part):
    first = lax.axis_index("feat") % 2 == 0
    out = []
    for j, ref in enumerate(near):
        blocks = []
        for at in range(0, part // LANES * HALF, HALF):
            a, b = ref[at : at + HALF, :], far[j, at : at + HALF, :]
            blocks.append(jnp.concatenate([jnp.where(first, a, b), jnp.where(first, b, a)], axis=0))
        out.append(jnp.concatenate(blocks, axis=1))
    return out


def back_project(images, scale, high, low, out):
    x = lax.axis_index("feat") // 2
    part, width = images[0].shape[1], high.shape[1]
    total = jnp.zeros((2 * K, width), f32)
    rest = jnp.zeros((K, width), f32)
    curve = jnp.zeros((2 * K, 2 * K), f32)
    for j, distance in enumerate(DISTANCES):
        base = pl.multiple_of((x ^ distance) * part, part)
        high_w, low_w = split(images[j] * scale[:, pl.ds(base, part)])
        high_i, low_i = split(images[j])
        pair = jnp.concatenate([high_w, low_w], axis=0)
        curve += lax.dot_general(
            pair, jnp.concatenate([high_i, low_i], axis=0), ROWS_BY_ROWS, preferred_element_type=f32
        )
        for piece in range(0, part, CHUNK):
            at = pl.ds(pl.multiple_of(base + piece, CHUNK), CHUNK)
            to = slice(piece, piece + CHUNK)
            total += jnp.dot(pair[:, to], high[at, :], preferred_element_type=f32)
            rest += jnp.dot(high_w[:, to], low[at, :], preferred_element_type=f32)
    curve = curve[0:K, 0:K] + curve[0:K, K:] + curve[K:, 0:K]
    put_blocks(out, total[0:K] + total[K:] + rest, pack(curve))


def k3(n0, n1, n2, n3, far, scale, high, low, out, kept, gram):
    part = kept.shape[2]
    gram[...] = unpack(n0[part // LANES * HALF :, :])
    images = get_images((n0, n1, n2, n3), far, part)
    for j in range(XCHIPS):
        kept[j] = images[j]
    back_project(images, scale, high, low, out)


def k4(z0, z1, z2, z3, field, norm, gram, high, low, residual, step, mine, other):
    total, tile = get_blocks(merged((z0, z1, z2, z3)))
    factor = norm[0:1, 0:1]
    curvature = unpack(tile) * factor + ridge_shift * gram[...]
    step_t = solve_t(curvature, gram[...])
    step[...] = step_t
    backward = total * factor + ridge_shift * field[...]
    now = field[...] - exact(step_t, backward)
    residual[...] = now
    tiles = jnp.concatenate([pack(row_gram(now, now)), pack(row_gram(now, field[...]))], axis=0)
    put_images(now, tiles, high, low, mine, other)


def k5(n0, n1, n2, n3, far, kept, gram, scale, high, low, out, coef, gram_new, cross):
    part = kept.shape[2]
    tiles = n0[part // LANES * HALF :, :]
    square = unpack(tiles[0:TILE])
    gram_new[...] = square
    cross[...] = unpack(tiles[TILE:])
    coef_t = solve_t(gram[...], square)
    coef[...] = coef_t
    chunks = get_images((n0, n1, n2, n3), far, part)
    images = [chunk + exact(coef_t, kept[j]) for j, chunk in enumerate(chunks)]
    back_project(images, scale, high, low, out)


def k6(z0, z1, z2, z3, field, residual, norm, gram, gram_new, cross, step, coef, solution_out, residual_out):
    coef_t = coef[...]
    mixed = row_gram(cross[...], coef_t)
    square = gram_new[...] + mixed + mixed.T + row_gram(exact(coef_t, gram[...]), coef_t)
    total, tile = get_blocks(merged((z0, z1, z2, z3)))
    factor = norm[0:1, 0:1]
    curvature = unpack(tile) * factor + ridge_shift * square
    step_t = solve_t(curvature, gram_new[...])
    direction = residual[...] + exact(coef_t, field[...])
    backward = total * factor + ridge_shift * direction
    solution_out[...] = exact(step[...], field[...]) + exact(step_t, direction)
    residual_out[...] = residual[...] - exact(step_t, backward)


def call(kernel, outs, operands, specs=None, scratch=(), limit=24):
    return pl.pallas_call(
        kernel,
        out_shape=outs,
        in_specs=specs or [IN_VMEM] * len(operands),
        out_specs=[IN_VMEM] * len(outs),
        scratch_shapes=scratch,
        compiler_params=pltpu.CompilerParams(vmem_limit_bytes=limit << 20),
        name=kernel.__name__,
    )(*operands)


def in_hbm(value):
    return pltpu.with_memory_space_constraint(value, pltpu.HBM)


def exchange(value, row_distance, feat_distance):
    pairs = [
        (r * 8 + f, (r ^ row_distance[f % 2]) * 8 + (f ^ feat_distance)) for r in range(16) for f in range(8)
    ]
    return lax.ppermute(value, ("rows", "feat"), pairs)


def gather_rows(value):
    got = {d: exchange(value, (d, 4 * d), 0) for d in (1, 3, 2)}
    value = (value + got[1]) + (got[3] + got[2])
    got = {d: exchange(value, (4 * d, d), 0) for d in (1, 3, 2)}
    return [value, got[1], got[3], got[2]]


def sum_feat(mine, other):
    here = (0, 0)
    value = mine + exchange(other, here, 1)
    got = {d: exchange(value[d], here, 2 * d) for d in (1, 3, 2)}
    value = (value[0] + got[1]) + (got[3] + got[2])
    got = {d: exchange(value, here, 2 * d) for d in (1, 3, 2)}
    near = [value, *(got[d] for d in DISTANCES[1:])]
    return [*near, exchange(jnp.stack(near), here, 1)]


def local(features, targets, counts, ranks):
    slots, width = features.shape
    part = slots // XCHIPS
    shape = jax.ShapeDtypeStruct
    summed = shape((width // LANES * K + TILE, LANES), f32)
    field_like, small = shape((K, width), f32), shape((K, K), f32)

    def images_like(tiles):
        return [shape((XCHIPS, part // LANES * HALF + tiles * TILE, LANES), f32)] * 2

    high, low, scale, out = call(
        k1,
        [pltpu.VMEM((slots, width), bf16), pltpu.VMEM((slots, width), bf16), shape((1, slots), f32), summed],
        (counts, in_hbm(ranks.reshape(1, slots)), in_hbm(targets), in_hbm(features)),
        [IN_SMEM, IN_HBM, IN_HBM, IN_HBM],
        (
            pltpu.VMEM((BUFFERS, CHUNK, width), f32),
            pltpu.VMEM((K, slots), f32),
            pltpu.VMEM((1, slots), jnp.int32),
            pltpu.VMEM((2 * K, slots), bf16),
            pltpu.SemaphoreType.DMA((BUFFERS,)),
            pltpu.SemaphoreType.DMA((2,)),
        ),
    )
    parts = gather_rows(out)
    field, norm, mine, other = call(k2, [field_like, shape((8, 128), f32), *images_like(1)], (*parts, high, low))
    parts = sum_feat(mine, other)
    out, kept, gram = call(k3, [summed, shape((XCHIPS, K, part), f32), small], (*parts, scale, high, low))
    parts = gather_rows(out)
    residual, step, mine, other = call(
        k4, [field_like, small, *images_like(2)], (*parts, field, norm, gram, high, low)
    )
    parts = sum_feat(mine, other)
    out, coef, gram_new, cross = call(
        k5, [summed, small, small, small], (*parts, kept, gram, scale, high, low)
    )
    parts = gather_rows(out)
    rest = (field, residual, norm, gram, gram_new, cross, step, coef)
    return tuple(call(k6, [field_like, field_like], (*parts, *rest)))


def solution(mesh):
    placed = (P("rows", "feat"), P(None, "rows"), P("rows"), P("rows"))
    return jax.shard_map(
        local,
        mesh=mesh,
        in_specs=placed,
        out_specs=(P(None, "feat"), P(None, "feat")),
        check_vma=False,
    )
```

time: 141 us -> 123 us (0.87)
  waiting for transfers between devices: 60 us -> 51.4 us
  starting transfers between devices: 43.4 us -> 39.3 us
  Pallas kernels: 34 us -> 30.8 us
  local copies, waits for them, and re-layouts: 1.79 us -> 0.03 us
    ppermute x34, waiting for transfers between devices: 60 us -> 51.4 us  [exchange(): return lax.ppermute(value, ('rows', 'feat'), pairs)]
    ppermute x34, starting transfers between devices: 43.4 us -> 39.3 us  [exchange(): return lax.ppermute(value, ('rows', 'feat'), pairs)]
    pallas_call x6, Pallas kernels: 34 us -> 30.8 us  [call(): pl.pallas_call(kernel, out_shape=outs, in_specs=specs or [IN_VMEM] * len(...]
    unnamed x4 -> x0, local copies, waits for them, and re-layouts: 1.75 us -> none
  transfers between devices with their start and end apart: 34 -> 34, of which waited for: 24 -> 26; matrix products, arithmetic and copies ran while one was open for 0% -> 0% of each run, Pallas kernels for 0% -> 0%
where the time goes in v2:
time: 123 us
  waiting for transfers between devices  51.4 us (42%)
  starting transfers between devices  39.3 us (32%)
  Pallas kernels  30.8 us (25%)
  between operations  1.42 us (1%)
    ppermute x34, waiting for transfers between devices, exchange(): return lax.ppermute(value, ('rows', 'feat'), pairs)  51.4 us
    ppermute x34, starting transfers between devices, exchange(): return lax.ppermute(value, ('rows', 'feat'), pairs)  39.3 us
    pallas_call x6, Pallas kernels, call(): pl.pallas_call(kernel, out_shape=outs, in_specs=specs or [IN_VMEM] * len(...  30.8 us
  transfers between devices with their start and end apart: 34, of which 26 were waited for; matrix products, arithmetic and copies ran while one was open for 0% of the time, Pallas kernels for 0%

profile of v2, /device:TPU:0, one launch (start us, length us, event | category | flops | bytes accessed | tf_op | source)
XLA Modules:
  0.0 123.3 jit_solution(17432835158494098718)
XLA Ops:
  1.3 7.8 %k1.1 = (bf16[4096,1024]{1,0:T(8,128)(2,1)S(1)}, bf16[4096,1024]{1,0:T(8,128)(2,1)S(1)}, f32[1,4096]{1,0:T(1,128)S(1)}, f32[264,128]{1,0:T(8,128)S(1)}) custom-call(s32[1]{0:T(128)S(6)} %copy.6.count, s32[1,4096]{1,0:T(1,128)} %bitcast.41, f32[32,4096]{1,0:T(8,128)} %targets_hbm.1, f32[4096,1024]{1,0:T(8,128)} %features.1), custom_call_target="tpu_custom_call" | custom-call | tf_op jit(solution)/shard_map/k1/pallas_call | solution.py:251
  9.1 4.0 %collective-permute-start.2 = (f32[264,128]{1,0:T(8,128)S(1)}, f32[264,128]{1,0:T(8,128)S(1)}, u32[]{:S(2)}, u32[]{:S(2)}) collective-permute-start(f32[264,128]{1,0:T(8,128)S(1)} %get-tuple-element.21), channel_id=1, source_target_pairs={{0,16},{1,65},{2,18},{3,67},{4,20},{5,69},{6,22},{7,71},{8,24},{9,... | collective-permute-start | bytes 405512 | tf_op jit(solution)/shard_map/ppermute | solution.py:270
  14.2 2.0 %collective-permute-done.2 = f32[264,128]{1,0:T(8,128)S(1)} collective-permute-done((f32[264,128]{1,0:T(8,128)S(1)}, f32[264,128]{1,0:T(8,128)S(1)}, u32[]{:S(2)}, u32[]{:S(2)}) %collective-permute-start.2) | collective-permute-done | bytes 135200 | tf_op jit(solution)/shard_map/ppermute | solution.py:270
  16.1 3.2 %collective-permute-done.1 = f32[264,128]{1,0:T(8,128)S(1)} collective-permute-done((f32[264,128]{1,0:T(8,128)S(1)}, f32[264,128]{1,0:T(8,128)S(1)}, u32[]{:S(2)}, u32[]{:S(2)}) %collective-permute-start.1) | collective-permute-done | bytes 135200 | tf_op jit(solution)/shard_map/ppermute | solution.py:270
  19.4 3.3 %collective-permute-start.5 = (f32[264,128]{1,0:T(8,128)S(1)}, f32[264,128]{1,0:T(8,128)S(1)}, u32[]{:S(2)}, u32[]{:S(2)}) collective-permute-start(f32[264,128]{1,0:T(8,128)S(1)} %add_add_fusion.2.p0), channel_id=1, source_target_pairs={{0,64},{1,17},{2,66},{3,19},{4,68},{5,21},{6,70},{7,23},{8,72},{9,... | collective-permute-start | bytes 405512 | tf_op jit(solution)/shard_map/ppermute | solution.py:270
  23.7 2.3 %collective-permute-done.5.p3 = f32[264,128]{1,0:T(8,128)S(1)} collective-permute-done((f32[264,128]{1,0:T(8,128)S(1)}, f32[264,128]{1,0:T(8,128)S(1)}, u32[]{:S(2)}, u32[]{:S(2)}) %collective-permute-start.5) | collective-permute-done | bytes 135200 | tf_op jit(solution)/shard_map/ppermute | solution.py:270
  26.0 2.9 %collective-permute-done.4.p2 = f32[264,128]{1,0:T(8,128)S(1)} collective-permute-done((f32[264,128]{1,0:T(8,128)S(1)}, f32[264,128]{1,0:T(8,128)S(1)}, u32[]{:S(2)}, u32[]{:S(2)}) %collective-permute-start.4) | collective-permute-done | bytes 135200 | tf_op jit(solution)/shard_map/ppermute | solution.py:270
  28.9 5.2 %k2.1 = (f32[32,1024]{1,0:T(8,128)S(1)}, f32[8,128]{1,0:T(8,128)S(1)}, f32[4,136,128]{2,1,0:T(8,128)S(1)}, f32[4,136,128]{2,1,0:T(8,128)S(1)}) custom-call(f32[264,128]{1,0:T(8,128)S(1)} %add_add_fusion.2.p0, f32[264,128]{1,0:T(8,128)S(1)} %collective-permute-done.3.p1, f32[264,128]{1,0:T(8,128)S(1)} %collective-permute-done.4.p2, ...), custom_call_target="tpu_custom_call" | custom-call | tf_op jit(solution)/shard_map/k2/pallas_call | solution.py:251
  35.9 3.1 %collective-permute-start.9 = (f32[136,128]{1,0:T(8,128)S(1)}, f32[136,128]{1,0:T(8,128)S(1)}, u32[]{:S(2)}, u32[]{:S(2)}) collective-permute-start(f32[136,128]{1,0:T(8,128)S(1)} %get-tuple-element.43), channel_id=1, source_target_pairs={{0,4},{1,5},{2,6},{3,7},{4,0},{5,1},{6,2},{7,3},{8,12},{9,13},{10,... | collective-permute-start | bytes 208904 | tf_op jit(solution)/shard_map/ppermute | solution.py:270
  40.1 1.6 %collective-permute-done.9 = f32[136,128]{1,0:T(8,128)S(1)} collective-permute-done((f32[136,128]{1,0:T(8,128)S(1)}, f32[136,128]{1,0:T(8,128)S(1)}, u32[]{:S(2)}, u32[]{:S(2)}) %collective-permute-start.9) | collective-permute-done | bytes 69664 | tf_op jit(solution)/shard_map/ppermute | solution.py:270
  41.7 2.7 %collective-permute-done.8 = f32[136,128]{1,0:T(8,128)S(1)} collective-permute-done((f32[136,128]{1,0:T(8,128)S(1)}, f32[136,128]{1,0:T(8,128)S(1)}, u32[]{:S(2)}, u32[]{:S(2)}) %collective-permute-start.8) | collective-permute-done | bytes 69664 | tf_op jit(solution)/shard_map/ppermute | solution.py:270
  48.1 3.0 %collective-permute-done.12.n3 = f32[136,128]{1,0:T(8,128)S(1)} collective-permute-done((f32[136,128]{1,0:T(8,128)S(1)}, f32[136,128]{1,0:T(8,128)S(1)}, u32[]{:S(2)}, u32[]{:S(2)}) %collective-permute-start.12) | collective-permute-done | bytes 69664 | tf_op jit(solution)/shard_map/ppermute | solution.py:270
  53.7 3.1 %k3.1 = (f32[264,128]{1,0:T(8,128)S(1)}, f32[4,32,1024]{2,1,0:T(8,128)S(1)}, f32[32,32]{1,0:T(8,128)S(1)}) custom-call(f32[136,128]{1,0:T(8,128)S(1)} %fusion.3.n0, f32[136,128]{1,0:T(8,128)S(1)} %collective-permute-done.10.n1, f32[136,128]{1,0:T(8,128)S(1)} %collective-permute-done.11.n2, f32[136,128]{1,0:T(8,128)S(1)} %collective-permute-done.12.n3, ...), custom_call_target="tpu_custom_call" | custom-call | tf_op jit(solution)/shard_map/k3/pallas_call | solution.py:251
  56.8 2.0 %collective-permute-start.16 = (f32[264,128]{1,0:T(8,128)S(1)}, f32[264,128]{1,0:T(8,128)S(1)}, u32[]{:S(2)}, u32[]{:S(2)}) collective-permute-start(f32[264,128]{1,0:T(8,128)S(1)} %get-tuple-element.27), channel_id=1, source_target_pairs={{0,16},{1,65},{2,18},{3,67},{4,20},{5,69},{6,22},{7,71},{8,24},{9,... | collective-permute-start | bytes 405512 | tf_op jit(solution)/shard_map/ppermute | solution.py:270
  60.3 3.0 %collective-permute-done.16 = f32[264,128]{1,0:T(8,128)S(1)} collective-permute-done((f32[264,128]{1,0:T(8,128)S(1)}, f32[264,128]{1,0:T(8,128)S(1)}, u32[]{:S(2)}, u32[]{:S(2)}) %collective-permute-start.16) | collective-permute-done | bytes 135200 | tf_op jit(solution)/shard_map/ppermute | solution.py:270
  63.4 1.6 %collective-permute-done.15 = f32[264,128]{1,0:T(8,128)S(1)} collective-permute-done((f32[264,128]{1,0:T(8,128)S(1)}, f32[264,128]{1,0:T(8,128)S(1)}, u32[]{:S(2)}, u32[]{:S(2)}) %collective-permute-start.15) | collective-permute-done | bytes 135200 | tf_op jit(solution)/shard_map/ppermute | solution.py:270
  65.0 1.6 %collective-permute-start.19 = (f32[264,128]{1,0:T(8,128)S(1)}, f32[264,128]{1,0:T(8,128)S(1)}, u32[]{:S(2)}, u32[]{:S(2)}) collective-permute-start(f32[264,128]{1,0:T(8,128)S(1)} %add_add_fusion.1.z0), channel_id=1, source_target_pairs={{0,64},{1,17},{2,66},{3,19},{4,68},{5,21},{6,70},{7,23},{8,72},{9,... | collective-permute-start | bytes 405512 | tf_op jit(solution)/shard_map/ppermute | solution.py:270
  68.5 3.0 %collective-permute-done.19.z3 = f32[264,128]{1,0:T(8,128)S(1)} collective-permute-done((f32[264,128]{1,0:T(8,128)S(1)}, f32[264,128]{1,0:T(8,128)S(1)}, u32[]{:S(2)}, u32[]{:S(2)}) %collective-permute-start.19) | collective-permute-done | bytes 135200 | tf_op jit(solution)/shard_map/ppermute | solution.py:270
  73.0 6.8 %k4.1 = (f32[32,1024]{1,0:T(8,128)S(1)}, f32[32,32]{1,0:T(8,128)S(1)}, f32[4,144,128]{2,1,0:T(8,128)S(1)}, f32[4,144,128]{2,1,0:T(8,128)S(1)}) custom-call(f32[264,128]{1,0:T(8,128)S(1)} %add_add_fusion.1.z0, f32[264,128]{1,0:T(8,128)S(1)} %collective-permute-done.17.z1, f32[264,128]{1,0:T(8,128)S(1)} %collective-permute-done.18.z2, ...), custom_call_target="tpu_custom_call" | custom-call | tf_op jit(solution)/shard_map/k4/pallas_call | solution.py:251
  81.5 2.1 %collective-permute-start.23 = (f32[144,128]{1,0:T(8,128)S(1)}, f32[144,128]{1,0:T(8,128)S(1)}, u32[]{:S(2)}, u32[]{:S(2)}) collective-permute-start(f32[144,128]{1,0:T(8,128)S(1)} %get-tuple-element.40), channel_id=1, source_target_pairs={{0,4},{1,5},{2,6},{3,7},{4,0},{5,1},{6,2},{7,3},{8,12},{9,13},{10,... | collective-permute-start | bytes 221192 | tf_op jit(solution)/shard_map/ppermute | solution.py:270
  85.1 2.4 %collective-permute-done.23 = f32[144,128]{1,0:T(8,128)S(1)} collective-permute-done((f32[144,128]{1,0:T(8,128)S(1)}, f32[144,128]{1,0:T(8,128)S(1)}, u32[]{:S(2)}, u32[]{:S(2)}) %collective-permute-start.23) | collective-permute-done | bytes 73760 | tf_op jit(solution)/shard_map/ppermute | solution.py:270
  87.5 1.7 %collective-permute-done.22 = f32[144,128]{1,0:T(8,128)S(1)} collective-permute-done((f32[144,128]{1,0:T(8,128)S(1)}, f32[144,128]{1,0:T(8,128)S(1)}, u32[]{:S(2)}, u32[]{:S(2)}) %collective-permute-start.22) | collective-permute-done | bytes 73760 | tf_op jit(solution)/shard_map/ppermute | solution.py:270
  89.2 1.7 %collective-permute-start.26 = (f32[144,128]{1,0:T(8,128)S(1)}, f32[144,128]{1,0:T(8,128)S(1)}, u32[]{:S(2)}, u32[]{:S(2)}) collective-permute-start(f32[144,128]{1,0:T(8,128)S(1)} %fusion.1.n0), channel_id=1, source_target_pairs={{0,4},{1,5},{2,6},{3,7},{4,0},{5,1},{6,2},{7,3},{8,12},{9,13},{10,... | collective-permute-start | bytes 221192 | tf_op jit(solution)/shard_map/ppermute | solution.py:270
  92.8 2.5 %collective-permute-done.26.n3 = f32[144,128]{1,0:T(8,128)S(1)} collective-permute-done((f32[144,128]{1,0:T(8,128)S(1)}, f32[144,128]{1,0:T(8,128)S(1)}, u32[]{:S(2)}, u32[]{:S(2)}) %collective-permute-start.26) | collective-permute-done | bytes 73760 | tf_op jit(solution)/shard_map/ppermute | solution.py:270
  98.6 5.0 %k5.1 = (f32[264,128]{1,0:T(8,128)S(1)}, f32[32,32]{1,0:T(8,128)S(1)}, f32[32,32]{1,0:T(8,128)S(1)}, f32[32,32]{1,0:T(8,128)S(1)}) custom-call(f32[144,128]{1,0:T(8,128)S(1)} %fusion.1.n0, f32[144,128]{1,0:T(8,128)S(1)} %collective-permute-done.24.n1, f32[144,128]{1,0:T(8,128)S(1)} %collective-permute-done.25.n2, f32[144,128]{1,0:T(8,128)S(1)} %collective-permute-done.26.n3, ...), custom_call_target="tpu_custom_call" | custom-call | tf_op jit(solution)/shard_map/k5/pallas_call | solution.py:251
  103.6 2.3 %collective-permute-start.30 = (f32[264,128]{1,0:T(8,128)S(1)}, f32[264,128]{1,0:T(8,128)S(1)}, u32[]{:S(2)}, u32[]{:S(2)}) collective-permute-start(f32[264,128]{1,0:T(8,128)S(1)} %get-tuple-element.34), channel_id=1, source_target_pairs={{0,16},{1,65},{2,18},{3,67},{4,20},{5,69},{6,22},{7,71},{8,24},{9,... | collective-permute-start | bytes 405512 | tf_op jit(solution)/shard_map/ppermute | solution.py:270
  107.1 3.0 %collective-permute-done.30 = f32[264,128]{1,0:T(8,128)S(1)} collective-permute-done((f32[264,128]{1,0:T(8,128)S(1)}, f32[264,128]{1,0:T(8,128)S(1)}, u32[]{:S(2)}, u32[]{:S(2)}) %collective-permute-start.30) | collective-permute-done | bytes 135200 | tf_op jit(solution)/shard_map/ppermute | solution.py:270
  110.2 1.9 %collective-permute-done.29 = f32[264,128]{1,0:T(8,128)S(1)} collective-permute-done((f32[264,128]{1,0:T(8,128)S(1)}, f32[264,128]{1,0:T(8,128)S(1)}, u32[]{:S(2)}, u32[]{:S(2)}) %collective-permute-start.29) | collective-permute-done | bytes 135200 | tf_op jit(solution)/shard_map/ppermute | solution.py:270
  112.1 2.1 %collective-permute-start.33 = (f32[264,128]{1,0:T(8,128)S(1)}, f32[264,128]{1,0:T(8,128)S(1)}, u32[]{:S(2)}, u32[]{:S(2)}) collective-permute-start(f32[264,128]{1,0:T(8,128)S(1)} %add_add_fusion.z0), channel_id=1, source_target_pairs={{0,64},{1,17},{2,66},{3,19},{4,68},{5,21},{6,70},{7,23},{8,72},{9,... | collective-permute-start | bytes 405512 | tf_op jit(solution)/shard_map/ppermute | solution.py:270
  115.7 3.0 %collective-permute-done.33.z3 = f32[264,128]{1,0:T(8,128)S(1)} collective-permute-done((f32[264,128]{1,0:T(8,128)S(1)}, f32[264,128]{1,0:T(8,128)S(1)}, u32[]{:S(2)}, u32[]{:S(2)}) %collective-permute-start.33) | collective-permute-done | bytes 135200 | tf_op jit(solution)/shard_map/ppermute | solution.py:270
  118.7 1.7 %collective-permute-done.32.z2 = f32[264,128]{1,0:T(8,128)S(1)} collective-permute-done((f32[264,128]{1,0:T(8,128)S(1)}, f32[264,128]{1,0:T(8,128)S(1)}, u32[]{:S(2)}, u32[]{:S(2)}) %collective-permute-start.32) | collective-permute-done | bytes 135200 | tf_op jit(solution)/shard_map/ppermute | solution.py:270
  120.4 2.9 %k6.1 = (f32[32,1024]{1,0:T(8,128)}, f32[32,1024]{1,0:T(8,128)}) custom-call(f32[264,128]{1,0:T(8,128)S(1)} %add_add_fusion.z0, f32[264,128]{1,0:T(8,128)S(1)} %collective-permute-done.31.z1, f32[264,128]{1,0:T(8,128)S(1)} %collective-permute-done.32.z2, f32[264,128]{1,0:T(8,128)S(1)} %collective-permute-done.33.z3, f32[32,1024]{1,0:T(8,128)S(1)} %get-tuple-element.28.field, ...), custom_call_target="tpu_custom_call" | custom-call | tf_op jit(solution)/shard_map/k6/pallas_call | solution.py:251
  (53 shorter events, 27.5 us)
Async XLA Ops:
  9.1 7.0 %collective-permute-start.2 = (f32[264,128]{1,0:T(8,128)S(1)}, f32[264,128]{1,0:T(8,128)S(1)}, u32[]{:S(2)}, u32[]{:S(2)}) collective-permute-start(f32[264,128]{1,0:T(8,128)S(1)} %get-tuple-element.21), channel_id=1, source_target_pairs={{0,16},{1,65},{2,18},{3,67},{4,20},{5,69},{6,22},{7,71},{8,24},{9,... | collective-permute-start | bytes 405512 | tf_op jit(solution)/shard_map/ppermute | solution.py:270
  13.2 6.2 %collective-permute-start.1 = (f32[264,128]{1,0:T(8,128)S(1)}, f32[264,128]{1,0:T(8,128)S(1)}, u32[]{:S(2)}, u32[]{:S(2)}) collective-permute-start(f32[264,128]{1,0:T(8,128)S(1)} %get-tuple-element.21), channel_id=1, source_target_pairs={{0,24},{1,97},{2,26},{3,99},{4,28},{5,101},{6,30},{7,103},{8,16},{... | collective-permute-start | bytes 405512 | tf_op jit(solution)/shard_map/ppermute | solution.py:270
  13.9 5.5 %collective-permute-start = (f32[264,128]{1,0:T(8,128)S(1)}, f32[264,128]{1,0:T(8,128)S(1)}, u32[]{:S(2)}, u32[]{:S(2)}) collective-permute-start(f32[264,128]{1,0:T(8,128)S(1)} %get-tuple-element.21), channel_id=1, source_target_pairs={{0,8},{1,33},{2,10},{3,35},{4,12},{5,37},{6,14},{7,39},{8,0},{9,41... | collective-permute-start | bytes 405512 | tf_op jit(solution)/shard_map/ppermute | solution.py:270
  19.4 6.6 %collective-permute-start.5 = (f32[264,128]{1,0:T(8,128)S(1)}, f32[264,128]{1,0:T(8,128)S(1)}, u32[]{:S(2)}, u32[]{:S(2)}) collective-permute-start(f32[264,128]{1,0:T(8,128)S(1)} %add_add_fusion.2.p0), channel_id=1, source_target_pairs={{0,64},{1,17},{2,66},{3,19},{4,68},{5,21},{6,70},{7,23},{8,72},{9,... | collective-permute-start | bytes 405512 | tf_op jit(solution)/shard_map/ppermute | solution.py:270
  22.7 6.2 %collective-permute-start.4 = (f32[264,128]{1,0:T(8,128)S(1)}, f32[264,128]{1,0:T(8,128)S(1)}, u32[]{:S(2)}, u32[]{:S(2)}) collective-permute-start(f32[264,128]{1,0:T(8,128)S(1)} %add_add_fusion.2.p0), channel_id=1, source_target_pairs={{0,96},{1,25},{2,98},{3,27},{4,100},{5,29},{6,102},{7,31},{8,104},... | collective-permute-start | bytes 405512 | tf_op jit(solution)/shard_map/ppermute | solution.py:270
  23.7 5.2 %collective-permute-start.3 = (f32[264,128]{1,0:T(8,128)S(1)}, f32[264,128]{1,0:T(8,128)S(1)}, u32[]{:S(2)}, u32[]{:S(2)}) collective-permute-start(f32[264,128]{1,0:T(8,128)S(1)} %add_add_fusion.2.p0), channel_id=1, source_target_pairs={{0,32},{1,9},{2,34},{3,11},{4,36},{5,13},{6,38},{7,15},{8,40},{9,1... | collective-permute-start | bytes 405512 | tf_op jit(solution)/shard_map/ppermute | solution.py:270
  35.9 5.9 %collective-permute-start.9 = (f32[136,128]{1,0:T(8,128)S(1)}, f32[136,128]{1,0:T(8,128)S(1)}, u32[]{:S(2)}, u32[]{:S(2)}) collective-permute-start(f32[136,128]{1,0:T(8,128)S(1)} %get-tuple-element.43), channel_id=1, source_target_pairs={{0,4},{1,5},{2,6},{3,7},{4,0},{5,1},{6,2},{7,3},{8,12},{9,13},{10,... | collective-permute-start | bytes 208904 | tf_op jit(solution)/shard_map/ppermute | solution.py:270
  39.0 5.5 %collective-permute-start.8 = (f32[136,128]{1,0:T(8,128)S(1)}, f32[136,128]{1,0:T(8,128)S(1)}, u32[]{:S(2)}, u32[]{:S(2)}) collective-permute-start(f32[136,128]{1,0:T(8,128)S(1)} %get-tuple-element.44), channel_id=1, source_target_pairs={{0,6},{1,7},{2,4},{3,5},{4,2},{5,3},{6,0},{7,1},{8,14},{9,15},{10,... | collective-permute-start | bytes 208904 | tf_op jit(solution)/shard_map/ppermute | solution.py:270
  40.1 4.4 %collective-permute-start.7 = (f32[136,128]{1,0:T(8,128)S(1)}, f32[136,128]{1,0:T(8,128)S(1)}, u32[]{:S(2)}, u32[]{:S(2)}) collective-permute-start(f32[136,128]{1,0:T(8,128)S(1)} %get-tuple-element.45), channel_id=1, source_target_pairs={{0,2},{1,3},{2,0},{3,1},{4,6},{5,7},{6,4},{7,5},{8,10},{9,11},{10,... | collective-permute-start | bytes 208904 | tf_op jit(solution)/shard_map/ppermute | solution.py:270
  44.5 6.5 %collective-permute-start.12 = (f32[136,128]{1,0:T(8,128)S(1)}, f32[136,128]{1,0:T(8,128)S(1)}, u32[]{:S(2)}, u32[]{:S(2)}) collective-permute-start(f32[136,128]{1,0:T(8,128)S(1)} %fusion.3.n0), channel_id=1, source_target_pairs={{0,4},{1,5},{2,6},{3,7},{4,0},{5,1},{6,2},{7,3},{8,12},{9,13},{10,... | collective-permute-start | bytes 208904 | tf_op jit(solution)/shard_map/ppermute | solution.py:270
  46.0 5.6 %collective-permute-start.11 = (f32[136,128]{1,0:T(8,128)S(1)}, f32[136,128]{1,0:T(8,128)S(1)}, u32[]{:S(2)}, u32[]{:S(2)}) collective-permute-start(f32[136,128]{1,0:T(8,128)S(1)} %fusion.3.n0), channel_id=1, source_target_pairs={{0,6},{1,7},{2,4},{3,5},{4,2},{5,3},{6,0},{7,1},{8,14},{9,15},{10,... | collective-permute-start | bytes 208904 | tf_op jit(solution)/shard_map/ppermute | solution.py:270
  47.5 4.3 %collective-permute-start.10 = (f32[136,128]{1,0:T(8,128)S(1)}, f32[136,128]{1,0:T(8,128)S(1)}, u32[]{:S(2)}, u32[]{:S(2)}) collective-permute-start(f32[136,128]{1,0:T(8,128)S(1)} %fusion.3.n0), channel_id=1, source_target_pairs={{0,2},{1,3},{2,0},{3,1},{4,6},{5,7},{6,4},{7,5},{8,10},{9,11},{10,... | collective-permute-start | bytes 208904 | tf_op jit(solution)/shard_map/ppermute | solution.py:270
  51.9 1.8 %collective-permute-start.13 = (f32[4,136,128]{2,1,0:T(8,128)S(1)}, f32[4,136,128]{2,1,0:T(8,128)S(1)}, u32[]{:S(2)}, u32[]{:S(2)}) collective-permute-start(f32[4,136,128]{2,1,0:T(8,128)S(1)} %pad_maximum_fusion.1), channel_id=1, source_target_pairs={{0,1},{1,0},{2,3},{3,2},{4,5},{5,4},{6,7},{7,6},{8,9},{9,8},{10,11... | collective-permute-start | bytes 835592 | tf_op jit(solution)/shard_map/ppermute | solution.py:270
  56.8 6.6 %collective-permute-start.16 = (f32[264,128]{1,0:T(8,128)S(1)}, f32[264,128]{1,0:T(8,128)S(1)}, u32[]{:S(2)}, u32[]{:S(2)}) collective-permute-start(f32[264,128]{1,0:T(8,128)S(1)} %get-tuple-element.27), channel_id=1, source_target_pairs={{0,16},{1,65},{2,18},{3,67},{4,20},{5,69},{6,22},{7,71},{8,24},{9,... | collective-permute-start | bytes 405512 | tf_op jit(solution)/shard_map/ppermute | solution.py:270
  58.7 6.2 %collective-permute-start.15 = (f32[264,128]{1,0:T(8,128)S(1)}, f32[264,128]{1,0:T(8,128)S(1)}, u32[]{:S(2)}, u32[]{:S(2)}) collective-permute-start(f32[264,128]{1,0:T(8,128)S(1)} %get-tuple-element.27), channel_id=1, source_target_pairs={{0,24},{1,97},{2,26},{3,99},{4,28},{5,101},{6,30},{7,103},{8,16},{... | collective-permute-start | bytes 405512 | tf_op jit(solution)/shard_map/ppermute | solution.py:270
  59.8 5.1 %collective-permute-start.14 = (f32[264,128]{1,0:T(8,128)S(1)}, f32[264,128]{1,0:T(8,128)S(1)}, u32[]{:S(2)}, u32[]{:S(2)}) collective-permute-start(f32[264,128]{1,0:T(8,128)S(1)} %get-tuple-element.27), channel_id=1, source_target_pairs={{0,8},{1,33},{2,10},{3,35},{4,12},{5,37},{6,14},{7,39},{8,0},{9,41... | collective-permute-start | bytes 405512 | tf_op jit(solution)/shard_map/ppermute | solution.py:270
  65.0 6.6 %collective-permute-start.19 = (f32[264,128]{1,0:T(8,128)S(1)}, f32[264,128]{1,0:T(8,128)S(1)}, u32[]{:S(2)}, u32[]{:S(2)}) collective-permute-start(f32[264,128]{1,0:T(8,128)S(1)} %add_add_fusion.1.z0), channel_id=1, source_target_pairs={{0,64},{1,17},{2,66},{3,19},{4,68},{5,21},{6,70},{7,23},{8,72},{9,... | collective-permute-start | bytes 405512 | tf_op jit(solution)/shard_map/ppermute | solution.py:270
  66.6 6.4 %collective-permute-start.18 = (f32[264,128]{1,0:T(8,128)S(1)}, f32[264,128]{1,0:T(8,128)S(1)}, u32[]{:S(2)}, u32[]{:S(2)}) collective-permute-start(f32[264,128]{1,0:T(8,128)S(1)} %add_add_fusion.1.z0), channel_id=1, source_target_pairs={{0,96},{1,25},{2,98},{3,27},{4,100},{5,29},{6,102},{7,31},{8,104},... | collective-permute-start | bytes 405512 | tf_op jit(solution)/shard_map/ppermute | solution.py:270
  68.0 5.0 %collective-permute-start.17 = (f32[264,128]{1,0:T(8,128)S(1)}, f32[264,128]{1,0:T(8,128)S(1)}, u32[]{:S(2)}, u32[]{:S(2)}) collective-permute-start(f32[264,128]{1,0:T(8,128)S(1)} %add_add_fusion.1.z0), channel_id=1, source_target_pairs={{0,32},{1,9},{2,34},{3,11},{4,36},{5,13},{6,38},{7,15},{8,40},{9,1... | collective-permute-start | bytes 405512 | tf_op jit(solution)/shard_map/ppermute | solution.py:270
  81.5 6.0 %collective-permute-start.23 = (f32[144,128]{1,0:T(8,128)S(1)}, f32[144,128]{1,0:T(8,128)S(1)}, u32[]{:S(2)}, u32[]{:S(2)}) collective-permute-start(f32[144,128]{1,0:T(8,128)S(1)} %get-tuple-element.40), channel_id=1, source_target_pairs={{0,4},{1,5},{2,6},{3,7},{4,0},{5,1},{6,2},{7,3},{8,12},{9,13},{10,... | collective-permute-start | bytes 221192 | tf_op jit(solution)/shard_map/ppermute | solution.py:270
  83.6 5.6 %collective-permute-start.22 = (f32[144,128]{1,0:T(8,128)S(1)}, f32[144,128]{1,0:T(8,128)S(1)}, u32[]{:S(2)}, u32[]{:S(2)}) collective-permute-start(f32[144,128]{1,0:T(8,128)S(1)} %get-tuple-element.41), channel_id=1, source_target_pairs={{0,6},{1,7},{2,4},{3,5},{4,2},{5,3},{6,0},{7,1},{8,14},{9,15},{10,... | collective-permute-start | bytes 221192 | tf_op jit(solution)/shard_map/ppermute | solution.py:270
  84.8 4.4 %collective-permute-start.21 = (f32[144,128]{1,0:T(8,128)S(1)}, f32[144,128]{1,0:T(8,128)S(1)}, u32[]{:S(2)}, u32[]{:S(2)}) collective-permute-start(f32[144,128]{1,0:T(8,128)S(1)} %get-tuple-element.42), channel_id=1, source_target_pairs={{0,2},{1,3},{2,0},{3,1},{4,6},{5,7},{6,4},{7,5},{8,10},{9,11},{10,... | collective-permute-start | bytes 221192 | tf_op jit(solution)/shard_map/ppermute | solution.py:270
  89.2 6.0 %collective-permute-start.26 = (f32[144,128]{1,0:T(8,128)S(1)}, f32[144,128]{1,0:T(8,128)S(1)}, u32[]{:S(2)}, u32[]{:S(2)}) collective-permute-start(f32[144,128]{1,0:T(8,128)S(1)} %fusion.1.n0), channel_id=1, source_target_pairs={{0,4},{1,5},{2,6},{3,7},{4,0},{5,1},{6,2},{7,3},{8,12},{9,13},{10,... | collective-permute-start | bytes 221192 | tf_op jit(solution)/shard_map/ppermute | solution.py:270
  90.9 5.6 %collective-permute-start.25 = (f32[144,128]{1,0:T(8,128)S(1)}, f32[144,128]{1,0:T(8,128)S(1)}, u32[]{:S(2)}, u32[]{:S(2)}) collective-permute-start(f32[144,128]{1,0:T(8,128)S(1)} %fusion.1.n0), channel_id=1, source_target_pairs={{0,6},{1,7},{2,4},{3,5},{4,2},{5,3},{6,0},{7,1},{8,14},{9,15},{10,... | collective-permute-start | bytes 221192 | tf_op jit(solution)/shard_map/ppermute | solution.py:270
  92.3 4.4 %collective-permute-start.24 = (f32[144,128]{1,0:T(8,128)S(1)}, f32[144,128]{1,0:T(8,128)S(1)}, u32[]{:S(2)}, u32[]{:S(2)}) collective-permute-start(f32[144,128]{1,0:T(8,128)S(1)} %fusion.1.n0), channel_id=1, source_target_pairs={{0,2},{1,3},{2,0},{3,1},{4,6},{5,7},{6,4},{7,5},{8,10},{9,11},{10,... | collective-permute-start | bytes 221192 | tf_op jit(solution)/shard_map/ppermute | solution.py:270
  96.7 1.9 %collective-permute-start.27 = (f32[4,144,128]{2,1,0:T(8,128)S(1)}, f32[4,144,128]{2,1,0:T(8,128)S(1)}, u32[]{:S(2)}, u32[]{:S(2)}) collective-permute-start(f32[4,144,128]{2,1,0:T(8,128)S(1)} %pad_maximum_fusion), channel_id=1, source_target_pairs={{0,1},{1,0},{2,3},{3,2},{4,5},{5,4},{6,7},{7,6},{8,9},{9,8},{10,11... | collective-permute-start | bytes 884744 | tf_op jit(solution)/shard_map/ppermute | solution.py:270
  103.6 6.6 %collective-permute-start.30 = (f32[264,128]{1,0:T(8,128)S(1)}, f32[264,128]{1,0:T(8,128)S(1)}, u32[]{:S(2)}, u32[]{:S(2)}) collective-permute-start(f32[264,128]{1,0:T(8,128)S(1)} %get-tuple-element.34), channel_id=1, source_target_pairs={{0,16},{1,65},{2,18},{3,67},{4,20},{5,69},{6,22},{7,71},{8,24},{9,... | collective-permute-start | bytes 405512 | tf_op jit(solution)/shard_map/ppermute | solution.py:270
  105.8 6.2 %collective-permute-start.29 = (f32[264,128]{1,0:T(8,128)S(1)}, f32[264,128]{1,0:T(8,128)S(1)}, u32[]{:S(2)}, u32[]{:S(2)}) collective-permute-start(f32[264,128]{1,0:T(8,128)S(1)} %get-tuple-element.34), channel_id=1, source_target_pairs={{0,24},{1,97},{2,26},{3,99},{4,28},{5,101},{6,30},{7,103},{8,16},{... | collective-permute-start | bytes 405512 | tf_op jit(solution)/shard_map/ppermute | solution.py:270
  106.7 5.3 %collective-permute-start.28 = (f32[264,128]{1,0:T(8,128)S(1)}, f32[264,128]{1,0:T(8,128)S(1)}, u32[]{:S(2)}, u32[]{:S(2)}) collective-permute-start(f32[264,128]{1,0:T(8,128)S(1)} %get-tuple-element.34), channel_id=1, source_target_pairs={{0,8},{1,33},{2,10},{3,35},{4,12},{5,37},{6,14},{7,39},{8,0},{9,41... | collective-permute-start | bytes 405512 | tf_op jit(solution)/shard_map/ppermute | solution.py:270
  112.1 6.6 %collective-permute-start.33 = (f32[264,128]{1,0:T(8,128)S(1)}, f32[264,128]{1,0:T(8,128)S(1)}, u32[]{:S(2)}, u32[]{:S(2)}) collective-permute-start(f32[264,128]{1,0:T(8,128)S(1)} %add_add_fusion.z0), channel_id=1, source_target_pairs={{0,64},{1,17},{2,66},{3,19},{4,68},{5,21},{6,70},{7,23},{8,72},{9,... | collective-permute-start | bytes 405512 | tf_op jit(solution)/shard_map/ppermute | solution.py:270
  114.2 6.2 %collective-permute-start.32 = (f32[264,128]{1,0:T(8,128)S(1)}, f32[264,128]{1,0:T(8,128)S(1)}, u32[]{:S(2)}, u32[]{:S(2)}) collective-permute-start(f32[264,128]{1,0:T(8,128)S(1)} %add_add_fusion.z0), channel_id=1, source_target_pairs={{0,96},{1,25},{2,98},{3,27},{4,100},{5,29},{6,102},{7,31},{8,104},... | collective-permute-start | bytes 405512 | tf_op jit(solution)/shard_map/ppermute | solution.py:270
  115.4 5.0 %collective-permute-start.31 = (f32[264,128]{1,0:T(8,128)S(1)}, f32[264,128]{1,0:T(8,128)S(1)}, u32[]{:S(2)}, u32[]{:S(2)}) collective-permute-start(f32[264,128]{1,0:T(8,128)S(1)} %add_add_fusion.z0), channel_id=1, source_target_pairs={{0,32},{1,9},{2,34},{3,11},{4,36},{5,13},{6,38},{7,15},{8,40},{9,1... | collective-permute-start | bytes 405512 | tf_op jit(solution)/shard_map/ppermute | solution.py:270
  (2 other events, 3.3 us)

commit v3 on v2

v3 whole, which is shorter than its diff:
```python
import jax
import jax.numpy as jnp
from jax import lax
from jax.experimental import pallas as pl
from jax.experimental.pallas import tpu as pltpu
from jax.sharding import PartitionSpec as P


K = 32
HALF = K // 2
LANES = 128
TILE = 8
XCHIPS = 4
ORDER = (2, 3, 1, 0)
FIRST = ORDER[0]
HERE = (0, 0)
CHUNK = 512
BUFFERS = 4
prio_power = 0.7
weight_power = 0.5
ridge_shift = 0.5
f32, bf16 = jnp.float32, jnp.bfloat16
IN_VMEM = pl.BlockSpec(memory_space=pltpu.VMEM)
IN_SMEM = pl.BlockSpec(memory_space=pltpu.SMEM)
IN_HBM = pl.BlockSpec(memory_space=pltpu.HBM)
ROWS_BY_ROWS = (((1,), (1,)), ((), ()))


def split(value):
    high = value.astype(bf16)
    return high, (value - high.astype(f32)).astype(bf16)


def exact(left, right):
    return jnp.dot(left, right, precision=lax.Precision.HIGHEST, preferred_element_type=f32)


def row_gram(left, right):
    return lax.dot_general(left, right, ROWS_BY_ROWS, precision=lax.Precision.HIGHEST, preferred_element_type=f32)


def solve_t(matrix, rhs_block):
    block = 4
    matrix = 0.5 * (matrix + matrix.T)
    table = jnp.concatenate([matrix, rhs_block], axis=1)
    row_id = lax.broadcasted_iota(jnp.int32, table.shape, 0)
    for k in range(0, K, block):
        columns = [jnp.broadcast_to(table[:, k + j : k + j + 1], table.shape) for j in range(block)]
        rows = [table[k + i : k + i + 1, :] for i in range(block)]
        pivot = [[column[k + i : k + i + 1, :] for column in columns] for i in range(block)]
        for p in range(block):
            inverse = 1.0 / pivot[p][p]
            rows[p] = rows[p] * inverse
            pivot[p] = [value * inverse for value in pivot[p]]
            for i in range(block):
                if i != p:
                    factor = pivot[i][p]
                    rows[i] = rows[i] - factor * rows[p]
                    pivot[i] = [value - factor * over for value, over in zip(pivot[i], pivot[p])]
        for j in range(block):
            table = table - columns[j] * rows[j]
        for i in range(block):
            table = jnp.where(row_id == k + i, rows[i], table)
    return table[:, K:].T


def merged(parts):
    a, b, c, d = (part[...] for part in parts)
    return (a + b) + (c + d)


def pack(square):
    return jnp.concatenate([square[i : i + TILE] for i in range(0, K, TILE)], axis=1)


def unpack(tile):
    return jnp.concatenate([tile[:, i : i + K] for i in range(0, LANES, K)], axis=0)


def put_blocks(out, value, tile):
    blocks = value.shape[1] // LANES
    for j in range(blocks):
        out[j * K : (j + 1) * K, :] = value[:, j * LANES : (j + 1) * LANES]
    out[blocks * K :, :] = tile


def get_blocks(stacked):
    blocks = stacked.shape[0] // K
    value = jnp.concatenate([stacked[j * K : (j + 1) * K] for j in range(blocks)], axis=1)
    return value, stacked[blocks * K :]


def k1(count, ranks_hbm, targets_hbm, features, high, low, scale, out, buf, targets, ranks, pair, sem, in_sem):
    slots, width = features.shape
    steps = slots // CHUNK
    small = [
        pltpu.make_async_copy(ranks_hbm, ranks, in_sem.at[0]),
        pltpu.make_async_copy(targets_hbm, targets, in_sem.at[1]),
    ]
    copies = [
        pltpu.make_async_copy(features.at[pl.ds(c * CHUNK, CHUNK)], buf.at[c % BUFFERS], sem.at[c % BUFFERS])
        for c in range(steps)
    ]
    for copy in small:
        copy.start()
    for c in range(BUFFERS):
        copies[c].start()
    live = lax.broadcasted_iota(jnp.int32, (1, slots), 1) < count[0]
    small[0].wait()
    log_rank = jnp.log(ranks[...].astype(f32))
    scale_now = jnp.where(live, jnp.exp((prio_power * weight_power) * log_rank), 0.0)
    scale[...] = scale_now
    prio_sum = jnp.sum(jnp.where(live, jnp.exp(-prio_power * log_rank), 0.0))
    small[1].wait()
    high_t, low_t = split(targets[...] * scale_now)
    pair[0:K, :] = high_t
    pair[K : 2 * K, :] = low_t
    total = jnp.zeros((2 * K, width), f32)
    rest = jnp.zeros((K, width), f32)
    for c in range(steps):
        at = slice(c * CHUNK, (c + 1) * CHUNK)
        copies[c].wait()
        high_f, low_f = split(buf[c % BUFFERS])
        if c + BUFFERS < steps:
            copies[c + BUFFERS].start()
        high[at, :] = high_f
        low[at, :] = low_f
        total += jnp.dot(pair[:, at], high_f, preferred_element_type=f32)
        rest += jnp.dot(pair[0:K, at], low_f, preferred_element_type=f32)
    row = lax.broadcasted_iota(jnp.int32, (TILE, LANES), 0)
    col = lax.broadcasted_iota(jnp.int32, (TILE, LANES), 1)
    tail = jnp.where(col == 0, prio_sum, jnp.where(col == 1, count[0].astype(f32), 0.0))
    put_blocks(out, total[0:K] + total[K:] + rest, jnp.where(row == 0, tail, 0.0))


def put_images(distance, pair, tiles, high, low, mine, other):
    place = lax.axis_index("feat")
    x, first = place // 2, place % 2 == 0
    part = high.shape[0] // XCHIPS
    base = pl.multiple_of((x ^ distance) * part, part)
    for piece in range(0, part, CHUNK):
        at = pl.ds(pl.multiple_of(base + piece, CHUNK), CHUNK)
        both = lax.dot_general(pair, high[at, :], ROWS_BY_ROWS, preferred_element_type=f32)
        rest = lax.dot_general(pair[0:K], low[at, :], ROWS_BY_ROWS, preferred_element_type=f32)
        value = both[0:K] + both[K:] + rest
        here = jnp.where(first, value[0:HALF], value[HALF:])
        there = jnp.where(first, value[HALF:], value[0:HALF])
        for j in range(0, CHUNK, LANES):
            to = (piece + j) // LANES * HALF
            mine[to : to + HALF, :] = here[:, j : j + LANES]
            other[to : to + HALF, :] = there[:, j : j + LANES]
    mine[part // LANES * HALF :, :] = tiles
    other[part // LANES * HALF :, :] = tiles


def put_pair(value, pair):
    high_v, low_v = split(value)
    pair[0:K, :] = high_v
    pair[K:, :] = low_v


def k2(p0, p1, p2, p3, high, low, field, norm, pair, tiles, mine, other):
    total, tile = get_blocks(merged((p0, p1, p2, p3)))
    factor = jnp.sqrt(tile[0:1, 0:1] / tile[0:1, 1:2])
    norm[...] = jnp.broadcast_to(factor, norm.shape)
    rhs_field = total * factor
    field[...] = rhs_field
    put_pair(rhs_field, pair)
    tiles[...] = pack(row_gram(rhs_field, rhs_field))
    put_images(FIRST, pair[...], tiles[...], high, low, mine, other)


def images_at(distance):
    def images_kernel(pair, tiles, high, low, mine, other):
        put_images(distance, pair[...], tiles[...], high, low, mine, other)

    return images_kernel


def get_images(near, far):
    first = lax.axis_index("feat") % 2 == 0
    blocks = []
    for at in range(0, near.shape[0], HALF):
        a, b = near[at : at + HALF, :], far[at : at + HALF, :]
        blocks.append(jnp.concatenate([jnp.where(first, a, b), jnp.where(first, b, a)], axis=0))
    return jnp.concatenate(blocks, axis=1)


def back_project(distance, images, scale, high, low, before, out):
    x = lax.axis_index("feat") // 2
    part, width = images.shape[1], high.shape[1]
    total = jnp.zeros((2 * K, width), f32)
    rest = jnp.zeros((K, width), f32)
    base = pl.multiple_of((x ^ distance) * part, part)
    high_w, low_w = split(images * scale[:, pl.ds(base, part)])
    pair = jnp.concatenate([high_w, low_w], axis=0)
    curve = lax.dot_general(pair, jnp.concatenate(split(images), axis=0), ROWS_BY_ROWS, preferred_element_type=f32)
    for piece in range(0, part, CHUNK):
        at = pl.ds(pl.multiple_of(base + piece, CHUNK), CHUNK)
        to = slice(piece, piece + CHUNK)
        total += jnp.dot(pair[:, to], high[at, :], preferred_element_type=f32)
        rest += jnp.dot(high_w[:, to], low[at, :], preferred_element_type=f32)
    value = total[0:K] + total[K:] + rest
    tile = pack(curve[0:K, 0:K] + curve[0:K, K:] + curve[K:, 0:K])
    if before is not None:
        value_before, tile_before = get_blocks(before[...])
        value, tile = value_before + value, tile_before + tile
    put_blocks(out, value, tile)


def back_at(distance, begins):
    def back_kernel(near, far, scale, high, low, *rest):
        before, (out, kept) = (None, rest) if begins else (rest[0], rest[1:])
        images = get_images(near, far)
        kept[...] = images
        back_project(distance, images, scale, high, low, before, out)

    return back_kernel


def mixed_back_at(distance, begins):
    def mixed_back_kernel(near, far, scale, high, low, coef, kept, *rest):
        before, (out,) = (None, rest) if begins else (rest[0], rest[1:])
        images = get_images(near, far) + exact(coef[...], kept[...])
        back_project(distance, images, scale, high, low, before, out)

    return mixed_back_kernel


def k4(z0, z1, z2, z3, field, norm, tile_b, high, low, residual, step, pair, tiles, mine, other):
    total, tile = get_blocks(merged((z0, z1, z2, z3)))
    factor = norm[0:1, 0:1]
    gram = unpack(tile_b[...])
    curvature = unpack(tile) * factor + ridge_shift * gram
    step_t = solve_t(curvature, gram)
    step[...] = step_t
    backward = total * factor + ridge_shift * field[...]
    now = field[...] - exact(step_t, backward)
    residual[...] = now
    put_pair(now, pair)
    tiles[0:TILE, :] = pack(row_gram(now, now))
    tiles[TILE:, :] = pack(row_gram(now, field[...]))
    put_images(FIRST, pair[...], tiles[...], high, low, mine, other)


def solve_coef(tile_b, tiles, coef):
    coef[...] = solve_t(unpack(tile_b[...]), unpack(tiles[0:TILE, :]))


def k6(z0, z1, z2, z3, field, residual, norm, tile_b, tiles, step, coef, solution_out, residual_out):
    coef_t = coef[...]
    gram_new = unpack(tiles[0:TILE, :])
    mixed = row_gram(unpack(tiles[TILE:, :]), coef_t)
    square = gram_new + mixed + mixed.T + row_gram(exact(coef_t, unpack(tile_b[...])), coef_t)
    total, tile = get_blocks(merged((z0, z1, z2, z3)))
    factor = norm[0:1, 0:1]
    curvature = unpack(tile) * factor + ridge_shift * square
    step_t = solve_t(curvature, gram_new)
    direction = residual[...] + exact(coef_t, field[...])
    backward = total * factor + ridge_shift * direction
    solution_out[...] = exact(step[...], field[...]) + exact(step_t, direction)
    residual_out[...] = residual[...] - exact(step_t, backward)


def call(kernel, outs, operands, specs=None, scratch=(), passes=0.0):
    cost = pl.CostEstimate(
        flops=int(passes * 3 * 2 * K * 4096 * 1024), bytes_accessed=int(passes * (1 << 24)), transcendentals=0
    )
    return pl.pallas_call(
        kernel,
        out_shape=outs,
        in_specs=specs or [IN_VMEM] * len(operands),
        out_specs=[IN_VMEM] * len(outs),
        scratch_shapes=scratch,
        compiler_params=pltpu.CompilerParams(vmem_limit_bytes=24 << 20),
        cost_estimate=cost,
        name=kernel.__name__,
    )(*operands)


def in_hbm(value):
    return pltpu.with_memory_space_constraint(value, pltpu.HBM)


def exchange(value, row_distance, feat_distance):
    pairs = [
        (r * 8 + f, (r ^ row_distance[f % 2]) * 8 + (f ^ feat_distance)) for r in range(16) for f in range(8)
    ]
    return lax.ppermute(value, ("rows", "feat"), pairs)


def gather_rows(value):
    got = {d: exchange(value, (d, 4 * d), 0) for d in (1, 3, 2)}
    value = (value + got[1]) + (got[3] + got[2])
    got = {d: exchange(value, (4 * d, d), 0) for d in (1, 3, 2)}
    return [value, got[1], got[3], got[2]]


def after(value, *earlier):
    return lax.optimization_barrier((value, *earlier))[0]


def sum_feat(first, images, pair, body):
    got, sent, waits = {}, {}, ()
    for distance in ORDER:
        mine, other = first if distance == FIRST else images(distance, after(pair, *waits))
        other = exchange(other, HERE, 1)
        if distance:
            sent[distance] = mine + other
            got[distance] = exchange(sent[distance], HERE, 2 * distance)
        waits = {ORDER[1]: (sent[FIRST],), ORDER[2]: tuple(sent.values())}.get(distance, ())
    tiles = (sent[FIRST][body:] + got[1][body:]) + (got[3][body:] + got[2][body:])
    return ((mine[0:body] + got[1][0:body]) + (got[3][0:body] + got[2][0:body])) + other[0:body], tiles


def spread_feat(value, project):
    got = {d: exchange(value, HERE, 2 * d) if d else value for d in ORDER}
    before = ()
    far = {d: exchange(got[d], HERE, 1) for d in (0, 1)}
    for d, then in ((0, 3), (1, 2), (3, None), (2, None)):
        before = project(d, got[d], far[d], before)
        if then is not None:
            far[then] = exchange(after(got[then], *before), HERE, 1)
    return before


def local(features, targets, counts, ranks):
    slots, width = features.shape
    part = slots // XCHIPS
    body = part // LANES * HALF
    shape = jax.ShapeDtypeStruct
    summed = shape((width // LANES * K + TILE, LANES), f32)
    field_like, small = shape((K, width), f32), shape((K, K), f32)
    pair_like = shape((2 * K, width), bf16)
    share = 1.0 / XCHIPS

    def tiles_like(tiles):
        return shape((tiles * TILE, LANES), f32)

    def images_like(tiles):
        return [shape((body + tiles * TILE, LANES), f32)] * 2

    high, low, scale, out = call(
        k1,
        [pltpu.VMEM((slots, width), bf16), pltpu.VMEM((slots, width), bf16), shape((1, slots), f32), summed],
        (counts, in_hbm(ranks.reshape(1, slots)), in_hbm(targets), in_hbm(features)),
        [IN_SMEM, IN_HBM, IN_HBM, IN_HBM],
        (
            pltpu.VMEM((BUFFERS, CHUNK, width), f32),
            pltpu.VMEM((K, slots), f32),
            pltpu.VMEM((1, slots), jnp.int32),
            pltpu.VMEM((2 * K, slots), bf16),
            pltpu.SemaphoreType.DMA((BUFFERS,)),
            pltpu.SemaphoreType.DMA((2,)),
        ),
        1.0,
    )

    def images(tiles):
        def of(distance, pair):
            count = tiles.shape[0] // TILE
            return call(images_at(distance), images_like(count), (pair, tiles, high, low), passes=share)

        return of

    parts = gather_rows(out)
    field, norm, pair, tiles, *first = call(
        k2,
        [field_like, tiles_like(1), pair_like, tiles_like(1), *images_like(1)],
        (*parts, high, low),
        passes=share,
    )
    own, tile_b = sum_feat(first, images(tiles), pair, body)
    kept = {}

    def project(distance, near, far, before):
        out, kept[distance] = call(
            back_at(distance, not before),
            [summed, shape((K, part), f32)],
            (near, far, scale, high, low, *before),
            passes=share,
        )
        return (out,)

    parts = gather_rows(*spread_feat(own, project))
    residual, step, pair, tiles, *first = call(
        k4,
        [field_like, small, pair_like, tiles_like(2), *images_like(2)],
        (*parts, field, norm, tile_b, high, low),
        passes=share,
    )
    own, tiles = sum_feat(first, images(tiles), pair, body)
    (coef,) = call(solve_coef, [small], (tile_b, tiles), passes=share)

    def mixed_project(distance, near, far, before):
        return call(
            mixed_back_at(distance, not before),
            [summed],
            (near, far, scale, high, low, coef, kept[distance], *before),
            passes=share,
        )

    parts = gather_rows(*spread_feat(own, mixed_project))
    rest = (field, residual, norm, tile_b, tiles, step, coef)
    return tuple(call(k6, [field_like, field_like], (*parts, *rest)))


def solution(mesh):
    placed = (P("rows", "feat"), P(None, "rows"), P("rows"), P("rows"))
    return jax.shard_map(
        local,
        mesh=mesh,
        in_specs=placed,
        out_specs=(P(None, "feat"), P(None, "feat")),
        check_vma=False,
    )
```

time: 123 us -> 117 us (0.951)
  waiting for transfers between devices: 51.4 us -> 39.2 us
  starting transfers between devices: 39.3 us -> 42.8 us
  Pallas kernels: 30.8 us -> 32.8 us
    ppermute x34 -> x46, waiting for transfers between devices: 51.4 us -> 39.2 us  [exchange(): return lax.ppermute(value, ('rows', 'feat'), pairs)]
    ppermute x34 -> x46, starting transfers between devices: 39.3 us -> 42.8 us  [exchange(): return lax.ppermute(value, ('rows', 'feat'), pairs)]
    pallas_call x6 -> x19, Pallas kernels: 30.8 us -> 32.8 us  [call(): pl.pallas_call(kernel, out_shape=outs, in_specs=specs or [IN_VMEM] * len(...]
  transfers between devices with their start and end apart: 34 -> 46, of which waited for: 26 -> 21; matrix products, arithmetic and copies ran while one was open for 0% -> 0% of each run, Pallas kernels for 0% -> 13%
where the time goes in v3:
time: 117 us; the launch traced here: 116 us
  starting transfers between devices  42.8 us (37%)
  waiting for transfers between devices  39.2 us (34%)
  Pallas kernels  32.8 us (28%)
  between operations  1.49 us (1%)
    ppermute x46, starting transfers between devices, exchange(): return lax.ppermute(value, ('rows', 'feat'), pairs)  42.8 us
    ppermute x46, waiting for transfers between devices, exchange(): return lax.ppermute(value, ('rows', 'feat'), pairs)  39.2 us
    pallas_call x19, Pallas kernels, call(): pl.pallas_call(kernel, out_shape=outs, in_specs=specs or [IN_VMEM] * len(...  32.8 us
  transfers between devices with their start and end apart: 46, of which 21 were waited for; matrix products, arithmetic and copies ran while one was open for 0% of the time, Pallas kernels for 13%

profile of v3, /device:TPU:0, one launch (start us, length us, event | category | flops | bytes accessed | tf_op | source)
XLA Modules:
  0.0 116.5 jit_solution(6894644735481092555)
XLA Ops:
  1.3 7.8 %k1.1 = (bf16[4096,1024]{1,0:T(8,128)(2,1)S(1)}, bf16[4096,1024]{1,0:T(8,128)(2,1)S(1)}, f32[1,4096]{1,0:T(1,128)S(1)}, f32[264,128]{1,0:T(8,128)S(1)}) custom-call(s32[1]{0:T(128)S(6)} %copy.6.count, s32[1,4096]{1,0:T(1,128)} %bitcast.1, f32[32,4096]{1,0:T(8,128)} %targets_hbm.1, f32[4096,1024]{1,0:T(8,128)} %features.1), custom_call_target="tpu_custom_call" | custom-call | flops 805306368 | bytes 16777216 | tf_op jit(solution)/shard_map/k1/pallas_call | solution.py:269
  9.1 4.0 %collective-permute-start.2 = (f32[264,128]{1,0:T(8,128)S(1)}, f32[264,128]{1,0:T(8,128)S(1)}, u32[]{:S(2)}, u32[]{:S(2)}) collective-permute-start(f32[264,128]{1,0:T(8,128)S(1)} %get-tuple-element.46), channel_id=1, source_target_pairs={{0,16},{1,65},{2,18},{3,67},{4,20},{5,69},{6,22},{7,71},{8,24},{9,... | collective-permute-start | bytes 405512 | tf_op jit(solution)/shard_map/ppermute | solution.py:289
  14.2 2.0 %collective-permute-done.2 = f32[264,128]{1,0:T(8,128)S(1)} collective-permute-done((f32[264,128]{1,0:T(8,128)S(1)}, f32[264,128]{1,0:T(8,128)S(1)}, u32[]{:S(2)}, u32[]{:S(2)}) %collective-permute-start.2) | collective-permute-done | bytes 135200 | tf_op jit(solution)/shard_map/ppermute | solution.py:289
  16.1 3.2 %collective-permute-done.1 = f32[264,128]{1,0:T(8,128)S(1)} collective-permute-done((f32[264,128]{1,0:T(8,128)S(1)}, f32[264,128]{1,0:T(8,128)S(1)}, u32[]{:S(2)}, u32[]{:S(2)}) %collective-permute-start.1) | collective-permute-done | bytes 135200 | tf_op jit(solution)/shard_map/ppermute | solution.py:289
  19.4 3.3 %collective-permute-start.5 = (f32[264,128]{1,0:T(8,128)S(1)}, f32[264,128]{1,0:T(8,128)S(1)}, u32[]{:S(2)}, u32[]{:S(2)}) collective-permute-start(f32[264,128]{1,0:T(8,128)S(1)} %add_add_fusion.2.p0), channel_id=1, source_target_pairs={{0,64},{1,17},{2,66},{3,19},{4,68},{5,21},{6,70},{7,23},{8,72},{9,... | collective-permute-start | bytes 405512 | tf_op jit(solution)/shard_map/ppermute | solution.py:289
  23.7 2.3 %collective-permute-done.5.p3 = f32[264,128]{1,0:T(8,128)S(1)} collective-permute-done((f32[264,128]{1,0:T(8,128)S(1)}, f32[264,128]{1,0:T(8,128)S(1)}, u32[]{:S(2)}, u32[]{:S(2)}) %collective-permute-start.5) | collective-permute-done | bytes 135200 | tf_op jit(solution)/shard_map/ppermute | solution.py:289
  26.0 2.9 %collective-permute-done.4.p2 = f32[264,128]{1,0:T(8,128)S(1)} collective-permute-done((f32[264,128]{1,0:T(8,128)S(1)}, f32[264,128]{1,0:T(8,128)S(1)}, u32[]{:S(2)}, u32[]{:S(2)}) %collective-permute-start.4) | collective-permute-done | bytes 135200 | tf_op jit(solution)/shard_map/ppermute | solution.py:289
  28.9 1.6 %k2.1 = (f32[32,1024]{1,0:T(8,128)S(1)}, f32[8,128]{1,0:T(8,128)S(1)}, bf16[64,1024]{1,0:T(8,128)(2,1)S(1)}, f32[8,128]{1,0:T(8,128)S(1)}, f32[136,128]{1,0:T(8,128)S(1)}, /*index=5*/f32[136,128]{1,0:T(8,128)S(1)}) custom-call(f32[264,128]{1,0:T(8,128)S(1)} %add_add_fusion.2.p0, f32[264,128]{1,0:T(8,128)S(1)} %collective-permute-done.3.p1, ...), custom_call_target="tpu_custom_call" | custom-call | flops 201326592 | bytes 4194304 | tf_op jit(solution)/shard_map/k2/pallas_call | solution.py:269
  33.9 3.1 %collective-permute-start.11 = (f32[136,128]{1,0:T(8,128)S(1)}, f32[136,128]{1,0:T(8,128)S(1)}, u32[]{:S(2)}, u32[]{:S(2)}) collective-permute-start(f32[136,128]{1,0:T(8,128)S(1)} %add.90), channel_id=1, source_target_pairs={{0,4},{1,5},{2,6},{3,7},{4,0},{5,1},{6,2},{7,3},{8,12},{9,13},{10,... | collective-permute-start | bytes 208904 | tf_op jit(solution)/shard_map/ppermute | solution.py:289
  40.0 2.6 %collective-permute-done.10 = f32[136,128]{1,0:T(8,128)S(1)} collective-permute-done((f32[136,128]{1,0:T(8,128)S(1)}, f32[136,128]{1,0:T(8,128)S(1)}, u32[]{:S(2)}, u32[]{:S(2)}) %collective-permute-start.10) | collective-permute-done | bytes 69664 | tf_op jit(solution)/shard_map/ppermute | solution.py:289
  43.1 2.0 %collective-permute-start.18 = (f32[128,128]{1,0:T(8,128)S(1)}, f32[128,128]{1,0:T(8,128)S(1)}, u32[]{:S(2)}, u32[]{:S(2)}) collective-permute-start(f32[128,128]{1,0:T(8,128)S(1)} %slice_add_fusion.3.near), channel_id=1, source_target_pairs={{0,6},{1,7},{2,4},{3,5},{4,2},{5,3},{6,0},{7,1},{8,14},{9,15},{10,... | collective-permute-start | bytes 196616 | tf_op jit(solution)/shard_map/ppermute | solution.py:289
  45.2 1.8 %collective-permute-done.14.near = f32[128,128]{1,0:T(8,128)S(1)} collective-permute-done((f32[128,128]{1,0:T(8,128)S(1)}, f32[128,128]{1,0:T(8,128)S(1)}, u32[]{:S(2)}, u32[]{:S(2)}) %collective-permute-start.14) | collective-permute-done | bytes 65568 | tf_op jit(solution)/shard_map/ppermute | solution.py:289
  47.0 1.9 %collective-permute-start.13 = (f32[128,128]{1,0:T(8,128)S(1)}, f32[128,128]{1,0:T(8,128)S(1)}, u32[]{:S(2)}, u32[]{:S(2)}) collective-permute-start(f32[128,128]{1,0:T(8,128)S(1)} %slice_add_fusion.3.near), channel_id=1, source_target_pairs={{0,4},{1,5},{2,6},{3,7},{4,0},{5,1},{6,2},{7,3},{8,12},{9,13},{10,... | collective-permute-start | bytes 196616 | tf_op jit(solution)/shard_map/ppermute | solution.py:289
  50.9 2.1 %collective-permute-done.13.near = f32[128,128]{1,0:T(8,128)S(1)} collective-permute-done((f32[128,128]{1,0:T(8,128)S(1)}, f32[128,128]{1,0:T(8,128)S(1)}, u32[]{:S(2)}, u32[]{:S(2)}) %collective-permute-start.13) | collective-permute-done | bytes 65568 | tf_op jit(solution)/shard_map/ppermute | solution.py:289
  55.1 2.0 %collective-permute-start.22 = (f32[264,128]{1,0:T(8,128)S(1)}, f32[264,128]{1,0:T(8,128)S(1)}, u32[]{:S(2)}, u32[]{:S(2)}) collective-permute-start(f32[264,128]{1,0:T(8,128)S(1)} %get-tuple-element.67), channel_id=1, source_target_pairs={{0,16},{1,65},{2,18},{3,67},{4,20},{5,69},{6,22},{7,71},{8,24},{9,... | collective-permute-start | bytes 405512 | tf_op jit(solution)/shard_map/ppermute | solution.py:289
  58.7 3.0 %collective-permute-done.22 = f32[264,128]{1,0:T(8,128)S(1)} collective-permute-done((f32[264,128]{1,0:T(8,128)S(1)}, f32[264,128]{1,0:T(8,128)S(1)}, u32[]{:S(2)}, u32[]{:S(2)}) %collective-permute-start.22) | collective-permute-done | bytes 135200 | tf_op jit(solution)/shard_map/ppermute | solution.py:289
  61.7 1.6 %collective-permute-done.21 = f32[264,128]{1,0:T(8,128)S(1)} collective-permute-done((f32[264,128]{1,0:T(8,128)S(1)}, f32[264,128]{1,0:T(8,128)S(1)}, u32[]{:S(2)}, u32[]{:S(2)}) %collective-permute-start.21) | collective-permute-done | bytes 135200 | tf_op jit(solution)/shard_map/ppermute | solution.py:289
  63.3 1.6 %collective-permute-start.25 = (f32[264,128]{1,0:T(8,128)S(1)}, f32[264,128]{1,0:T(8,128)S(1)}, u32[]{:S(2)}, u32[]{:S(2)}) collective-permute-start(f32[264,128]{1,0:T(8,128)S(1)} %add_add_fusion.1.z0), channel_id=1, source_target_pairs={{0,64},{1,17},{2,66},{3,19},{4,68},{5,21},{6,70},{7,23},{8,72},{9,... | collective-permute-start | bytes 405512 | tf_op jit(solution)/shard_map/ppermute | solution.py:289
  66.9 3.0 %collective-permute-done.25.z3 = f32[264,128]{1,0:T(8,128)S(1)} collective-permute-done((f32[264,128]{1,0:T(8,128)S(1)}, f32[264,128]{1,0:T(8,128)S(1)}, u32[]{:S(2)}, u32[]{:S(2)}) %collective-permute-start.25) | collective-permute-done | bytes 135200 | tf_op jit(solution)/shard_map/ppermute | solution.py:289
  71.4 3.2 %k4.1 = (f32[32,1024]{1,0:T(8,128)S(1)}, f32[32,32]{1,0:T(8,128)S(1)}, bf16[64,1024]{1,0:T(8,128)(2,1)S(1)}, f32[16,128]{1,0:T(8,128)S(1)}, f32[144,128]{1,0:T(8,128)S(1)}, /*index=5*/f32[144,128]{1,0:T(8,128)S(1)}) custom-call(f32[264,128]{1,0:T(8,128)S(1)} %add_add_fusion.1.z0, f32[264,128]{1,0:T(8,128)S(1)} %collective-permute-done.23.z1, ...), custom_call_target="tpu_custom_call" | custom-call | flops 201326592 | bytes 4194304 | tf_op jit(solution)/shard_map/k4/pallas_call | solution.py:269
  78.0 1.9 %collective-permute-start.31 = (f32[144,128]{1,0:T(8,128)S(1)}, f32[144,128]{1,0:T(8,128)S(1)}, u32[]{:S(2)}, u32[]{:S(2)}) collective-permute-start(f32[144,128]{1,0:T(8,128)S(1)} %add.103), channel_id=1, source_target_pairs={{0,4},{1,5},{2,6},{3,7},{4,0},{5,1},{6,2},{7,3},{8,12},{9,13},{10,... | collective-permute-start | bytes 221192 | tf_op jit(solution)/shard_map/ppermute | solution.py:289
  84.2 1.6 %collective-permute-done.30 = f32[144,128]{1,0:T(8,128)S(1)} collective-permute-done((f32[144,128]{1,0:T(8,128)S(1)}, f32[144,128]{1,0:T(8,128)S(1)}, u32[]{:S(2)}, u32[]{:S(2)}) %collective-permute-start.30) | collective-permute-done | bytes 73760 | tf_op jit(solution)/shard_map/ppermute | solution.py:289
  86.3 2.0 %collective-permute-start.38 = (f32[128,128]{1,0:T(8,128)S(1)}, f32[128,128]{1,0:T(8,128)S(1)}, u32[]{:S(2)}, u32[]{:S(2)}) collective-permute-start(f32[128,128]{1,0:T(8,128)S(1)} %slice_add_fusion.near), channel_id=1, source_target_pairs={{0,6},{1,7},{2,4},{3,5},{4,2},{5,3},{6,0},{7,1},{8,14},{9,15},{10,... | collective-permute-start | bytes 196616 | tf_op jit(solution)/shard_map/ppermute | solution.py:289
  88.3 1.7 %collective-permute-start.33 = (f32[128,128]{1,0:T(8,128)S(1)}, f32[128,128]{1,0:T(8,128)S(1)}, u32[]{:S(2)}, u32[]{:S(2)}) collective-permute-start(f32[128,128]{1,0:T(8,128)S(1)} %slice_add_fusion.near), channel_id=1, source_target_pairs={{0,4},{1,5},{2,6},{3,7},{4,0},{5,1},{6,2},{7,3},{8,12},{9,13},{10,... | collective-permute-start | bytes 196616 | tf_op jit(solution)/shard_map/ppermute | solution.py:289
  90.2 1.5 %solve_coef.1.coef = f32[32,32]{1,0:T(8,128)S(1)} custom-call(f32[8,128]{1,0:T(8,128)S(1)} %fusion.3.tile_b, f32[16,128]{1,0:T(8,128)S(1)} %fusion.2.tiles), custom_call_target="tpu_custom_call" | custom-call | flops 201326592 | bytes 4194304 | tf_op jit(solution)/shard_map/solve_coef/pallas_call | solution.py:269
  96.8 2.2 %collective-permute-start.42 = (f32[264,128]{1,0:T(8,128)S(1)}, f32[264,128]{1,0:T(8,128)S(1)}, u32[]{:S(2)}, u32[]{:S(2)}) collective-permute-start(f32[264,128]{1,0:T(8,128)S(1)} %mixed_back_kernel.7), channel_id=1, source_target_pairs={{0,16},{1,65},{2,18},{3,67},{4,20},{5,69},{6,22},{7,71},{8,24},{9,... | collective-permute-start | bytes 405512 | tf_op jit(solution)/shard_map/ppermute | solution.py:289
  100.3 3.0 %collective-permute-done.42 = f32[264,128]{1,0:T(8,128)S(1)} collective-permute-done((f32[264,128]{1,0:T(8,128)S(1)}, f32[264,128]{1,0:T(8,128)S(1)}, u32[]{:S(2)}, u32[]{:S(2)}) %collective-permute-start.42) | collective-permute-done | bytes 135200 | tf_op jit(solution)/shard_map/ppermute | solution.py:289
  103.4 1.9 %collective-permute-done.41 = f32[264,128]{1,0:T(8,128)S(1)} collective-permute-done((f32[264,128]{1,0:T(8,128)S(1)}, f32[264,128]{1,0:T(8,128)S(1)}, u32[]{:S(2)}, u32[]{:S(2)}) %collective-permute-start.41) | collective-permute-done | bytes 135200 | tf_op jit(solution)/shard_map/ppermute | solution.py:289
  105.3 2.1 %collective-permute-start.45 = (f32[264,128]{1,0:T(8,128)S(1)}, f32[264,128]{1,0:T(8,128)S(1)}, u32[]{:S(2)}, u32[]{:S(2)}) collective-permute-start(f32[264,128]{1,0:T(8,128)S(1)} %add_add_fusion.z0), channel_id=1, source_target_pairs={{0,64},{1,17},{2,66},{3,19},{4,68},{5,21},{6,70},{7,23},{8,72},{9,... | collective-permute-start | bytes 405512 | tf_op jit(solution)/shard_map/ppermute | solution.py:289
  108.8 3.0 %collective-permute-done.45.z3 = f32[264,128]{1,0:T(8,128)S(1)} collective-permute-done((f32[264,128]{1,0:T(8,128)S(1)}, f32[264,128]{1,0:T(8,128)S(1)}, u32[]{:S(2)}, u32[]{:S(2)}) %collective-permute-start.45) | collective-permute-done | bytes 135200 | tf_op jit(solution)/shard_map/ppermute | solution.py:289
  111.9 1.7 %collective-permute-done.44.z2 = f32[264,128]{1,0:T(8,128)S(1)} collective-permute-done((f32[264,128]{1,0:T(8,128)S(1)}, f32[264,128]{1,0:T(8,128)S(1)}, u32[]{:S(2)}, u32[]{:S(2)}) %collective-permute-start.44) | collective-permute-done | bytes 135200 | tf_op jit(solution)/shard_map/ppermute | solution.py:289
  113.6 2.9 %k6.1 = (f32[32,1024]{1,0:T(8,128)}, f32[32,1024]{1,0:T(8,128)}) custom-call(f32[264,128]{1,0:T(8,128)S(1)} %add_add_fusion.z0, f32[264,128]{1,0:T(8,128)S(1)} %collective-permute-done.43.z1, f32[264,128]{1,0:T(8,128)S(1)} %collective-permute-done.44.z2, f32[264,128]{1,0:T(8,128)S(1)} %collective-permute-done.45.z3, f32[32,1024]{1,0:T(8,128)S(1)} %get-tuple-element.68.field, ...), custom_call_target="tpu_custom_call" | custom-call | tf_op jit(solution)/shard_map/k6/pallas_call | solution.py:269
  (92 shorter events, 34.4 us)
Async XLA Ops:
  9.1 7.0 %collective-permute-start.2 = (f32[264,128]{1,0:T(8,128)S(1)}, f32[264,128]{1,0:T(8,128)S(1)}, u32[]{:S(2)}, u32[]{:S(2)}) collective-permute-start(f32[264,128]{1,0:T(8,128)S(1)} %get-tuple-element.46), channel_id=1, source_target_pairs={{0,16},{1,65},{2,18},{3,67},{4,20},{5,69},{6,22},{7,71},{8,24},{9,... | collective-permute-start | bytes 405512 | tf_op jit(solution)/shard_map/ppermute | solution.py:289
  13.1 6.2 %collective-permute-start.1 = (f32[264,128]{1,0:T(8,128)S(1)}, f32[264,128]{1,0:T(8,128)S(1)}, u32[]{:S(2)}, u32[]{:S(2)}) collective-permute-start(f32[264,128]{1,0:T(8,128)S(1)} %get-tuple-element.46), channel_id=1, source_target_pairs={{0,24},{1,97},{2,26},{3,99},{4,28},{5,101},{6,30},{7,103},{8,16},{... | collective-permute-start | bytes 405512 | tf_op jit(solution)/shard_map/ppermute | solution.py:289
  13.9 5.5 %collective-permute-start = (f32[264,128]{1,0:T(8,128)S(1)}, f32[264,128]{1,0:T(8,128)S(1)}, u32[]{:S(2)}, u32[]{:S(2)}) collective-permute-start(f32[264,128]{1,0:T(8,128)S(1)} %get-tuple-element.46), channel_id=1, source_target_pairs={{0,8},{1,33},{2,10},{3,35},{4,12},{5,37},{6,14},{7,39},{8,0},{9,41... | collective-permute-start | bytes 405512 | tf_op jit(solution)/shard_map/ppermute | solution.py:289
  19.4 6.6 %collective-permute-start.5 = (f32[264,128]{1,0:T(8,128)S(1)}, f32[264,128]{1,0:T(8,128)S(1)}, u32[]{:S(2)}, u32[]{:S(2)}) collective-permute-start(f32[264,128]{1,0:T(8,128)S(1)} %add_add_fusion.2.p0), channel_id=1, source_target_pairs={{0,64},{1,17},{2,66},{3,19},{4,68},{5,21},{6,70},{7,23},{8,72},{9,... | collective-permute-start | bytes 405512 | tf_op jit(solution)/shard_map/ppermute | solution.py:289
  22.7 6.2 %collective-permute-start.4 = (f32[264,128]{1,0:T(8,128)S(1)}, f32[264,128]{1,0:T(8,128)S(1)}, u32[]{:S(2)}, u32[]{:S(2)}) collective-permute-start(f32[264,128]{1,0:T(8,128)S(1)} %add_add_fusion.2.p0), channel_id=1, source_target_pairs={{0,96},{1,25},{2,98},{3,27},{4,100},{5,29},{6,102},{7,31},{8,104},... | collective-permute-start | bytes 405512 | tf_op jit(solution)/shard_map/ppermute | solution.py:289
  23.7 5.2 %collective-permute-start.3 = (f32[264,128]{1,0:T(8,128)S(1)}, f32[264,128]{1,0:T(8,128)S(1)}, u32[]{:S(2)}, u32[]{:S(2)}) collective-permute-start(f32[264,128]{1,0:T(8,128)S(1)} %add_add_fusion.2.p0), channel_id=1, source_target_pairs={{0,32},{1,9},{2,34},{3,11},{4,36},{5,13},{6,38},{7,15},{8,40},{9,1... | collective-permute-start | bytes 405512 | tf_op jit(solution)/shard_map/ppermute | solution.py:289
  31.9 5.1 %collective-permute-start.7 = (f32[136,128]{1,0:T(8,128)S(1)}, f32[136,128]{1,0:T(8,128)S(1)}, u32[]{:S(2)}, u32[]{:S(2)}) collective-permute-start(f32[136,128]{1,0:T(8,128)S(1)} %get-tuple-element.54), channel_id=1, source_target_pairs={{0,1},{1,0},{2,3},{3,2},{4,5},{5,4},{6,7},{7,6},{8,9},{9,8},{10,11... | collective-permute-start | bytes 208904 | tf_op jit(solution)/shard_map/ppermute | solution.py:289
  33.8 4.4 %collective-permute-start.8 = (f32[136,128]{1,0:T(8,128)S(1)}, f32[136,128]{1,0:T(8,128)S(1)}, u32[]{:S(2)}, u32[]{:S(2)}) collective-permute-start(f32[136,128]{1,0:T(8,128)S(1)} %get-tuple-element.57), channel_id=1, source_target_pairs={{0,1},{1,0},{2,3},{3,2},{4,5},{5,4},{6,7},{7,6},{8,9},{9,8},{10,11... | collective-permute-start | bytes 208904 | tf_op jit(solution)/shard_map/ppermute | solution.py:289
  33.9 6.1 %collective-permute-start.11 = (f32[136,128]{1,0:T(8,128)S(1)}, f32[136,128]{1,0:T(8,128)S(1)}, u32[]{:S(2)}, u32[]{:S(2)}) collective-permute-start(f32[136,128]{1,0:T(8,128)S(1)} %add.90), channel_id=1, source_target_pairs={{0,4},{1,5},{2,6},{3,7},{4,0},{5,1},{6,2},{7,3},{8,12},{9,13},{10,... | collective-permute-start | bytes 208904 | tf_op jit(solution)/shard_map/ppermute | solution.py:289
  37.0 5.6 %collective-permute-start.10 = (f32[136,128]{1,0:T(8,128)S(1)}, f32[136,128]{1,0:T(8,128)S(1)}, u32[]{:S(2)}, u32[]{:S(2)}) collective-permute-start(f32[136,128]{1,0:T(8,128)S(1)} %add.91), channel_id=1, source_target_pairs={{0,6},{1,7},{2,4},{3,5},{4,2},{5,3},{6,0},{7,1},{8,14},{9,15},{10,... | collective-permute-start | bytes 208904 | tf_op jit(solution)/shard_map/ppermute | solution.py:289
  38.2 4.4 %collective-permute-start.9 = (f32[136,128]{1,0:T(8,128)S(1)}, f32[136,128]{1,0:T(8,128)S(1)}, u32[]{:S(2)}, u32[]{:S(2)}) collective-permute-start(f32[136,128]{1,0:T(8,128)S(1)} %add.92), channel_id=1, source_target_pairs={{0,2},{1,3},{2,0},{3,1},{4,6},{5,7},{6,4},{7,5},{8,10},{9,11},{10,... | collective-permute-start | bytes 208904 | tf_op jit(solution)/shard_map/ppermute | solution.py:289
  43.1 5.7 %collective-permute-start.16 = (f32[128,128]{1,0:T(8,128)S(1)}, f32[128,128]{1,0:T(8,128)S(1)}, u32[]{:S(2)}, u32[]{:S(2)}) collective-permute-start(f32[128,128]{1,0:T(8,128)S(1)} %slice_add_fusion.3.near), channel_id=1, source_target_pairs={{0,1},{1,0},{2,3},{3,2},{4,5},{5,4},{6,7},{7,6},{8,9},{9,8},{10,11... | collective-permute-start | bytes 196616 | tf_op jit(solution)/shard_map/ppermute | solution.py:289
  43.1 6.6 %collective-permute-start.18 = (f32[128,128]{1,0:T(8,128)S(1)}, f32[128,128]{1,0:T(8,128)S(1)}, u32[]{:S(2)}, u32[]{:S(2)}) collective-permute-start(f32[128,128]{1,0:T(8,128)S(1)} %slice_add_fusion.3.near), channel_id=1, source_target_pairs={{0,6},{1,7},{2,4},{3,5},{4,2},{5,3},{6,0},{7,1},{8,14},{9,15},{10,... | collective-permute-start | bytes 196616 | tf_op jit(solution)/shard_map/ppermute | solution.py:289
  47.0 6.0 %collective-permute-start.13 = (f32[128,128]{1,0:T(8,128)S(1)}, f32[128,128]{1,0:T(8,128)S(1)}, u32[]{:S(2)}, u32[]{:S(2)}) collective-permute-start(f32[128,128]{1,0:T(8,128)S(1)} %slice_add_fusion.3.near), channel_id=1, source_target_pairs={{0,4},{1,5},{2,6},{3,7},{4,0},{5,1},{6,2},{7,3},{8,12},{9,13},{10,... | collective-permute-start | bytes 196616 | tf_op jit(solution)/shard_map/ppermute | solution.py:289
  55.1 6.6 %collective-permute-start.22 = (f32[264,128]{1,0:T(8,128)S(1)}, f32[264,128]{1,0:T(8,128)S(1)}, u32[]{:S(2)}, u32[]{:S(2)}) collective-permute-start(f32[264,128]{1,0:T(8,128)S(1)} %get-tuple-element.67), channel_id=1, source_target_pairs={{0,16},{1,65},{2,18},{3,67},{4,20},{5,69},{6,22},{7,71},{8,24},{9,... | collective-permute-start | bytes 405512 | tf_op jit(solution)/shard_map/ppermute | solution.py:289
  57.1 6.2 %collective-permute-start.21 = (f32[264,128]{1,0:T(8,128)S(1)}, f32[264,128]{1,0:T(8,128)S(1)}, u32[]{:S(2)}, u32[]{:S(2)}) collective-permute-start(f32[264,128]{1,0:T(8,128)S(1)} %get-tuple-element.67), channel_id=1, source_target_pairs={{0,24},{1,97},{2,26},{3,99},{4,28},{5,101},{6,30},{7,103},{8,16},{... | collective-permute-start | bytes 405512 | tf_op jit(solution)/shard_map/ppermute | solution.py:289
  58.2 5.2 %collective-permute-start.20 = (f32[264,128]{1,0:T(8,128)S(1)}, f32[264,128]{1,0:T(8,128)S(1)}, u32[]{:S(2)}, u32[]{:S(2)}) collective-permute-start(f32[264,128]{1,0:T(8,128)S(1)} %get-tuple-element.67), channel_id=1, source_target_pairs={{0,8},{1,33},{2,10},{3,35},{4,12},{5,37},{6,14},{7,39},{8,0},{9,41... | collective-permute-start | bytes 405512 | tf_op jit(solution)/shard_map/ppermute | solution.py:289
  63.3 6.6 %collective-permute-start.25 = (f32[264,128]{1,0:T(8,128)S(1)}, f32[264,128]{1,0:T(8,128)S(1)}, u32[]{:S(2)}, u32[]{:S(2)}) collective-permute-start(f32[264,128]{1,0:T(8,128)S(1)} %add_add_fusion.1.z0), channel_id=1, source_target_pairs={{0,64},{1,17},{2,66},{3,19},{4,68},{5,21},{6,70},{7,23},{8,72},{9,... | collective-permute-start | bytes 405512 | tf_op jit(solution)/shard_map/ppermute | solution.py:289
  65.0 6.4 %collective-permute-start.24 = (f32[264,128]{1,0:T(8,128)S(1)}, f32[264,128]{1,0:T(8,128)S(1)}, u32[]{:S(2)}, u32[]{:S(2)}) collective-permute-start(f32[264,128]{1,0:T(8,128)S(1)} %add_add_fusion.1.z0), channel_id=1, source_target_pairs={{0,96},{1,25},{2,98},{3,27},{4,100},{5,29},{6,102},{7,31},{8,104},... | collective-permute-start | bytes 405512 | tf_op jit(solution)/shard_map/ppermute | solution.py:289
  66.4 5.0 %collective-permute-start.23 = (f32[264,128]{1,0:T(8,128)S(1)}, f32[264,128]{1,0:T(8,128)S(1)}, u32[]{:S(2)}, u32[]{:S(2)}) collective-permute-start(f32[264,128]{1,0:T(8,128)S(1)} %add_add_fusion.1.z0), channel_id=1, source_target_pairs={{0,32},{1,9},{2,34},{3,11},{4,36},{5,13},{6,38},{7,15},{8,40},{9,1... | collective-permute-start | bytes 405512 | tf_op jit(solution)/shard_map/ppermute | solution.py:289
  78.0 6.2 %collective-permute-start.31 = (f32[144,128]{1,0:T(8,128)S(1)}, f32[144,128]{1,0:T(8,128)S(1)}, u32[]{:S(2)}, u32[]{:S(2)}) collective-permute-start(f32[144,128]{1,0:T(8,128)S(1)} %add.103), channel_id=1, source_target_pairs={{0,4},{1,5},{2,6},{3,7},{4,0},{5,1},{6,2},{7,3},{8,12},{9,13},{10,... | collective-permute-start | bytes 221192 | tf_op jit(solution)/shard_map/ppermute | solution.py:289
  80.0 5.8 %collective-permute-start.30 = (f32[144,128]{1,0:T(8,128)S(1)}, f32[144,128]{1,0:T(8,128)S(1)}, u32[]{:S(2)}, u32[]{:S(2)}) collective-permute-start(f32[144,128]{1,0:T(8,128)S(1)} %add.104), channel_id=1, source_target_pairs={{0,6},{1,7},{2,4},{3,5},{4,2},{5,3},{6,0},{7,1},{8,14},{9,15},{10,... | collective-permute-start | bytes 221192 | tf_op jit(solution)/shard_map/ppermute | solution.py:289
  81.2 4.5 %collective-permute-start.29 = (f32[144,128]{1,0:T(8,128)S(1)}, f32[144,128]{1,0:T(8,128)S(1)}, u32[]{:S(2)}, u32[]{:S(2)}) collective-permute-start(f32[144,128]{1,0:T(8,128)S(1)} %add.105), channel_id=1, source_target_pairs={{0,2},{1,3},{2,0},{3,1},{4,6},{5,7},{6,4},{7,5},{8,10},{9,11},{10,... | collective-permute-start | bytes 221192 | tf_op jit(solution)/shard_map/ppermute | solution.py:289
  85.8 4.3 %collective-permute-start.34 = (f32[128,128]{1,0:T(8,128)S(1)}, f32[128,128]{1,0:T(8,128)S(1)}, u32[]{:S(2)}, u32[]{:S(2)}) collective-permute-start(f32[128,128]{1,0:T(8,128)S(1)} %slice_add_fusion.near), channel_id=1, source_target_pairs={{0,2},{1,3},{2,0},{3,1},{4,6},{5,7},{6,4},{7,5},{8,10},{9,11},{10,... | collective-permute-start | bytes 196616 | tf_op jit(solution)/shard_map/ppermute | solution.py:289
  86.3 6.5 %collective-permute-start.38 = (f32[128,128]{1,0:T(8,128)S(1)}, f32[128,128]{1,0:T(8,128)S(1)}, u32[]{:S(2)}, u32[]{:S(2)}) collective-permute-start(f32[128,128]{1,0:T(8,128)S(1)} %slice_add_fusion.near), channel_id=1, source_target_pairs={{0,6},{1,7},{2,4},{3,5},{4,2},{5,3},{6,0},{7,1},{8,14},{9,15},{10,... | collective-permute-start | bytes 196616 | tf_op jit(solution)/shard_map/ppermute | solution.py:289
  88.3 6.1 %collective-permute-start.33 = (f32[128,128]{1,0:T(8,128)S(1)}, f32[128,128]{1,0:T(8,128)S(1)}, u32[]{:S(2)}, u32[]{:S(2)}) collective-permute-start(f32[128,128]{1,0:T(8,128)S(1)} %slice_add_fusion.near), channel_id=1, source_target_pairs={{0,4},{1,5},{2,6},{3,7},{4,0},{5,1},{6,2},{7,3},{8,12},{9,13},{10,... | collective-permute-start | bytes 196616 | tf_op jit(solution)/shard_map/ppermute | solution.py:289
  96.8 6.6 %collective-permute-start.42 = (f32[264,128]{1,0:T(8,128)S(1)}, f32[264,128]{1,0:T(8,128)S(1)}, u32[]{:S(2)}, u32[]{:S(2)}) collective-permute-start(f32[264,128]{1,0:T(8,128)S(1)} %mixed_back_kernel.7), channel_id=1, source_target_pairs={{0,16},{1,65},{2,18},{3,67},{4,20},{5,69},{6,22},{7,71},{8,24},{9,... | collective-permute-start | bytes 405512 | tf_op jit(solution)/shard_map/ppermute | solution.py:289
  99.0 6.2 %collective-permute-start.41 = (f32[264,128]{1,0:T(8,128)S(1)}, f32[264,128]{1,0:T(8,128)S(1)}, u32[]{:S(2)}, u32[]{:S(2)}) collective-permute-start(f32[264,128]{1,0:T(8,128)S(1)} %mixed_back_kernel.7), channel_id=1, source_target_pairs={{0,24},{1,97},{2,26},{3,99},{4,28},{5,101},{6,30},{7,103},{8,16},{... | collective-permute-start | bytes 405512 | tf_op jit(solution)/shard_map/ppermute | solution.py:289
  99.9 5.3 %collective-permute-start.40 = (f32[264,128]{1,0:T(8,128)S(1)}, f32[264,128]{1,0:T(8,128)S(1)}, u32[]{:S(2)}, u32[]{:S(2)}) collective-permute-start(f32[264,128]{1,0:T(8,128)S(1)} %mixed_back_kernel.7), channel_id=1, source_target_pairs={{0,8},{1,33},{2,10},{3,35},{4,12},{5,37},{6,14},{7,39},{8,0},{9,41... | collective-permute-start | bytes 405512 | tf_op jit(solution)/shard_map/ppermute | solution.py:289
  105.3 6.6 %collective-permute-start.45 = (f32[264,128]{1,0:T(8,128)S(1)}, f32[264,128]{1,0:T(8,128)S(1)}, u32[]{:S(2)}, u32[]{:S(2)}) collective-permute-start(f32[264,128]{1,0:T(8,128)S(1)} %add_add_fusion.z0), channel_id=1, source_target_pairs={{0,64},{1,17},{2,66},{3,19},{4,68},{5,21},{6,70},{7,23},{8,72},{9,... | collective-permute-start | bytes 405512 | tf_op jit(solution)/shard_map/ppermute | solution.py:289
  107.3 6.2 %collective-permute-start.44 = (f32[264,128]{1,0:T(8,128)S(1)}, f32[264,128]{1,0:T(8,128)S(1)}, u32[]{:S(2)}, u32[]{:S(2)}) collective-permute-start(f32[264,128]{1,0:T(8,128)S(1)} %add_add_fusion.z0), channel_id=1, source_target_pairs={{0,96},{1,25},{2,98},{3,27},{4,100},{5,29},{6,102},{7,31},{8,104},... | collective-permute-start | bytes 405512 | tf_op jit(solution)/shard_map/ppermute | solution.py:289
  108.5 5.0 %collective-permute-start.43 = (f32[264,128]{1,0:T(8,128)S(1)}, f32[264,128]{1,0:T(8,128)S(1)}, u32[]{:S(2)}, u32[]{:S(2)}) collective-permute-start(f32[264,128]{1,0:T(8,128)S(1)} %add_add_fusion.z0), channel_id=1, source_target_pairs={{0,32},{1,9},{2,34},{3,11},{4,36},{5,13},{6,38},{7,15},{8,40},{9,1... | collective-permute-start | bytes 405512 | tf_op jit(solution)/shard_map/ppermute | solution.py:289
  (14 other events, 38.4 us)

commit v4 on v3

--- a/solution.py
+++ b/solution.py
@@ -15,7 +15,8 @@
 FIRST = ORDER[0]
 HERE = (0, 0)
 CHUNK = 512
-BUFFERS = 4
+STREAM = 256
+BUFFERS = 8
 prio_power = 0.7
 weight_power = 0.5
 ridge_shift = 0.5
@@ -40,27 +41,28 @@
 
 
 def solve_t(matrix, rhs_block):
-    block = 4
     matrix = 0.5 * (matrix + matrix.T)
     table = jnp.concatenate([matrix, rhs_block], axis=1)
-    row_id = lax.broadcasted_iota(jnp.int32, table.shape, 0)
-    for k in range(0, K, block):
-        columns = [jnp.broadcast_to(table[:, k + j : k + j + 1], table.shape) for j in range(block)]
-        rows = [table[k + i : k + i + 1, :] for i in range(block)]
-        pivot = [[column[k + i : k + i + 1, :] for column in columns] for i in range(block)]
-        for p in range(block):
+    for k in range(0, K, TILE):
+        columns = [jnp.broadcast_to(table[:, k + j : k + j + 1], table.shape) for j in range(TILE)]
+        rows = [table[k + i : k + i + 1, :] for i in range(TILE)]
+        pivot = [[column[k + i : k + i + 1, :] for column in columns] for i in range(TILE)]
+        for p in range(TILE):
             inverse = 1.0 / pivot[p][p]
             rows[p] = rows[p] * inverse
             pivot[p] = [value * inverse for value in pivot[p]]
-            for i in range(block):
+            for i in range(TILE):
                 if i != p:
                     factor = pivot[i][p]
                     rows[i] = rows[i] - factor * rows[p]
-                    pivot[i] = [value - factor * over for value, over in zip(pivot[i], pivot[p])]
-        for j in range(block):
-            table = table - columns[j] * rows[j]
-        for i in range(block):
-            table = jnp.where(row_id == k + i, rows[i], table)
+                    for j in range(p + 1, TILE):
+                        pivot[i][j] = pivot[i][j] - factor * pivot[p][j]
+        change = columns[0] * rows[0]
+        for j in range(1, TILE):
+            change = change + columns[j] * rows[j]
+        table = table - change
+        pieces = [table[0:k], *rows, table[k + TILE :]]
+        table = jnp.concatenate([piece for piece in pieces if piece.shape[0]], axis=0)
     return table[:, K:].T
 
 
@@ -90,15 +92,15 @@
     return value, stacked[blocks * K :]
 
 
-def k1(count, ranks_hbm, targets_hbm, features, high, low, scale, out, buf, targets, ranks, pair, sem, in_sem):
+def k1(count, ranks_hbm, targets_hbm, features, high, low, scale, out, buf, targets, ranks, sem, in_sem):
     slots, width = features.shape
-    steps = slots // CHUNK
+    steps = slots // STREAM
     small = [
         pltpu.make_async_copy(ranks_hbm, ranks, in_sem.at[0]),
         pltpu.make_async_copy(targets_hbm, targets, in_sem.at[1]),
     ]
     copies = [
-        pltpu.make_async_copy(features.at[pl.ds(c * CHUNK, CHUNK)], buf.at[c % BUFFERS], sem.at[c % BUFFERS])
+        pltpu.make_async_copy(features.at[pl.ds(c * STREAM, STREAM)], buf.at[c % BUFFERS], sem.at[c % BUFFERS])
         for c in range(steps)
     ]
     for copy in small:
@@ -112,21 +114,19 @@
     scale[...] = scale_now
     prio_sum = jnp.sum(jnp.where(live, jnp.exp(-prio_power * log_rank), 0.0))
     small[1].wait()
-    high_t, low_t = split(targets[...] * scale_now)
-    pair[0:K, :] = high_t
-    pair[K : 2 * K, :] = low_t
     total = jnp.zeros((2 * K, width), f32)
     rest = jnp.zeros((K, width), f32)
     for c in range(steps):
-        at = slice(c * CHUNK, (c + 1) * CHUNK)
+        at = slice(c * STREAM, (c + 1) * STREAM)
+        high_t, low_t = split(targets[:, at] * scale_now[:, at])
         copies[c].wait()
         high_f, low_f = split(buf[c % BUFFERS])
         if c + BUFFERS < steps:
             copies[c + BUFFERS].start()
         high[at, :] = high_f
         low[at, :] = low_f
-        total += jnp.dot(pair[:, at], high_f, preferred_element_type=f32)
-        rest += jnp.dot(pair[0:K, at], low_f, preferred_element_type=f32)
+        total += jnp.dot(jnp.concatenate([high_t, low_t], axis=0), high_f, preferred_element_type=f32)
+        rest += jnp.dot(high_t, low_f, preferred_element_type=f32)
     row = lax.broadcasted_iota(jnp.int32, (TILE, LANES), 0)
     col = lax.broadcasted_iota(jnp.int32, (TILE, LANES), 1)
     tail = jnp.where(col == 0, prio_sum, jnp.where(col == 1, count[0].astype(f32), 0.0))
@@ -247,18 +247,21 @@
     coef[...] = solve_t(unpack(tile_b[...]), unpack(tiles[0:TILE, :]))
 
 
-def k6(z0, z1, z2, z3, field, residual, norm, tile_b, tiles, step, coef, solution_out, residual_out):
+def prepare(field, residual, tile_b, tiles, step, coef, begun, direction, square):
     coef_t = coef[...]
-    gram_new = unpack(tiles[0:TILE, :])
     mixed = row_gram(unpack(tiles[TILE:, :]), coef_t)
-    square = gram_new + mixed + mixed.T + row_gram(exact(coef_t, unpack(tile_b[...])), coef_t)
+    square[...] = unpack(tiles[0:TILE, :]) + mixed + mixed.T + row_gram(exact(coef_t, unpack(tile_b[...])), coef_t)
+    direction[...] = residual[...] + exact(coef_t, field[...])
+    begun[...] = exact(step[...], field[...])
+
+
+def k6(z0, z1, z2, z3, residual, norm, tiles, begun, direction, square, solution_out, residual_out):
     total, tile = get_blocks(merged((z0, z1, z2, z3)))
     factor = norm[0:1, 0:1]
-    curvature = unpack(tile) * factor + ridge_shift * square
-    step_t = solve_t(curvature, gram_new)
-    direction = residual[...] + exact(coef_t, field[...])
-    backward = total * factor + ridge_shift * direction
-    solution_out[...] = exact(step[...], field[...]) + exact(step_t, direction)
+    curvature = unpack(tile) * factor + ridge_shift * square[...]
+    step_t = solve_t(curvature, unpack(tiles[0:TILE, :]))
+    backward = total * factor + ridge_shift * direction[...]
+    solution_out[...] = begun[...] + exact(step_t, direction[...])
     residual_out[...] = residual[...] - exact(step_t, backward)
 
 
@@ -315,12 +318,12 @@
 
 def spread_feat(value, project):
     got = {d: exchange(value, HERE, 2 * d) if d else value for d in ORDER}
-    before = ()
-    far = {d: exchange(got[d], HERE, 1) for d in (0, 1)}
-    for d, then in ((0, 3), (1, 2), (3, None), (2, None)):
+    far = {0: exchange(got[0], HERE, 1)}
+    before = project(0, got[0], far[0], ())
+    for d in (2, 3, 1):
+        far[d] = exchange(after(got[d], *before), HERE, 1)
+    for d in (2, 3, 1):
         before = project(d, got[d], far[d], before)
-        if then is not None:
-            far[then] = exchange(after(got[then], *before), HERE, 1)
     return before
 
 
@@ -346,10 +349,9 @@
         (counts, in_hbm(ranks.reshape(1, slots)), in_hbm(targets), in_hbm(features)),
         [IN_SMEM, IN_HBM, IN_HBM, IN_HBM],
         (
-            pltpu.VMEM((BUFFERS, CHUNK, width), f32),
+            pltpu.VMEM((BUFFERS, STREAM, width), f32),
             pltpu.VMEM((K, slots), f32),
             pltpu.VMEM((1, slots), jnp.int32),
-            pltpu.VMEM((2 * K, slots), bf16),
             pltpu.SemaphoreType.DMA((BUFFERS,)),
             pltpu.SemaphoreType.DMA((2,)),
         ),
@@ -378,7 +380,7 @@
             back_at(distance, not before),
             [summed, shape((K, part), f32)],
             (near, far, scale, high, low, *before),
-            passes=share,
+            passes=share if before else share,
         )
         return (out,)
 
@@ -401,8 +403,8 @@
         )
 
     parts = gather_rows(*spread_feat(own, mixed_project))
-    rest = (field, residual, norm, tile_b, tiles, step, coef)
-    return tuple(call(k6, [field_like, field_like], (*parts, *rest)))
+    ready = call(prepare, [field_like, field_like, small], (field, residual, tile_b, tiles, step, coef))
+    return tuple(call(k6, [field_like, field_like], (*parts, residual, norm, tiles, *ready)))
 
 
 def solution(mesh):

time: 117 us -> 114 us (0.974)
  starting transfers between devices: 42.8 us -> 41.5 us
    ppermute x46, starting transfers between devices: 42.8 us -> 41.5 us  [exchange(): return lax.ppermute(value, ('rows', 'feat'), pairs)]
    pallas_call x19 -> x20, Pallas kernels: 32.8 us -> 31.8 us  [call(): pl.pallas_call(kernel, out_shape=outs, in_specs=specs or [IN_VMEM] * len(...]
  transfers between devices with their start and end apart: 46 -> 46, of which waited for: 21 -> 20; matrix products, arithmetic and copies ran while one was open for 0% -> 0% of each run, Pallas kernels for 13% -> 14%
where the time goes in v4:
time: 114 us
  starting transfers between devices  41.5 us (36%)
  waiting for transfers between devices  38.6 us (34%)
  Pallas kernels  31.8 us (28%)
  between operations  1.5 us (1%)
    ppermute x46, starting transfers between devices, exchange(): return lax.ppermute(value, ('rows', 'feat'), pairs)  41.5 us
    ppermute x46, waiting for transfers between devices, exchange(): return lax.ppermute(value, ('rows', 'feat'), pairs)  38.6 us
    pallas_call x20, Pallas kernels, call(): pl.pallas_call(kernel, out_shape=outs, in_specs=specs or [IN_VMEM] * len(...  31.8 us
  transfers between devices with their start and end apart: 46, of which 20 were waited for; matrix products, arithmetic and copies ran while one was open for 0% of the time, Pallas kernels for 14%

profile of v4, /device:TPU:0, one launch (start us, length us, event | category | flops | bytes accessed | tf_op | source)
XLA Modules:
  0.0 113.5 jit_solution(14669091616631980586)
XLA Ops:
  1.3 7.5 %k1.1 = (bf16[4096,1024]{1,0:T(8,128)(2,1)S(1)}, bf16[4096,1024]{1,0:T(8,128)(2,1)S(1)}, f32[1,4096]{1,0:T(1,128)S(1)}, f32[264,128]{1,0:T(8,128)S(1)}) custom-call(s32[1]{0:T(128)S(6)} %copy.6.count, s32[1,4096]{1,0:T(1,128)} %bitcast.1, f32[32,4096]{1,0:T(8,128)} %targets_hbm.1, f32[4096,1024]{1,0:T(8,128)} %features.1), custom_call_target="tpu_custom_call" | custom-call | flops 805306368 | bytes 16777216 | tf_op jit(solution)/shard_map/k1/pallas_call | solution.py:272
  8.8 4.0 %collective-permute-start.2 = (f32[264,128]{1,0:T(8,128)S(1)}, f32[264,128]{1,0:T(8,128)S(1)}, u32[]{:S(2)}, u32[]{:S(2)}) collective-permute-start(f32[264,128]{1,0:T(8,128)S(1)} %get-tuple-element.51), channel_id=1, source_target_pairs={{0,16},{1,65},{2,18},{3,67},{4,20},{5,69},{6,22},{7,71},{8,24},{9,... | collective-permute-start | bytes 405512 | tf_op jit(solution)/shard_map/ppermute | solution.py:292
  13.9 2.0 %collective-permute-done.2 = f32[264,128]{1,0:T(8,128)S(1)} collective-permute-done((f32[264,128]{1,0:T(8,128)S(1)}, f32[264,128]{1,0:T(8,128)S(1)}, u32[]{:S(2)}, u32[]{:S(2)}) %collective-permute-start.2) | collective-permute-done | bytes 135200 | tf_op jit(solution)/shard_map/ppermute | solution.py:292
  15.9 3.2 %collective-permute-done.1 = f32[264,128]{1,0:T(8,128)S(1)} collective-permute-done((f32[264,128]{1,0:T(8,128)S(1)}, f32[264,128]{1,0:T(8,128)S(1)}, u32[]{:S(2)}, u32[]{:S(2)}) %collective-permute-start.1) | collective-permute-done | bytes 135200 | tf_op jit(solution)/shard_map/ppermute | solution.py:292
  19.1 3.3 %collective-permute-start.5 = (f32[264,128]{1,0:T(8,128)S(1)}, f32[264,128]{1,0:T(8,128)S(1)}, u32[]{:S(2)}, u32[]{:S(2)}) collective-permute-start(f32[264,128]{1,0:T(8,128)S(1)} %add_add_fusion.2.p0), channel_id=1, source_target_pairs={{0,64},{1,17},{2,66},{3,19},{4,68},{5,21},{6,70},{7,23},{8,72},{9,... | collective-permute-start | bytes 405512 | tf_op jit(solution)/shard_map/ppermute | solution.py:292
  23.5 2.3 %collective-permute-done.5.p3 = f32[264,128]{1,0:T(8,128)S(1)} collective-permute-done((f32[264,128]{1,0:T(8,128)S(1)}, f32[264,128]{1,0:T(8,128)S(1)}, u32[]{:S(2)}, u32[]{:S(2)}) %collective-permute-start.5) | collective-permute-done | bytes 135200 | tf_op jit(solution)/shard_map/ppermute | solution.py:292
  25.7 2.9 %collective-permute-done.4.p2 = f32[264,128]{1,0:T(8,128)S(1)} collective-permute-done((f32[264,128]{1,0:T(8,128)S(1)}, f32[264,128]{1,0:T(8,128)S(1)}, u32[]{:S(2)}, u32[]{:S(2)}) %collective-permute-start.4) | collective-permute-done | bytes 135200 | tf_op jit(solution)/shard_map/ppermute | solution.py:292
  28.6 1.6 %k2.1 = (f32[32,1024]{1,0:T(8,128)S(1)}, f32[8,128]{1,0:T(8,128)S(1)}, bf16[64,1024]{1,0:T(8,128)(2,1)S(1)}, f32[8,128]{1,0:T(8,128)S(1)}, f32[136,128]{1,0:T(8,128)S(1)}, /*index=5*/f32[136,128]{1,0:T(8,128)S(1)}) custom-call(f32[264,128]{1,0:T(8,128)S(1)} %add_add_fusion.2.p0, f32[264,128]{1,0:T(8,128)S(1)} %collective-permute-done.3.p1, ...), custom_call_target="tpu_custom_call" | custom-call | flops 201326592 | bytes 4194304 | tf_op jit(solution)/shard_map/k2/pallas_call | solution.py:272
  33.6 3.1 %collective-permute-start.11 = (f32[136,128]{1,0:T(8,128)S(1)}, f32[136,128]{1,0:T(8,128)S(1)}, u32[]{:S(2)}, u32[]{:S(2)}) collective-permute-start(f32[136,128]{1,0:T(8,128)S(1)} %add.90), channel_id=1, source_target_pairs={{0,4},{1,5},{2,6},{3,7},{4,0},{5,1},{6,2},{7,3},{8,12},{9,13},{10,... | collective-permute-start | bytes 208904 | tf_op jit(solution)/shard_map/ppermute | solution.py:292
  39.7 2.6 %collective-permute-done.10 = f32[136,128]{1,0:T(8,128)S(1)} collective-permute-done((f32[136,128]{1,0:T(8,128)S(1)}, f32[136,128]{1,0:T(8,128)S(1)}, u32[]{:S(2)}, u32[]{:S(2)}) %collective-permute-start.10) | collective-permute-done | bytes 69664 | tf_op jit(solution)/shard_map/ppermute | solution.py:292
  42.5 2.0 %collective-permute-start.18 = (f32[128,128]{1,0:T(8,128)S(1)}, f32[128,128]{1,0:T(8,128)S(1)}, u32[]{:S(2)}, u32[]{:S(2)}) collective-permute-start(f32[128,128]{1,0:T(8,128)S(1)} %slice_add_fusion.3.near), channel_id=1, source_target_pairs={{0,4},{1,5},{2,6},{3,7},{4,0},{5,1},{6,2},{7,3},{8,12},{9,13},{10,... | collective-permute-start | bytes 196616 | tf_op jit(solution)/shard_map/ppermute | solution.py:292
  46.9 1.6 %collective-permute-done.18.near = f32[128,128]{1,0:T(8,128)S(1)} collective-permute-done((f32[128,128]{1,0:T(8,128)S(1)}, f32[128,128]{1,0:T(8,128)S(1)}, u32[]{:S(2)}, u32[]{:S(2)}) %collective-permute-start.18) | collective-permute-done | bytes 65568 | tf_op jit(solution)/shard_map/ppermute | solution.py:292
  48.5 1.5 %collective-permute-done.16.near = f32[128,128]{1,0:T(8,128)S(1)} collective-permute-done((f32[128,128]{1,0:T(8,128)S(1)}, f32[128,128]{1,0:T(8,128)S(1)}, u32[]{:S(2)}, u32[]{:S(2)}) %collective-permute-start.16) | collective-permute-done | bytes 65568 | tf_op jit(solution)/shard_map/ppermute | solution.py:292
  53.1 2.0 %collective-permute-start.22 = (f32[264,128]{1,0:T(8,128)S(1)}, f32[264,128]{1,0:T(8,128)S(1)}, u32[]{:S(2)}, u32[]{:S(2)}) collective-permute-start(f32[264,128]{1,0:T(8,128)S(1)} %get-tuple-element.73), channel_id=1, source_target_pairs={{0,16},{1,65},{2,18},{3,67},{4,20},{5,69},{6,22},{7,71},{8,24},{9,... | collective-permute-start | bytes 405512 | tf_op jit(solution)/shard_map/ppermute | solution.py:292
  56.7 3.0 %collective-permute-done.22 = f32[264,128]{1,0:T(8,128)S(1)} collective-permute-done((f32[264,128]{1,0:T(8,128)S(1)}, f32[264,128]{1,0:T(8,128)S(1)}, u32[]{:S(2)}, u32[]{:S(2)}) %collective-permute-start.22) | collective-permute-done | bytes 135200 | tf_op jit(solution)/shard_map/ppermute | solution.py:292
  59.7 1.6 %collective-permute-done.21 = f32[264,128]{1,0:T(8,128)S(1)} collective-permute-done((f32[264,128]{1,0:T(8,128)S(1)}, f32[264,128]{1,0:T(8,128)S(1)}, u32[]{:S(2)}, u32[]{:S(2)}) %collective-permute-start.21) | collective-permute-done | bytes 135200 | tf_op jit(solution)/shard_map/ppermute | solution.py:292
  61.3 1.6 %collective-permute-start.25 = (f32[264,128]{1,0:T(8,128)S(1)}, f32[264,128]{1,0:T(8,128)S(1)}, u32[]{:S(2)}, u32[]{:S(2)}) collective-permute-start(f32[264,128]{1,0:T(8,128)S(1)} %add_add_fusion.1.z0), channel_id=1, source_target_pairs={{0,64},{1,17},{2,66},{3,19},{4,68},{5,21},{6,70},{7,23},{8,72},{9,... | collective-permute-start | bytes 405512 | tf_op jit(solution)/shard_map/ppermute | solution.py:292
  62.9 1.4 %collective-permute-start.24 = (f32[264,128]{1,0:T(8,128)S(1)}, f32[264,128]{1,0:T(8,128)S(1)}, u32[]{:S(2)}, u32[]{:S(2)}) collective-permute-start(f32[264,128]{1,0:T(8,128)S(1)} %add_add_fusion.1.z0), channel_id=1, source_target_pairs={{0,96},{1,25},{2,98},{3,27},{4,100},{5,29},{6,102},{7,31},{8,104},... | collective-permute-start | bytes 405512 | tf_op jit(solution)/shard_map/ppermute | solution.py:292
  64.9 3.0 %collective-permute-done.25.z3 = f32[264,128]{1,0:T(8,128)S(1)} collective-permute-done((f32[264,128]{1,0:T(8,128)S(1)}, f32[264,128]{1,0:T(8,128)S(1)}, u32[]{:S(2)}, u32[]{:S(2)}) %collective-permute-start.25) | collective-permute-done | bytes 135200 | tf_op jit(solution)/shard_map/ppermute | solution.py:292
  67.9 1.4 %collective-permute-done.24.z2 = f32[264,128]{1,0:T(8,128)S(1)} collective-permute-done((f32[264,128]{1,0:T(8,128)S(1)}, f32[264,128]{1,0:T(8,128)S(1)}, u32[]{:S(2)}, u32[]{:S(2)}) %collective-permute-start.24) | collective-permute-done | bytes 135200 | tf_op jit(solution)/shard_map/ppermute | solution.py:292
  69.4 2.9 %k4.1 = (f32[32,1024]{1,0:T(8,128)S(1)}, f32[32,32]{1,0:T(8,128)S(1)}, bf16[64,1024]{1,0:T(8,128)(2,1)S(1)}, f32[16,128]{1,0:T(8,128)S(1)}, f32[144,128]{1,0:T(8,128)S(1)}, /*index=5*/f32[144,128]{1,0:T(8,128)S(1)}) custom-call(f32[264,128]{1,0:T(8,128)S(1)} %add_add_fusion.1.z0, f32[264,128]{1,0:T(8,128)S(1)} %collective-permute-done.23.z1, ...), custom_call_target="tpu_custom_call" | custom-call | flops 201326592 | bytes 4194304 | tf_op jit(solution)/shard_map/k4/pallas_call | solution.py:272
  75.7 1.7 %collective-permute-start.31 = (f32[144,128]{1,0:T(8,128)S(1)}, f32[144,128]{1,0:T(8,128)S(1)}, u32[]{:S(2)}, u32[]{:S(2)}) collective-permute-start(f32[144,128]{1,0:T(8,128)S(1)} %add.103), channel_id=1, source_target_pairs={{0,4},{1,5},{2,6},{3,7},{4,0},{5,1},{6,2},{7,3},{8,12},{9,13},{10,... | collective-permute-start | bytes 221192 | tf_op jit(solution)/shard_map/ppermute | solution.py:292
  77.4 1.4 %collective-permute-start.30 = (f32[144,128]{1,0:T(8,128)S(1)}, f32[144,128]{1,0:T(8,128)S(1)}, u32[]{:S(2)}, u32[]{:S(2)}) collective-permute-start(f32[144,128]{1,0:T(8,128)S(1)} %add.104), channel_id=1, source_target_pairs={{0,6},{1,7},{2,4},{3,5},{4,2},{5,3},{6,0},{7,1},{8,14},{9,15},{10,... | collective-permute-start | bytes 221192 | tf_op jit(solution)/shard_map/ppermute | solution.py:292
  81.9 1.5 %collective-permute-done.30 = f32[144,128]{1,0:T(8,128)S(1)} collective-permute-done((f32[144,128]{1,0:T(8,128)S(1)}, f32[144,128]{1,0:T(8,128)S(1)}, u32[]{:S(2)}, u32[]{:S(2)}) %collective-permute-start.30) | collective-permute-done | bytes 73760 | tf_op jit(solution)/shard_map/ppermute | solution.py:292
  83.4 1.9 %collective-permute-start.38 = (f32[128,128]{1,0:T(8,128)S(1)}, f32[128,128]{1,0:T(8,128)S(1)}, u32[]{:S(2)}, u32[]{:S(2)}) collective-permute-start(f32[128,128]{1,0:T(8,128)S(1)} %slice_add_fusion.near), channel_id=1, source_target_pairs={{0,4},{1,5},{2,6},{3,7},{4,0},{5,1},{6,2},{7,3},{8,12},{9,13},{10,... | collective-permute-start | bytes 196616 | tf_op jit(solution)/shard_map/ppermute | solution.py:292
  94.5 2.2 %collective-permute-start.42 = (f32[264,128]{1,0:T(8,128)S(1)}, f32[264,128]{1,0:T(8,128)S(1)}, u32[]{:S(2)}, u32[]{:S(2)}) collective-permute-start(f32[264,128]{1,0:T(8,128)S(1)} %mixed_back_kernel.7), channel_id=1, source_target_pairs={{0,16},{1,65},{2,18},{3,67},{4,20},{5,69},{6,22},{7,71},{8,24},{9,... | collective-permute-start | bytes 405512 | tf_op jit(solution)/shard_map/ppermute | solution.py:292
  98.1 3.0 %collective-permute-done.42 = f32[264,128]{1,0:T(8,128)S(1)} collective-permute-done((f32[264,128]{1,0:T(8,128)S(1)}, f32[264,128]{1,0:T(8,128)S(1)}, u32[]{:S(2)}, u32[]{:S(2)}) %collective-permute-start.42) | collective-permute-done | bytes 135200 | tf_op jit(solution)/shard_map/ppermute | solution.py:292
  101.1 1.9 %collective-permute-done.41 = f32[264,128]{1,0:T(8,128)S(1)} collective-permute-done((f32[264,128]{1,0:T(8,128)S(1)}, f32[264,128]{1,0:T(8,128)S(1)}, u32[]{:S(2)}, u32[]{:S(2)}) %collective-permute-start.41) | collective-permute-done | bytes 135200 | tf_op jit(solution)/shard_map/ppermute | solution.py:292
  103.0 2.1 %collective-permute-start.45 = (f32[264,128]{1,0:T(8,128)S(1)}, f32[264,128]{1,0:T(8,128)S(1)}, u32[]{:S(2)}, u32[]{:S(2)}) collective-permute-start(f32[264,128]{1,0:T(8,128)S(1)} %add_add_fusion.z0), channel_id=1, source_target_pairs={{0,64},{1,17},{2,66},{3,19},{4,68},{5,21},{6,70},{7,23},{8,72},{9,... | collective-permute-start | bytes 405512 | tf_op jit(solution)/shard_map/ppermute | solution.py:292
  107.2 2.4 %collective-permute-done.45.z3 = f32[264,128]{1,0:T(8,128)S(1)} collective-permute-done((f32[264,128]{1,0:T(8,128)S(1)}, f32[264,128]{1,0:T(8,128)S(1)}, u32[]{:S(2)}, u32[]{:S(2)}) %collective-permute-start.45) | collective-permute-done | bytes 135200 | tf_op jit(solution)/shard_map/ppermute | solution.py:292
  109.6 1.7 %collective-permute-done.44.z2 = f32[264,128]{1,0:T(8,128)S(1)} collective-permute-done((f32[264,128]{1,0:T(8,128)S(1)}, f32[264,128]{1,0:T(8,128)S(1)}, u32[]{:S(2)}, u32[]{:S(2)}) %collective-permute-start.44) | collective-permute-done | bytes 135200 | tf_op jit(solution)/shard_map/ppermute | solution.py:292
  111.3 2.2 %k6.1 = (f32[32,1024]{1,0:T(8,128)}, f32[32,1024]{1,0:T(8,128)}) custom-call(f32[264,128]{1,0:T(8,128)S(1)} %add_add_fusion.z0, f32[264,128]{1,0:T(8,128)S(1)} %collective-permute-done.43.z1, f32[264,128]{1,0:T(8,128)S(1)} %collective-permute-done.44.z2, f32[264,128]{1,0:T(8,128)S(1)} %collective-permute-done.45.z3, ...), custom_call_target="tpu_custom_call" | custom-call | tf_op jit(solution)/shard_map/k6/pallas_call | solution.py:272
  (93 shorter events, 35.3 us)
Async XLA Ops:
  8.8 7.0 %collective-permute-start.2 = (f32[264,128]{1,0:T(8,128)S(1)}, f32[264,128]{1,0:T(8,128)S(1)}, u32[]{:S(2)}, u32[]{:S(2)}) collective-permute-start(f32[264,128]{1,0:T(8,128)S(1)} %get-tuple-element.51), channel_id=1, source_target_pairs={{0,16},{1,65},{2,18},{3,67},{4,20},{5,69},{6,22},{7,71},{8,24},{9,... | collective-permute-start | bytes 405512 | tf_op jit(solution)/shard_map/ppermute | solution.py:292
  12.9 6.2 %collective-permute-start.1 = (f32[264,128]{1,0:T(8,128)S(1)}, f32[264,128]{1,0:T(8,128)S(1)}, u32[]{:S(2)}, u32[]{:S(2)}) collective-permute-start(f32[264,128]{1,0:T(8,128)S(1)} %get-tuple-element.51), channel_id=1, source_target_pairs={{0,24},{1,97},{2,26},{3,99},{4,28},{5,101},{6,30},{7,103},{8,16},{... | collective-permute-start | bytes 405512 | tf_op jit(solution)/shard_map/ppermute | solution.py:292
  13.6 5.5 %collective-permute-start = (f32[264,128]{1,0:T(8,128)S(1)}, f32[264,128]{1,0:T(8,128)S(1)}, u32[]{:S(2)}, u32[]{:S(2)}) collective-permute-start(f32[264,128]{1,0:T(8,128)S(1)} %get-tuple-element.51), channel_id=1, source_target_pairs={{0,8},{1,33},{2,10},{3,35},{4,12},{5,37},{6,14},{7,39},{8,0},{9,41... | collective-permute-start | bytes 405512 | tf_op jit(solution)/shard_map/ppermute | solution.py:292
  19.1 6.6 %collective-permute-start.5 = (f32[264,128]{1,0:T(8,128)S(1)}, f32[264,128]{1,0:T(8,128)S(1)}, u32[]{:S(2)}, u32[]{:S(2)}) collective-permute-start(f32[264,128]{1,0:T(8,128)S(1)} %add_add_fusion.2.p0), channel_id=1, source_target_pairs={{0,64},{1,17},{2,66},{3,19},{4,68},{5,21},{6,70},{7,23},{8,72},{9,... | collective-permute-start | bytes 405512 | tf_op jit(solution)/shard_map/ppermute | solution.py:292
  22.4 6.2 %collective-permute-start.4 = (f32[264,128]{1,0:T(8,128)S(1)}, f32[264,128]{1,0:T(8,128)S(1)}, u32[]{:S(2)}, u32[]{:S(2)}) collective-permute-start(f32[264,128]{1,0:T(8,128)S(1)} %add_add_fusion.2.p0), channel_id=1, source_target_pairs={{0,96},{1,25},{2,98},{3,27},{4,100},{5,29},{6,102},{7,31},{8,104},... | collective-permute-start | bytes 405512 | tf_op jit(solution)/shard_map/ppermute | solution.py:292
  23.5 5.2 %collective-permute-start.3 = (f32[264,128]{1,0:T(8,128)S(1)}, f32[264,128]{1,0:T(8,128)S(1)}, u32[]{:S(2)}, u32[]{:S(2)}) collective-permute-start(f32[264,128]{1,0:T(8,128)S(1)} %add_add_fusion.2.p0), channel_id=1, source_target_pairs={{0,32},{1,9},{2,34},{3,11},{4,36},{5,13},{6,38},{7,15},{8,40},{9,1... | collective-permute-start | bytes 405512 | tf_op jit(solution)/shard_map/ppermute | solution.py:292
  31.6 5.1 %collective-permute-start.7 = (f32[136,128]{1,0:T(8,128)S(1)}, f32[136,128]{1,0:T(8,128)S(1)}, u32[]{:S(2)}, u32[]{:S(2)}) collective-permute-start(f32[136,128]{1,0:T(8,128)S(1)} %get-tuple-element.59), channel_id=1, source_target_pairs={{0,1},{1,0},{2,3},{3,2},{4,5},{5,4},{6,7},{7,6},{8,9},{9,8},{10,11... | collective-permute-start | bytes 208904 | tf_op jit(solution)/shard_map/ppermute | solution.py:292
  33.5 4.4 %collective-permute-start.8 = (f32[136,128]{1,0:T(8,128)S(1)}, f32[136,128]{1,0:T(8,128)S(1)}, u32[]{:S(2)}, u32[]{:S(2)}) collective-permute-start(f32[136,128]{1,0:T(8,128)S(1)} %get-tuple-element.62), channel_id=1, source_target_pairs={{0,1},{1,0},{2,3},{3,2},{4,5},{5,4},{6,7},{7,6},{8,9},{9,8},{10,11... | collective-permute-start | bytes 208904 | tf_op jit(solution)/shard_map/ppermute | solution.py:292
  33.6 6.1 %collective-permute-start.11 = (f32[136,128]{1,0:T(8,128)S(1)}, f32[136,128]{1,0:T(8,128)S(1)}, u32[]{:S(2)}, u32[]{:S(2)}) collective-permute-start(f32[136,128]{1,0:T(8,128)S(1)} %add.90), channel_id=1, source_target_pairs={{0,4},{1,5},{2,6},{3,7},{4,0},{5,1},{6,2},{7,3},{8,12},{9,13},{10,... | collective-permute-start | bytes 208904 | tf_op jit(solution)/shard_map/ppermute | solution.py:292
  36.7 5.6 %collective-permute-start.10 = (f32[136,128]{1,0:T(8,128)S(1)}, f32[136,128]{1,0:T(8,128)S(1)}, u32[]{:S(2)}, u32[]{:S(2)}) collective-permute-start(f32[136,128]{1,0:T(8,128)S(1)} %add.91), channel_id=1, source_target_pairs={{0,6},{1,7},{2,4},{3,5},{4,2},{5,3},{6,0},{7,1},{8,14},{9,15},{10,... | collective-permute-start | bytes 208904 | tf_op jit(solution)/shard_map/ppermute | solution.py:292
  37.9 4.4 %collective-permute-start.9 = (f32[136,128]{1,0:T(8,128)S(1)}, f32[136,128]{1,0:T(8,128)S(1)}, u32[]{:S(2)}, u32[]{:S(2)}) collective-permute-start(f32[136,128]{1,0:T(8,128)S(1)} %add.92), channel_id=1, source_target_pairs={{0,2},{1,3},{2,0},{3,1},{4,6},{5,7},{6,4},{7,5},{8,10},{9,11},{10,... | collective-permute-start | bytes 208904 | tf_op jit(solution)/shard_map/ppermute | solution.py:292
  42.5 6.0 %collective-permute-start.18 = (f32[128,128]{1,0:T(8,128)S(1)}, f32[128,128]{1,0:T(8,128)S(1)}, u32[]{:S(2)}, u32[]{:S(2)}) collective-permute-start(f32[128,128]{1,0:T(8,128)S(1)} %slice_add_fusion.3.near), channel_id=1, source_target_pairs={{0,4},{1,5},{2,6},{3,7},{4,0},{5,1},{6,2},{7,3},{8,12},{9,13},{10,... | collective-permute-start | bytes 196616 | tf_op jit(solution)/shard_map/ppermute | solution.py:292
  44.5 5.5 %collective-permute-start.16 = (f32[128,128]{1,0:T(8,128)S(1)}, f32[128,128]{1,0:T(8,128)S(1)}, u32[]{:S(2)}, u32[]{:S(2)}) collective-permute-start(f32[128,128]{1,0:T(8,128)S(1)} %slice_add_fusion.3.near), channel_id=1, source_target_pairs={{0,6},{1,7},{2,4},{3,5},{4,2},{5,3},{6,0},{7,1},{8,14},{9,15},{10,... | collective-permute-start | bytes 196616 | tf_op jit(solution)/shard_map/ppermute | solution.py:292
  45.6 4.3 %collective-permute-start.13 = (f32[128,128]{1,0:T(8,128)S(1)}, f32[128,128]{1,0:T(8,128)S(1)}, u32[]{:S(2)}, u32[]{:S(2)}) collective-permute-start(f32[128,128]{1,0:T(8,128)S(1)} %slice_add_fusion.3.near), channel_id=1, source_target_pairs={{0,2},{1,3},{2,0},{3,1},{4,6},{5,7},{6,4},{7,5},{8,10},{9,11},{10,... | collective-permute-start | bytes 196616 | tf_op jit(solution)/shard_map/ppermute | solution.py:292
  53.1 6.6 %collective-permute-start.22 = (f32[264,128]{1,0:T(8,128)S(1)}, f32[264,128]{1,0:T(8,128)S(1)}, u32[]{:S(2)}, u32[]{:S(2)}) collective-permute-start(f32[264,128]{1,0:T(8,128)S(1)} %get-tuple-element.73), channel_id=1, source_target_pairs={{0,16},{1,65},{2,18},{3,67},{4,20},{5,69},{6,22},{7,71},{8,24},{9,... | collective-permute-start | bytes 405512 | tf_op jit(solution)/shard_map/ppermute | solution.py:292
  55.1 6.2 %collective-permute-start.21 = (f32[264,128]{1,0:T(8,128)S(1)}, f32[264,128]{1,0:T(8,128)S(1)}, u32[]{:S(2)}, u32[]{:S(2)}) collective-permute-start(f32[264,128]{1,0:T(8,128)S(1)} %get-tuple-element.73), channel_id=1, source_target_pairs={{0,24},{1,97},{2,26},{3,99},{4,28},{5,101},{6,30},{7,103},{8,16},{... | collective-permute-start | bytes 405512 | tf_op jit(solution)/shard_map/ppermute | solution.py:292
  56.1 5.1 %collective-permute-start.20 = (f32[264,128]{1,0:T(8,128)S(1)}, f32[264,128]{1,0:T(8,128)S(1)}, u32[]{:S(2)}, u32[]{:S(2)}) collective-permute-start(f32[264,128]{1,0:T(8,128)S(1)} %get-tuple-element.73), channel_id=1, source_target_pairs={{0,8},{1,33},{2,10},{3,35},{4,12},{5,37},{6,14},{7,39},{8,0},{9,41... | collective-permute-start | bytes 405512 | tf_op jit(solution)/shard_map/ppermute | solution.py:292
  61.3 6.6 %collective-permute-start.25 = (f32[264,128]{1,0:T(8,128)S(1)}, f32[264,128]{1,0:T(8,128)S(1)}, u32[]{:S(2)}, u32[]{:S(2)}) collective-permute-start(f32[264,128]{1,0:T(8,128)S(1)} %add_add_fusion.1.z0), channel_id=1, source_target_pairs={{0,64},{1,17},{2,66},{3,19},{4,68},{5,21},{6,70},{7,23},{8,72},{9,... | collective-permute-start | bytes 405512 | tf_op jit(solution)/shard_map/ppermute | solution.py:292
  62.9 6.4 %collective-permute-start.24 = (f32[264,128]{1,0:T(8,128)S(1)}, f32[264,128]{1,0:T(8,128)S(1)}, u32[]{:S(2)}, u32[]{:S(2)}) collective-permute-start(f32[264,128]{1,0:T(8,128)S(1)} %add_add_fusion.1.z0), channel_id=1, source_target_pairs={{0,96},{1,25},{2,98},{3,27},{4,100},{5,29},{6,102},{7,31},{8,104},... | collective-permute-start | bytes 405512 | tf_op jit(solution)/shard_map/ppermute | solution.py:292
  64.3 5.0 %collective-permute-start.23 = (f32[264,128]{1,0:T(8,128)S(1)}, f32[264,128]{1,0:T(8,128)S(1)}, u32[]{:S(2)}, u32[]{:S(2)}) collective-permute-start(f32[264,128]{1,0:T(8,128)S(1)} %add_add_fusion.1.z0), channel_id=1, source_target_pairs={{0,32},{1,9},{2,34},{3,11},{4,36},{5,13},{6,38},{7,15},{8,40},{9,1... | collective-permute-start | bytes 405512 | tf_op jit(solution)/shard_map/ppermute | solution.py:292
  75.7 6.2 %collective-permute-start.31 = (f32[144,128]{1,0:T(8,128)S(1)}, f32[144,128]{1,0:T(8,128)S(1)}, u32[]{:S(2)}, u32[]{:S(2)}) collective-permute-start(f32[144,128]{1,0:T(8,128)S(1)} %add.103), channel_id=1, source_target_pairs={{0,4},{1,5},{2,6},{3,7},{4,0},{5,1},{6,2},{7,3},{8,12},{9,13},{10,... | collective-permute-start | bytes 221192 | tf_op jit(solution)/shard_map/ppermute | solution.py:292
  77.4 6.0 %collective-permute-start.30 = (f32[144,128]{1,0:T(8,128)S(1)}, f32[144,128]{1,0:T(8,128)S(1)}, u32[]{:S(2)}, u32[]{:S(2)}) collective-permute-start(f32[144,128]{1,0:T(8,128)S(1)} %add.104), channel_id=1, source_target_pairs={{0,6},{1,7},{2,4},{3,5},{4,2},{5,3},{6,0},{7,1},{8,14},{9,15},{10,... | collective-permute-start | bytes 221192 | tf_op jit(solution)/shard_map/ppermute | solution.py:292
  78.8 4.6 %collective-permute-start.29 = (f32[144,128]{1,0:T(8,128)S(1)}, f32[144,128]{1,0:T(8,128)S(1)}, u32[]{:S(2)}, u32[]{:S(2)}) collective-permute-start(f32[144,128]{1,0:T(8,128)S(1)} %add.105), channel_id=1, source_target_pairs={{0,2},{1,3},{2,0},{3,1},{4,6},{5,7},{6,4},{7,5},{8,10},{9,11},{10,... | collective-permute-start | bytes 221192 | tf_op jit(solution)/shard_map/ppermute | solution.py:292
  83.4 5.9 %collective-permute-start.38 = (f32[128,128]{1,0:T(8,128)S(1)}, f32[128,128]{1,0:T(8,128)S(1)}, u32[]{:S(2)}, u32[]{:S(2)}) collective-permute-start(f32[128,128]{1,0:T(8,128)S(1)} %slice_add_fusion.near), channel_id=1, source_target_pairs={{0,4},{1,5},{2,6},{3,7},{4,0},{5,1},{6,2},{7,3},{8,12},{9,13},{10,... | collective-permute-start | bytes 196616 | tf_op jit(solution)/shard_map/ppermute | solution.py:292
  85.3 5.5 %collective-permute-start.36 = (f32[128,128]{1,0:T(8,128)S(1)}, f32[128,128]{1,0:T(8,128)S(1)}, u32[]{:S(2)}, u32[]{:S(2)}) collective-permute-start(f32[128,128]{1,0:T(8,128)S(1)} %slice_add_fusion.near), channel_id=1, source_target_pairs={{0,6},{1,7},{2,4},{3,5},{4,2},{5,3},{6,0},{7,1},{8,14},{9,15},{10,... | collective-permute-start | bytes 196616 | tf_op jit(solution)/shard_map/ppermute | solution.py:292
  86.5 4.5 %collective-permute-start.33 = (f32[128,128]{1,0:T(8,128)S(1)}, f32[128,128]{1,0:T(8,128)S(1)}, u32[]{:S(2)}, u32[]{:S(2)}) collective-permute-start(f32[128,128]{1,0:T(8,128)S(1)} %slice_add_fusion.near), channel_id=1, source_target_pairs={{0,2},{1,3},{2,0},{3,1},{4,6},{5,7},{6,4},{7,5},{8,10},{9,11},{10,... | collective-permute-start | bytes 196616 | tf_op jit(solution)/shard_map/ppermute | solution.py:292
  94.5 6.6 %collective-permute-start.42 = (f32[264,128]{1,0:T(8,128)S(1)}, f32[264,128]{1,0:T(8,128)S(1)}, u32[]{:S(2)}, u32[]{:S(2)}) collective-permute-start(f32[264,128]{1,0:T(8,128)S(1)} %mixed_back_kernel.7), channel_id=1, source_target_pairs={{0,16},{1,65},{2,18},{3,67},{4,20},{5,69},{6,22},{7,71},{8,24},{9,... | collective-permute-start | bytes 405512 | tf_op jit(solution)/shard_map/ppermute | solution.py:292
  96.7 6.2 %collective-permute-start.41 = (f32[264,128]{1,0:T(8,128)S(1)}, f32[264,128]{1,0:T(8,128)S(1)}, u32[]{:S(2)}, u32[]{:S(2)}) collective-permute-start(f32[264,128]{1,0:T(8,128)S(1)} %mixed_back_kernel.7), channel_id=1, source_target_pairs={{0,24},{1,97},{2,26},{3,99},{4,28},{5,101},{6,30},{7,103},{8,16},{... | collective-permute-start | bytes 405512 | tf_op jit(solution)/shard_map/ppermute | solution.py:292
  97.6 5.3 %collective-permute-start.40 = (f32[264,128]{1,0:T(8,128)S(1)}, f32[264,128]{1,0:T(8,128)S(1)}, u32[]{:S(2)}, u32[]{:S(2)}) collective-permute-start(f32[264,128]{1,0:T(8,128)S(1)} %mixed_back_kernel.7), channel_id=1, source_target_pairs={{0,8},{1,33},{2,10},{3,35},{4,12},{5,37},{6,14},{7,39},{8,0},{9,41... | collective-permute-start | bytes 405512 | tf_op jit(solution)/shard_map/ppermute | solution.py:292
  103.0 6.6 %collective-permute-start.45 = (f32[264,128]{1,0:T(8,128)S(1)}, f32[264,128]{1,0:T(8,128)S(1)}, u32[]{:S(2)}, u32[]{:S(2)}) collective-permute-start(f32[264,128]{1,0:T(8,128)S(1)} %add_add_fusion.z0), channel_id=1, source_target_pairs={{0,64},{1,17},{2,66},{3,19},{4,68},{5,21},{6,70},{7,23},{8,72},{9,... | collective-permute-start | bytes 405512 | tf_op jit(solution)/shard_map/ppermute | solution.py:292
  105.1 6.2 %collective-permute-start.44 = (f32[264,128]{1,0:T(8,128)S(1)}, f32[264,128]{1,0:T(8,128)S(1)}, u32[]{:S(2)}, u32[]{:S(2)}) collective-permute-start(f32[264,128]{1,0:T(8,128)S(1)} %add_add_fusion.z0), channel_id=1, source_target_pairs={{0,96},{1,25},{2,98},{3,27},{4,100},{5,29},{6,102},{7,31},{8,104},... | collective-permute-start | bytes 405512 | tf_op jit(solution)/shard_map/ppermute | solution.py:292
  106.3 5.0 %collective-permute-start.43 = (f32[264,128]{1,0:T(8,128)S(1)}, f32[264,128]{1,0:T(8,128)S(1)}, u32[]{:S(2)}, u32[]{:S(2)}) collective-permute-start(f32[264,128]{1,0:T(8,128)S(1)} %add_add_fusion.z0), channel_id=1, source_target_pairs={{0,32},{1,9},{2,34},{3,11},{4,36},{5,13},{6,38},{7,15},{8,40},{9,1... | collective-permute-start | bytes 405512 | tf_op jit(solution)/shard_map/ppermute | solution.py:292
  (14 other events, 33.4 us)

commit v5 on v4

--- a/solution.py
+++ b/solution.py
@@ -219,47 +219,56 @@
 
 
 def mixed_back_at(distance, begins):
-    def mixed_back_kernel(near, far, scale, high, low, coef, kept, *rest):
+    def mixed_back_kernel(near, far, scale, high, low, mix, kept, *rest):
         before, (out,) = (None, rest) if begins else (rest[0], rest[1:])
-        images = get_images(near, far) + exact(coef[...], kept[...])
+        was = kept[...]
+        images = was + exact(mix[...], jnp.concatenate([was, get_images(near, far)], axis=0))
         back_project(distance, images, scale, high, low, before, out)
 
     return mixed_back_kernel
 
 
-def k4(z0, z1, z2, z3, field, norm, tile_b, high, low, residual, step, pair, tiles, mine, other):
+def k4(z0, z1, z2, z3, field, norm, high, low, applied, curve, pair, tiles, mine, other):
     total, tile = get_blocks(merged((z0, z1, z2, z3)))
     factor = norm[0:1, 0:1]
+    curve[...] = tile * factor
+    backward = total * factor + ridge_shift * field[...]
+    applied[...] = backward
+    put_pair(backward, pair)
+    tiles[0:TILE, :] = pack(row_gram(backward, backward))
+    tiles[TILE:, :] = pack(row_gram(backward, field[...]))
+    put_images(FIRST, pair[...], tiles[...], high, low, mine, other)
+
+
+def first_step(curve, tile_b, step):
     gram = unpack(tile_b[...])
-    curvature = unpack(tile) * factor + ridge_shift * gram
-    step_t = solve_t(curvature, gram)
-    step[...] = step_t
-    backward = total * factor + ridge_shift * field[...]
-    now = field[...] - exact(step_t, backward)
+    step[...] = solve_t(unpack(curve[...]) + ridge_shift * gram, gram)
+
+
+def solve_coef(tile_b, tiles, step, mix, gram_new, cross):
+    gram, step_t = unpack(tile_b[...]), step[...]
+    moved = exact(step_t, unpack(tiles[TILE:, :]))
+    square = gram - moved - moved.T + row_gram(exact(step_t, unpack(tiles[0:TILE, :])), step_t)
+    gram_new[...] = square
+    cross[...] = gram - moved
+    mix[...] = jnp.concatenate([solve_t(gram, square), -step_t], axis=1)
+
+
+def prepare(field, applied, tile_b, mix, gram_new, cross, step, residual, begun, direction, square):
+    coef_t = mix[:, 0:K]
+    mixed = row_gram(cross[...], coef_t)
+    square[...] = gram_new[...] + mixed + mixed.T + row_gram(exact(coef_t, unpack(tile_b[...])), coef_t)
+    now = field[...] - exact(step[...], applied[...])
     residual[...] = now
-    put_pair(now, pair)
-    tiles[0:TILE, :] = pack(row_gram(now, now))
-    tiles[TILE:, :] = pack(row_gram(now, field[...]))
-    put_images(FIRST, pair[...], tiles[...], high, low, mine, other)
-
-
-def solve_coef(tile_b, tiles, coef):
-    coef[...] = solve_t(unpack(tile_b[...]), unpack(tiles[0:TILE, :]))
-
-
-def prepare(field, residual, tile_b, tiles, step, coef, begun, direction, square):
-    coef_t = coef[...]
-    mixed = row_gram(unpack(tiles[TILE:, :]), coef_t)
-    square[...] = unpack(tiles[0:TILE, :]) + mixed + mixed.T + row_gram(exact(coef_t, unpack(tile_b[...])), coef_t)
-    direction[...] = residual[...] + exact(coef_t, field[...])
+    direction[...] = now + exact(coef_t, field[...])
     begun[...] = exact(step[...], field[...])
 
 
-def k6(z0, z1, z2, z3, residual, norm, tiles, begun, direction, square, solution_out, residual_out):
+def k6(z0, z1, z2, z3, norm, gram_new, residual, begun, direction, square, solution_out, residual_out):
     total, tile = get_blocks(merged((z0, z1, z2, z3)))
     factor = norm[0:1, 0:1]
     curvature = unpack(tile) * factor + ridge_shift * square[...]
-    step_t = solve_t(curvature, unpack(tiles[0:TILE, :]))
+    step_t = solve_t(curvature, gram_new[...])
     backward = total * factor + ridge_shift * direction[...]
     solution_out[...] = begun[...] + exact(step_t, direction[...])
     residual_out[...] = residual[...] - exact(step_t, backward)
@@ -303,7 +312,7 @@
     return lax.optimization_barrier((value, *earlier))[0]
 
 
-def sum_feat(first, images, pair, body):
+def sum_feat(first, images, pair, body, beside=None):
     got, sent, waits = {}, {}, ()
     for distance in ORDER:
         mine, other = first if distance == FIRST else images(distance, after(pair, *waits))
@@ -312,8 +321,12 @@
             sent[distance] = mine + other
             got[distance] = exchange(sent[distance], HERE, 2 * distance)
         waits = {ORDER[1]: (sent[FIRST],), ORDER[2]: tuple(sent.values())}.get(distance, ())
+    extra = None
+    if beside is not None:
+        extra = beside(mine)
+        got[1], extra = lax.optimization_barrier((got[1], extra))
     tiles = (sent[FIRST][body:] + got[1][body:]) + (got[3][body:] + got[2][body:])
-    return ((mine[0:body] + got[1][0:body]) + (got[3][0:body] + got[2][0:body])) + other[0:body], tiles
+    return ((mine[0:body] + got[1][0:body]) + (got[3][0:body] + got[2][0:body])) + other[0:body], tiles, extra
 
 
 def spread_feat(value, project):
@@ -372,7 +385,7 @@
         (*parts, high, low),
         passes=share,
     )
-    own, tile_b = sum_feat(first, images(tiles), pair, body)
+    own, tile_b, _ = sum_feat(first, images(tiles), pair, body)
     kept = {}
 
     def project(distance, near, far, before):
@@ -385,26 +398,30 @@
         return (out,)
 
     parts = gather_rows(*spread_feat(own, project))
-    residual, step, pair, tiles, *first = call(
+    applied, curve, pair, tiles, *first = call(
         k4,
-        [field_like, small, pair_like, tiles_like(2), *images_like(2)],
-        (*parts, field, norm, tile_b, high, low),
+        [field_like, tiles_like(1), pair_like, tiles_like(2), *images_like(2)],
+        (*parts, field, norm, high, low),
         passes=share,
     )
-    own, tiles = sum_feat(first, images(tiles), pair, body)
-    (coef,) = call(solve_coef, [small], (tile_b, tiles), passes=share)
+
+    def begin(own_images):
+        return call(first_step, [small], (after(curve, own_images), tile_b), passes=share)[0]
+
+    own, tiles, step = sum_feat(first, images(tiles), pair, body, begin)
+    mix, gram_new, cross = call(solve_coef, [shape((K, 2 * K), f32), small, small], (tile_b, tiles, step), passes=share)
 
     def mixed_project(distance, near, far, before):
         return call(
             mixed_back_at(distance, not before),
             [summed],
-            (near, far, scale, high, low, coef, kept[distance], *before),
+            (near, far, scale, high, low, mix, kept[distance], *before),
             passes=share,
         )
 
     parts = gather_rows(*spread_feat(own, mixed_project))
-    ready = call(prepare, [field_like, field_like, small], (field, residual, tile_b, tiles, step, coef))
-    return tuple(call(k6, [field_like, field_like], (*parts, residual, norm, tiles, *ready)))
+    ready = call(prepare, [field_like] * 3 + [small], (field, applied, tile_b, mix, gram_new, cross, step))
+    return tuple(call(k6, [field_like, field_like], (*parts, norm, gram_new, *ready)))
 
 
 def solution(mesh):

time: 114 us -> 112 us (0.982)
  waiting for transfers between devices: 38.6 us -> 36.9 us
    ppermute x46, waiting for transfers between devices: 38.6 us -> 36.9 us  [exchange(): return lax.ppermute(value, ('rows', 'feat'), pairs)]
    pallas_call x20 -> x21, Pallas kernels: 31.8 us -> 32 us  [call(): pl.pallas_call(kernel, out_shape=outs, in_specs=specs or [IN_VMEM] * len(...]
  transfers between devices with their start and end apart: 46 -> 46, of which waited for: 20 -> 20; matrix products, arithmetic and copies ran while one was open for 0% -> 0% of each run, Pallas kernels for 14% -> 15%
where the time goes in v5:
time: 112 us
  starting transfers between devices  41.5 us (37%)
  waiting for transfers between devices  36.9 us (33%)
  Pallas kernels  32 us (29%)
  between operations  1.53 us (1%)
    ppermute x46, starting transfers between devices, exchange(): return lax.ppermute(value, ('rows', 'feat'), pairs)  41.5 us
    ppermute x46, waiting for transfers between devices, exchange(): return lax.ppermute(value, ('rows', 'feat'), pairs)  36.9 us
    pallas_call x21, Pallas kernels, call(): pl.pallas_call(kernel, out_shape=outs, in_specs=specs or [IN_VMEM] * len(...  32 us
  transfers between devices with their start and end apart: 46, of which 20 were waited for; matrix products, arithmetic and copies ran while one was open for 0% of the time, Pallas kernels for 15%

profile of v5, /device:TPU:0, one launch (start us, length us, event | category | flops | bytes accessed | tf_op | source)
XLA Modules:
  0.0 112.2 jit_solution(10233979227028882176)
XLA Ops:
  1.3 7.5 %k1.1 = (bf16[4096,1024]{1,0:T(8,128)(2,1)S(1)}, bf16[4096,1024]{1,0:T(8,128)(2,1)S(1)}, f32[1,4096]{1,0:T(1,128)S(1)}, f32[264,128]{1,0:T(8,128)S(1)}) custom-call(s32[1]{0:T(128)S(6)} %copy.6.count, s32[1,4096]{1,0:T(1,128)} %bitcast.1, f32[32,4096]{1,0:T(8,128)} %targets_hbm.1, f32[4096,1024]{1,0:T(8,128)} %features.1), custom_call_target="tpu_custom_call" | custom-call | flops 805306368 | bytes 16777216 | tf_op jit(solution)/shard_map/k1/pallas_call | solution.py:281
  8.8 4.0 %collective-permute-start.2 = (f32[264,128]{1,0:T(8,128)S(1)}, f32[264,128]{1,0:T(8,128)S(1)}, u32[]{:S(2)}, u32[]{:S(2)}) collective-permute-start(f32[264,128]{1,0:T(8,128)S(1)} %get-tuple-element.58), channel_id=1, source_target_pairs={{0,16},{1,65},{2,18},{3,67},{4,20},{5,69},{6,22},{7,71},{8,24},{9,... | collective-permute-start | bytes 405512 | tf_op jit(solution)/shard_map/ppermute | solution.py:301
  13.9 2.0 %collective-permute-done.2 = f32[264,128]{1,0:T(8,128)S(1)} collective-permute-done((f32[264,128]{1,0:T(8,128)S(1)}, f32[264,128]{1,0:T(8,128)S(1)}, u32[]{:S(2)}, u32[]{:S(2)}) %collective-permute-start.2) | collective-permute-done | bytes 135200 | tf_op jit(solution)/shard_map/ppermute | solution.py:301
  15.8 3.2 %collective-permute-done.1 = f32[264,128]{1,0:T(8,128)S(1)} collective-permute-done((f32[264,128]{1,0:T(8,128)S(1)}, f32[264,128]{1,0:T(8,128)S(1)}, u32[]{:S(2)}, u32[]{:S(2)}) %collective-permute-start.1) | collective-permute-done | bytes 135200 | tf_op jit(solution)/shard_map/ppermute | solution.py:301
  19.1 3.3 %collective-permute-start.5 = (f32[264,128]{1,0:T(8,128)S(1)}, f32[264,128]{1,0:T(8,128)S(1)}, u32[]{:S(2)}, u32[]{:S(2)}) collective-permute-start(f32[264,128]{1,0:T(8,128)S(1)} %add_add_fusion.2.p0), channel_id=1, source_target_pairs={{0,64},{1,17},{2,66},{3,19},{4,68},{5,21},{6,70},{7,23},{8,72},{9,... | collective-permute-start | bytes 405512 | tf_op jit(solution)/shard_map/ppermute | solution.py:301
  23.4 2.3 %collective-permute-done.5.p3 = f32[264,128]{1,0:T(8,128)S(1)} collective-permute-done((f32[264,128]{1,0:T(8,128)S(1)}, f32[264,128]{1,0:T(8,128)S(1)}, u32[]{:S(2)}, u32[]{:S(2)}) %collective-permute-start.5) | collective-permute-done | bytes 135200 | tf_op jit(solution)/shard_map/ppermute | solution.py:301
  25.7 2.9 %collective-permute-done.4.p2 = f32[264,128]{1,0:T(8,128)S(1)} collective-permute-done((f32[264,128]{1,0:T(8,128)S(1)}, f32[264,128]{1,0:T(8,128)S(1)}, u32[]{:S(2)}, u32[]{:S(2)}) %collective-permute-start.4) | collective-permute-done | bytes 135200 | tf_op jit(solution)/shard_map/ppermute | solution.py:301
  28.6 1.6 %k2.1 = (f32[32,1024]{1,0:T(8,128)S(1)}, f32[8,128]{1,0:T(8,128)S(1)}, bf16[64,1024]{1,0:T(8,128)(2,1)S(1)}, f32[8,128]{1,0:T(8,128)S(1)}, f32[136,128]{1,0:T(8,128)S(1)}, /*index=5*/f32[136,128]{1,0:T(8,128)S(1)}) custom-call(f32[264,128]{1,0:T(8,128)S(1)} %add_add_fusion.2.p0, f32[264,128]{1,0:T(8,128)S(1)} %collective-permute-done.3.p1, ...), custom_call_target="tpu_custom_call" | custom-call | flops 201326592 | bytes 4194304 | tf_op jit(solution)/shard_map/k2/pallas_call | solution.py:281
  33.6 3.1 %collective-permute-start.11 = (f32[136,128]{1,0:T(8,128)S(1)}, f32[136,128]{1,0:T(8,128)S(1)}, u32[]{:S(2)}, u32[]{:S(2)}) collective-permute-start(f32[136,128]{1,0:T(8,128)S(1)} %add.90), channel_id=1, source_target_pairs={{0,4},{1,5},{2,6},{3,7},{4,0},{5,1},{6,2},{7,3},{8,12},{9,13},{10,... | collective-permute-start | bytes 208904 | tf_op jit(solution)/shard_map/ppermute | solution.py:301
  39.7 2.6 %collective-permute-done.10 = f32[136,128]{1,0:T(8,128)S(1)} collective-permute-done((f32[136,128]{1,0:T(8,128)S(1)}, f32[136,128]{1,0:T(8,128)S(1)}, u32[]{:S(2)}, u32[]{:S(2)}) %collective-permute-start.10) | collective-permute-done | bytes 69664 | tf_op jit(solution)/shard_map/ppermute | solution.py:301
  42.5 2.0 %collective-permute-start.18 = (f32[128,128]{1,0:T(8,128)S(1)}, f32[128,128]{1,0:T(8,128)S(1)}, u32[]{:S(2)}, u32[]{:S(2)}) collective-permute-start(f32[128,128]{1,0:T(8,128)S(1)} %slice_add_fusion.2.near), channel_id=1, source_target_pairs={{0,4},{1,5},{2,6},{3,7},{4,0},{5,1},{6,2},{7,3},{8,12},{9,13},{10,... | collective-permute-start | bytes 196616 | tf_op jit(solution)/shard_map/ppermute | solution.py:301
  46.9 1.6 %collective-permute-done.18.near = f32[128,128]{1,0:T(8,128)S(1)} collective-permute-done((f32[128,128]{1,0:T(8,128)S(1)}, f32[128,128]{1,0:T(8,128)S(1)}, u32[]{:S(2)}, u32[]{:S(2)}) %collective-permute-start.18) | collective-permute-done | bytes 65568 | tf_op jit(solution)/shard_map/ppermute | solution.py:301
  48.5 1.5 %collective-permute-done.16.near = f32[128,128]{1,0:T(8,128)S(1)} collective-permute-done((f32[128,128]{1,0:T(8,128)S(1)}, f32[128,128]{1,0:T(8,128)S(1)}, u32[]{:S(2)}, u32[]{:S(2)}) %collective-permute-start.16) | collective-permute-done | bytes 65568 | tf_op jit(solution)/shard_map/ppermute | solution.py:301
  53.1 1.9 %collective-permute-start.22 = (f32[264,128]{1,0:T(8,128)S(1)}, f32[264,128]{1,0:T(8,128)S(1)}, u32[]{:S(2)}, u32[]{:S(2)}) collective-permute-start(f32[264,128]{1,0:T(8,128)S(1)} %get-tuple-element.80), channel_id=1, source_target_pairs={{0,16},{1,65},{2,18},{3,67},{4,20},{5,69},{6,22},{7,71},{8,24},{9,... | collective-permute-start | bytes 405512 | tf_op jit(solution)/shard_map/ppermute | solution.py:301
  56.7 3.0 %collective-permute-done.22 = f32[264,128]{1,0:T(8,128)S(1)} collective-permute-done((f32[264,128]{1,0:T(8,128)S(1)}, f32[264,128]{1,0:T(8,128)S(1)}, u32[]{:S(2)}, u32[]{:S(2)}) %collective-permute-start.22) | collective-permute-done | bytes 135200 | tf_op jit(solution)/shard_map/ppermute | solution.py:301
  59.7 1.6 %collective-permute-done.21 = f32[264,128]{1,0:T(8,128)S(1)} collective-permute-done((f32[264,128]{1,0:T(8,128)S(1)}, f32[264,128]{1,0:T(8,128)S(1)}, u32[]{:S(2)}, u32[]{:S(2)}) %collective-permute-start.21) | collective-permute-done | bytes 135200 | tf_op jit(solution)/shard_map/ppermute | solution.py:301
  61.3 1.6 %collective-permute-start.25 = (f32[264,128]{1,0:T(8,128)S(1)}, f32[264,128]{1,0:T(8,128)S(1)}, u32[]{:S(2)}, u32[]{:S(2)}) collective-permute-start(f32[264,128]{1,0:T(8,128)S(1)} %add_add_fusion.1.z0), channel_id=1, source_target_pairs={{0,64},{1,17},{2,66},{3,19},{4,68},{5,21},{6,70},{7,23},{8,72},{9,... | collective-permute-start | bytes 405512 | tf_op jit(solution)/shard_map/ppermute | solution.py:301
  62.9 1.4 %collective-permute-start.24 = (f32[264,128]{1,0:T(8,128)S(1)}, f32[264,128]{1,0:T(8,128)S(1)}, u32[]{:S(2)}, u32[]{:S(2)}) collective-permute-start(f32[264,128]{1,0:T(8,128)S(1)} %add_add_fusion.1.z0), channel_id=1, source_target_pairs={{0,96},{1,25},{2,98},{3,27},{4,100},{5,29},{6,102},{7,31},{8,104},... | collective-permute-start | bytes 405512 | tf_op jit(solution)/shard_map/ppermute | solution.py:301
  64.9 3.0 %collective-permute-done.25.z3 = f32[264,128]{1,0:T(8,128)S(1)} collective-permute-done((f32[264,128]{1,0:T(8,128)S(1)}, f32[264,128]{1,0:T(8,128)S(1)}, u32[]{:S(2)}, u32[]{:S(2)}) %collective-permute-start.25) | collective-permute-done | bytes 135200 | tf_op jit(solution)/shard_map/ppermute | solution.py:301
  67.9 1.4 %collective-permute-done.24.z2 = f32[264,128]{1,0:T(8,128)S(1)} collective-permute-done((f32[264,128]{1,0:T(8,128)S(1)}, f32[264,128]{1,0:T(8,128)S(1)}, u32[]{:S(2)}, u32[]{:S(2)}) %collective-permute-start.24) | collective-permute-done | bytes 135200 | tf_op jit(solution)/shard_map/ppermute | solution.py:301
  69.4 1.6 %k4.1 = (f32[32,1024]{1,0:T(8,128)S(1)}, f32[8,128]{1,0:T(8,128)S(1)}, bf16[64,1024]{1,0:T(8,128)(2,1)S(1)}, f32[16,128]{1,0:T(8,128)S(1)}, f32[144,128]{1,0:T(8,128)S(1)}, /*index=5*/f32[144,128]{1,0:T(8,128)S(1)}) custom-call(f32[264,128]{1,0:T(8,128)S(1)} %add_add_fusion.1.z0, f32[264,128]{1,0:T(8,128)S(1)} %collective-permute-done.23.z1, ...), custom_call_target="tpu_custom_call" | custom-call | flops 201326592 | bytes 4194304 | tf_op jit(solution)/shard_map/k4/pallas_call | solution.py:281
  74.3 1.7 %collective-permute-start.31 = (f32[144,128]{1,0:T(8,128)S(1)}, f32[144,128]{1,0:T(8,128)S(1)}, u32[]{:S(2)}, u32[]{:S(2)}) collective-permute-start(f32[144,128]{1,0:T(8,128)S(1)} %add.100), channel_id=1, source_target_pairs={{0,4},{1,5},{2,6},{3,7},{4,0},{5,1},{6,2},{7,3},{8,12},{9,13},{10,... | collective-permute-start | bytes 221192 | tf_op jit(solution)/shard_map/ppermute | solution.py:301
  76.0 1.4 %collective-permute-start.30 = (f32[144,128]{1,0:T(8,128)S(1)}, f32[144,128]{1,0:T(8,128)S(1)}, u32[]{:S(2)}, u32[]{:S(2)}) collective-permute-start(f32[144,128]{1,0:T(8,128)S(1)} %add.101), channel_id=1, source_target_pairs={{0,6},{1,7},{2,4},{3,5},{4,2},{5,3},{6,0},{7,1},{8,14},{9,15},{10,... | collective-permute-start | bytes 221192 | tf_op jit(solution)/shard_map/ppermute | solution.py:301
  82.1 1.9 %collective-permute-start.38 = (f32[128,128]{1,0:T(8,128)S(1)}, f32[128,128]{1,0:T(8,128)S(1)}, u32[]{:S(2)}, u32[]{:S(2)}) collective-permute-start(f32[128,128]{1,0:T(8,128)S(1)} %slice_add_fusion.near), channel_id=1, source_target_pairs={{0,4},{1,5},{2,6},{3,7},{4,0},{5,1},{6,2},{7,3},{8,12},{9,13},{10,... | collective-permute-start | bytes 196616 | tf_op jit(solution)/shard_map/ppermute | solution.py:301
  85.7 1.5 %solve_coef.1 = (f32[32,64]{1,0:T(8,128)S(1)}, f32[32,32]{1,0:T(8,128)S(1)}, f32[32,32]{1,0:T(8,128)S(1)}) custom-call(f32[8,128]{1,0:T(8,128)S(1)} %fusion.3.tile_b, f32[16,128]{1,0:T(8,128)S(1)} %fusion.2.tiles, f32[32,32]{1,0:T(8,128)S(1)} %first_step.1.step), custom_call_target="tpu_custom_call" | custom-call | flops 201326592 | bytes 4194304 | tf_op jit(solution)/shard_map/solve_coef/pallas_call | solution.py:281
  93.2 2.2 %collective-permute-start.42 = (f32[264,128]{1,0:T(8,128)S(1)}, f32[264,128]{1,0:T(8,128)S(1)}, u32[]{:S(2)}, u32[]{:S(2)}) collective-permute-start(f32[264,128]{1,0:T(8,128)S(1)} %mixed_back_kernel.7), channel_id=1, source_target_pairs={{0,16},{1,65},{2,18},{3,67},{4,20},{5,69},{6,22},{7,71},{8,24},{9,... | collective-permute-start | bytes 405512 | tf_op jit(solution)/shard_map/ppermute | solution.py:301
  96.7 3.0 %collective-permute-done.42 = f32[264,128]{1,0:T(8,128)S(1)} collective-permute-done((f32[264,128]{1,0:T(8,128)S(1)}, f32[264,128]{1,0:T(8,128)S(1)}, u32[]{:S(2)}, u32[]{:S(2)}) %collective-permute-start.42) | collective-permute-done | bytes 135200 | tf_op jit(solution)/shard_map/ppermute | solution.py:301
  99.8 1.9 %collective-permute-done.41 = f32[264,128]{1,0:T(8,128)S(1)} collective-permute-done((f32[264,128]{1,0:T(8,128)S(1)}, f32[264,128]{1,0:T(8,128)S(1)}, u32[]{:S(2)}, u32[]{:S(2)}) %collective-permute-start.41) | collective-permute-done | bytes 135200 | tf_op jit(solution)/shard_map/ppermute | solution.py:301
  101.7 2.1 %collective-permute-start.45 = (f32[264,128]{1,0:T(8,128)S(1)}, f32[264,128]{1,0:T(8,128)S(1)}, u32[]{:S(2)}, u32[]{:S(2)}) collective-permute-start(f32[264,128]{1,0:T(8,128)S(1)} %add_add_fusion.z0), channel_id=1, source_target_pairs={{0,64},{1,17},{2,66},{3,19},{4,68},{5,21},{6,70},{7,23},{8,72},{9,... | collective-permute-start | bytes 405512 | tf_op jit(solution)/shard_map/ppermute | solution.py:301
  105.9 2.3 %collective-permute-done.45.z3 = f32[264,128]{1,0:T(8,128)S(1)} collective-permute-done((f32[264,128]{1,0:T(8,128)S(1)}, f32[264,128]{1,0:T(8,128)S(1)}, u32[]{:S(2)}, u32[]{:S(2)}) %collective-permute-start.45) | collective-permute-done | bytes 135200 | tf_op jit(solution)/shard_map/ppermute | solution.py:301
  108.3 1.7 %collective-permute-done.44.z2 = f32[264,128]{1,0:T(8,128)S(1)} collective-permute-done((f32[264,128]{1,0:T(8,128)S(1)}, f32[264,128]{1,0:T(8,128)S(1)}, u32[]{:S(2)}, u32[]{:S(2)}) %collective-permute-start.44) | collective-permute-done | bytes 135200 | tf_op jit(solution)/shard_map/ppermute | solution.py:301
  110.0 2.2 %k6.1 = (f32[32,1024]{1,0:T(8,128)}, f32[32,1024]{1,0:T(8,128)}) custom-call(f32[264,128]{1,0:T(8,128)S(1)} %add_add_fusion.z0, f32[264,128]{1,0:T(8,128)S(1)} %collective-permute-done.43.z1, f32[264,128]{1,0:T(8,128)S(1)} %collective-permute-done.44.z2, f32[264,128]{1,0:T(8,128)S(1)} %collective-permute-done.45.z3, f32[8,128]{1,0:T(8,128)S(1)} %get-tuple-element.82.norm, ...), custom_call_target="tpu_custom_call" | custom-call | tf_op jit(solution)/shard_map/k6/pallas_call | solution.py:281
  (94 shorter events, 35.4 us)
Async XLA Ops:
  8.8 7.0 %collective-permute-start.2 = (f32[264,128]{1,0:T(8,128)S(1)}, f32[264,128]{1,0:T(8,128)S(1)}, u32[]{:S(2)}, u32[]{:S(2)}) collective-permute-start(f32[264,128]{1,0:T(8,128)S(1)} %get-tuple-element.58), channel_id=1, source_target_pairs={{0,16},{1,65},{2,18},{3,67},{4,20},{5,69},{6,22},{7,71},{8,24},{9,... | collective-permute-start | bytes 405512 | tf_op jit(solution)/shard_map/ppermute | solution.py:301
  12.9 6.2 %collective-permute-start.1 = (f32[264,128]{1,0:T(8,128)S(1)}, f32[264,128]{1,0:T(8,128)S(1)}, u32[]{:S(2)}, u32[]{:S(2)}) collective-permute-start(f32[264,128]{1,0:T(8,128)S(1)} %get-tuple-element.58), channel_id=1, source_target_pairs={{0,24},{1,97},{2,26},{3,99},{4,28},{5,101},{6,30},{7,103},{8,16},{... | collective-permute-start | bytes 405512 | tf_op jit(solution)/shard_map/ppermute | solution.py:301
  13.6 5.5 %collective-permute-start = (f32[264,128]{1,0:T(8,128)S(1)}, f32[264,128]{1,0:T(8,128)S(1)}, u32[]{:S(2)}, u32[]{:S(2)}) collective-permute-start(f32[264,128]{1,0:T(8,128)S(1)} %get-tuple-element.58), channel_id=1, source_target_pairs={{0,8},{1,33},{2,10},{3,35},{4,12},{5,37},{6,14},{7,39},{8,0},{9,41... | collective-permute-start | bytes 405512 | tf_op jit(solution)/shard_map/ppermute | solution.py:301
  19.1 6.6 %collective-permute-start.5 = (f32[264,128]{1,0:T(8,128)S(1)}, f32[264,128]{1,0:T(8,128)S(1)}, u32[]{:S(2)}, u32[]{:S(2)}) collective-permute-start(f32[264,128]{1,0:T(8,128)S(1)} %add_add_fusion.2.p0), channel_id=1, source_target_pairs={{0,64},{1,17},{2,66},{3,19},{4,68},{5,21},{6,70},{7,23},{8,72},{9,... | collective-permute-start | bytes 405512 | tf_op jit(solution)/shard_map/ppermute | solution.py:301
  22.4 6.2 %collective-permute-start.4 = (f32[264,128]{1,0:T(8,128)S(1)}, f32[264,128]{1,0:T(8,128)S(1)}, u32[]{:S(2)}, u32[]{:S(2)}) collective-permute-start(f32[264,128]{1,0:T(8,128)S(1)} %add_add_fusion.2.p0), channel_id=1, source_target_pairs={{0,96},{1,25},{2,98},{3,27},{4,100},{5,29},{6,102},{7,31},{8,104},... | collective-permute-start | bytes 405512 | tf_op jit(solution)/shard_map/ppermute | solution.py:301
  23.4 5.2 %collective-permute-start.3 = (f32[264,128]{1,0:T(8,128)S(1)}, f32[264,128]{1,0:T(8,128)S(1)}, u32[]{:S(2)}, u32[]{:S(2)}) collective-permute-start(f32[264,128]{1,0:T(8,128)S(1)} %add_add_fusion.2.p0), channel_id=1, source_target_pairs={{0,32},{1,9},{2,34},{3,11},{4,36},{5,13},{6,38},{7,15},{8,40},{9,1... | collective-permute-start | bytes 405512 | tf_op jit(solution)/shard_map/ppermute | solution.py:301
  31.6 5.1 %collective-permute-start.7 = (f32[136,128]{1,0:T(8,128)S(1)}, f32[136,128]{1,0:T(8,128)S(1)}, u32[]{:S(2)}, u32[]{:S(2)}) collective-permute-start(f32[136,128]{1,0:T(8,128)S(1)} %get-tuple-element.66), channel_id=1, source_target_pairs={{0,1},{1,0},{2,3},{3,2},{4,5},{5,4},{6,7},{7,6},{8,9},{9,8},{10,11... | collective-permute-start | bytes 208904 | tf_op jit(solution)/shard_map/ppermute | solution.py:301
  33.5 4.4 %collective-permute-start.8 = (f32[136,128]{1,0:T(8,128)S(1)}, f32[136,128]{1,0:T(8,128)S(1)}, u32[]{:S(2)}, u32[]{:S(2)}) collective-permute-start(f32[136,128]{1,0:T(8,128)S(1)} %get-tuple-element.69), channel_id=1, source_target_pairs={{0,1},{1,0},{2,3},{3,2},{4,5},{5,4},{6,7},{7,6},{8,9},{9,8},{10,11... | collective-permute-start | bytes 208904 | tf_op jit(solution)/shard_map/ppermute | solution.py:301
  33.6 6.1 %collective-permute-start.11 = (f32[136,128]{1,0:T(8,128)S(1)}, f32[136,128]{1,0:T(8,128)S(1)}, u32[]{:S(2)}, u32[]{:S(2)}) collective-permute-start(f32[136,128]{1,0:T(8,128)S(1)} %add.90), channel_id=1, source_target_pairs={{0,4},{1,5},{2,6},{3,7},{4,0},{5,1},{6,2},{7,3},{8,12},{9,13},{10,... | collective-permute-start | bytes 208904 | tf_op jit(solution)/shard_map/ppermute | solution.py:301
  36.7 5.6 %collective-permute-start.10 = (f32[136,128]{1,0:T(8,128)S(1)}, f32[136,128]{1,0:T(8,128)S(1)}, u32[]{:S(2)}, u32[]{:S(2)}) collective-permute-start(f32[136,128]{1,0:T(8,128)S(1)} %add.91), channel_id=1, source_target_pairs={{0,6},{1,7},{2,4},{3,5},{4,2},{5,3},{6,0},{7,1},{8,14},{9,15},{10,... | collective-permute-start | bytes 208904 | tf_op jit(solution)/shard_map/ppermute | solution.py:301
  37.9 4.4 %collective-permute-start.9 = (f32[136,128]{1,0:T(8,128)S(1)}, f32[136,128]{1,0:T(8,128)S(1)}, u32[]{:S(2)}, u32[]{:S(2)}) collective-permute-start(f32[136,128]{1,0:T(8,128)S(1)} %add.92), channel_id=1, source_target_pairs={{0,2},{1,3},{2,0},{3,1},{4,6},{5,7},{6,4},{7,5},{8,10},{9,11},{10,... | collective-permute-start | bytes 208904 | tf_op jit(solution)/shard_map/ppermute | solution.py:301
  42.5 6.0 %collective-permute-start.18 = (f32[128,128]{1,0:T(8,128)S(1)}, f32[128,128]{1,0:T(8,128)S(1)}, u32[]{:S(2)}, u32[]{:S(2)}) collective-permute-start(f32[128,128]{1,0:T(8,128)S(1)} %slice_add_fusion.2.near), channel_id=1, source_target_pairs={{0,4},{1,5},{2,6},{3,7},{4,0},{5,1},{6,2},{7,3},{8,12},{9,13},{10,... | collective-permute-start | bytes 196616 | tf_op jit(solution)/shard_map/ppermute | solution.py:301
  44.5 5.5 %collective-permute-start.16 = (f32[128,128]{1,0:T(8,128)S(1)}, f32[128,128]{1,0:T(8,128)S(1)}, u32[]{:S(2)}, u32[]{:S(2)}) collective-permute-start(f32[128,128]{1,0:T(8,128)S(1)} %slice_add_fusion.2.near), channel_id=1, source_target_pairs={{0,6},{1,7},{2,4},{3,5},{4,2},{5,3},{6,0},{7,1},{8,14},{9,15},{10,... | collective-permute-start | bytes 196616 | tf_op jit(solution)/shard_map/ppermute | solution.py:301
  45.6 4.3 %collective-permute-start.13 = (f32[128,128]{1,0:T(8,128)S(1)}, f32[128,128]{1,0:T(8,128)S(1)}, u32[]{:S(2)}, u32[]{:S(2)}) collective-permute-start(f32[128,128]{1,0:T(8,128)S(1)} %slice_add_fusion.2.near), channel_id=1, source_target_pairs={{0,2},{1,3},{2,0},{3,1},{4,6},{5,7},{6,4},{7,5},{8,10},{9,11},{10,... | collective-permute-start | bytes 196616 | tf_op jit(solution)/shard_map/ppermute | solution.py:301
  53.1 6.6 %collective-permute-start.22 = (f32[264,128]{1,0:T(8,128)S(1)}, f32[264,128]{1,0:T(8,128)S(1)}, u32[]{:S(2)}, u32[]{:S(2)}) collective-permute-start(f32[264,128]{1,0:T(8,128)S(1)} %get-tuple-element.80), channel_id=1, source_target_pairs={{0,16},{1,65},{2,18},{3,67},{4,20},{5,69},{6,22},{7,71},{8,24},{9,... | collective-permute-start | bytes 405512 | tf_op jit(solution)/shard_map/ppermute | solution.py:301
  55.0 6.2 %collective-permute-start.21 = (f32[264,128]{1,0:T(8,128)S(1)}, f32[264,128]{1,0:T(8,128)S(1)}, u32[]{:S(2)}, u32[]{:S(2)}) collective-permute-start(f32[264,128]{1,0:T(8,128)S(1)} %get-tuple-element.80), channel_id=1, source_target_pairs={{0,24},{1,97},{2,26},{3,99},{4,28},{5,101},{6,30},{7,103},{8,16},{... | collective-permute-start | bytes 405512 | tf_op jit(solution)/shard_map/ppermute | solution.py:301
  56.1 5.1 %collective-permute-start.20 = (f32[264,128]{1,0:T(8,128)S(1)}, f32[264,128]{1,0:T(8,128)S(1)}, u32[]{:S(2)}, u32[]{:S(2)}) collective-permute-start(f32[264,128]{1,0:T(8,128)S(1)} %get-tuple-element.80), channel_id=1, source_target_pairs={{0,8},{1,33},{2,10},{3,35},{4,12},{5,37},{6,14},{7,39},{8,0},{9,41... | collective-permute-start | bytes 405512 | tf_op jit(solution)/shard_map/ppermute | solution.py:301
  61.3 6.6 %collective-permute-start.25 = (f32[264,128]{1,0:T(8,128)S(1)}, f32[264,128]{1,0:T(8,128)S(1)}, u32[]{:S(2)}, u32[]{:S(2)}) collective-permute-start(f32[264,128]{1,0:T(8,128)S(1)} %add_add_fusion.1.z0), channel_id=1, source_target_pairs={{0,64},{1,17},{2,66},{3,19},{4,68},{5,21},{6,70},{7,23},{8,72},{9,... | collective-permute-start | bytes 405512 | tf_op jit(solution)/shard_map/ppermute | solution.py:301
  62.9 6.4 %collective-permute-start.24 = (f32[264,128]{1,0:T(8,128)S(1)}, f32[264,128]{1,0:T(8,128)S(1)}, u32[]{:S(2)}, u32[]{:S(2)}) collective-permute-start(f32[264,128]{1,0:T(8,128)S(1)} %add_add_fusion.1.z0), channel_id=1, source_target_pairs={{0,96},{1,25},{2,98},{3,27},{4,100},{5,29},{6,102},{7,31},{8,104},... | collective-permute-start | bytes 405512 | tf_op jit(solution)/shard_map/ppermute | solution.py:301
  64.3 5.0 %collective-permute-start.23 = (f32[264,128]{1,0:T(8,128)S(1)}, f32[264,128]{1,0:T(8,128)S(1)}, u32[]{:S(2)}, u32[]{:S(2)}) collective-permute-start(f32[264,128]{1,0:T(8,128)S(1)} %add_add_fusion.1.z0), channel_id=1, source_target_pairs={{0,32},{1,9},{2,34},{3,11},{4,36},{5,13},{6,38},{7,15},{8,40},{9,1... | collective-permute-start | bytes 405512 | tf_op jit(solution)/shard_map/ppermute | solution.py:301
  74.3 7.6 %collective-permute-start.31 = (f32[144,128]{1,0:T(8,128)S(1)}, f32[144,128]{1,0:T(8,128)S(1)}, u32[]{:S(2)}, u32[]{:S(2)}) collective-permute-start(f32[144,128]{1,0:T(8,128)S(1)} %add.100), channel_id=1, source_target_pairs={{0,4},{1,5},{2,6},{3,7},{4,0},{5,1},{6,2},{7,3},{8,12},{9,13},{10,... | collective-permute-start | bytes 221192 | tf_op jit(solution)/shard_map/ppermute | solution.py:301
  76.0 6.0 %collective-permute-start.30 = (f32[144,128]{1,0:T(8,128)S(1)}, f32[144,128]{1,0:T(8,128)S(1)}, u32[]{:S(2)}, u32[]{:S(2)}) collective-permute-start(f32[144,128]{1,0:T(8,128)S(1)} %add.101), channel_id=1, source_target_pairs={{0,6},{1,7},{2,4},{3,5},{4,2},{5,3},{6,0},{7,1},{8,14},{9,15},{10,... | collective-permute-start | bytes 221192 | tf_op jit(solution)/shard_map/ppermute | solution.py:301
  77.5 4.4 %collective-permute-start.29 = (f32[144,128]{1,0:T(8,128)S(1)}, f32[144,128]{1,0:T(8,128)S(1)}, u32[]{:S(2)}, u32[]{:S(2)}) collective-permute-start(f32[144,128]{1,0:T(8,128)S(1)} %add.102), channel_id=1, source_target_pairs={{0,2},{1,3},{2,0},{3,1},{4,6},{5,7},{6,4},{7,5},{8,10},{9,11},{10,... | collective-permute-start | bytes 221192 | tf_op jit(solution)/shard_map/ppermute | solution.py:301
  82.1 6.2 %collective-permute-start.38 = (f32[128,128]{1,0:T(8,128)S(1)}, f32[128,128]{1,0:T(8,128)S(1)}, u32[]{:S(2)}, u32[]{:S(2)}) collective-permute-start(f32[128,128]{1,0:T(8,128)S(1)} %slice_add_fusion.near), channel_id=1, source_target_pairs={{0,4},{1,5},{2,6},{3,7},{4,0},{5,1},{6,2},{7,3},{8,12},{9,13},{10,... | collective-permute-start | bytes 196616 | tf_op jit(solution)/shard_map/ppermute | solution.py:301
  84.0 5.5 %collective-permute-start.36 = (f32[128,128]{1,0:T(8,128)S(1)}, f32[128,128]{1,0:T(8,128)S(1)}, u32[]{:S(2)}, u32[]{:S(2)}) collective-permute-start(f32[128,128]{1,0:T(8,128)S(1)} %slice_add_fusion.near), channel_id=1, source_target_pairs={{0,6},{1,7},{2,4},{3,5},{4,2},{5,3},{6,0},{7,1},{8,14},{9,15},{10,... | collective-permute-start | bytes 196616 | tf_op jit(solution)/shard_map/ppermute | solution.py:301
  85.2 4.5 %collective-permute-start.33 = (f32[128,128]{1,0:T(8,128)S(1)}, f32[128,128]{1,0:T(8,128)S(1)}, u32[]{:S(2)}, u32[]{:S(2)}) collective-permute-start(f32[128,128]{1,0:T(8,128)S(1)} %slice_add_fusion.near), channel_id=1, source_target_pairs={{0,2},{1,3},{2,0},{3,1},{4,6},{5,7},{6,4},{7,5},{8,10},{9,11},{10,... | collective-permute-start | bytes 196616 | tf_op jit(solution)/shard_map/ppermute | solution.py:301
  93.2 6.6 %collective-permute-start.42 = (f32[264,128]{1,0:T(8,128)S(1)}, f32[264,128]{1,0:T(8,128)S(1)}, u32[]{:S(2)}, u32[]{:S(2)}) collective-permute-start(f32[264,128]{1,0:T(8,128)S(1)} %mixed_back_kernel.7), channel_id=1, source_target_pairs={{0,16},{1,65},{2,18},{3,67},{4,20},{5,69},{6,22},{7,71},{8,24},{9,... | collective-permute-start | bytes 405512 | tf_op jit(solution)/shard_map/ppermute | solution.py:301
  95.4 6.2 %collective-permute-start.41 = (f32[264,128]{1,0:T(8,128)S(1)}, f32[264,128]{1,0:T(8,128)S(1)}, u32[]{:S(2)}, u32[]{:S(2)}) collective-permute-start(f32[264,128]{1,0:T(8,128)S(1)} %mixed_back_kernel.7), channel_id=1, source_target_pairs={{0,24},{1,97},{2,26},{3,99},{4,28},{5,101},{6,30},{7,103},{8,16},{... | collective-permute-start | bytes 405512 | tf_op jit(solution)/shard_map/ppermute | solution.py:301
  96.3 5.3 %collective-permute-start.40 = (f32[264,128]{1,0:T(8,128)S(1)}, f32[264,128]{1,0:T(8,128)S(1)}, u32[]{:S(2)}, u32[]{:S(2)}) collective-permute-start(f32[264,128]{1,0:T(8,128)S(1)} %mixed_back_kernel.7), channel_id=1, source_target_pairs={{0,8},{1,33},{2,10},{3,35},{4,12},{5,37},{6,14},{7,39},{8,0},{9,41... | collective-permute-start | bytes 405512 | tf_op jit(solution)/shard_map/ppermute | solution.py:301
  101.7 6.6 %collective-permute-start.45 = (f32[264,128]{1,0:T(8,128)S(1)}, f32[264,128]{1,0:T(8,128)S(1)}, u32[]{:S(2)}, u32[]{:S(2)}) collective-permute-start(f32[264,128]{1,0:T(8,128)S(1)} %add_add_fusion.z0), channel_id=1, source_target_pairs={{0,64},{1,17},{2,66},{3,19},{4,68},{5,21},{6,70},{7,23},{8,72},{9,... | collective-permute-start | bytes 405512 | tf_op jit(solution)/shard_map/ppermute | solution.py:301
  103.8 6.2 %collective-permute-start.44 = (f32[264,128]{1,0:T(8,128)S(1)}, f32[264,128]{1,0:T(8,128)S(1)}, u32[]{:S(2)}, u32[]{:S(2)}) collective-permute-start(f32[264,128]{1,0:T(8,128)S(1)} %add_add_fusion.z0), channel_id=1, source_target_pairs={{0,96},{1,25},{2,98},{3,27},{4,100},{5,29},{6,102},{7,31},{8,104},... | collective-permute-start | bytes 405512 | tf_op jit(solution)/shard_map/ppermute | solution.py:301
  105.0 5.0 %collective-permute-start.43 = (f32[264,128]{1,0:T(8,128)S(1)}, f32[264,128]{1,0:T(8,128)S(1)}, u32[]{:S(2)}, u32[]{:S(2)}) collective-permute-start(f32[264,128]{1,0:T(8,128)S(1)} %add_add_fusion.z0), channel_id=1, source_target_pairs={{0,32},{1,9},{2,34},{3,11},{4,36},{5,13},{6,38},{7,15},{8,40},{9,1... | collective-permute-start | bytes 405512 | tf_op jit(solution)/shard_map/ppermute | solution.py:301
  (14 other events, 33.4 us)

commit v6 on v5

--- a/solution.py
+++ b/solution.py
@@ -14,7 +14,7 @@
 ORDER = (2, 3, 1, 0)
 FIRST = ORDER[0]
 HERE = (0, 0)
-CHUNK = 512
+CHUNK = 1024
 STREAM = 256
 BUFFERS = 8
 prio_power = 0.7

time: 112 us -> 112 us (level)
  no operation moved by 1% of the time
where the time goes in v6:
time: 112 us
  starting transfers between devices  41.5 us (37%)
  waiting for transfers between devices  37.1 us (33%)
  Pallas kernels  31.6 us (28%)
  between operations  1.5 us (1%)
    ppermute x46, starting transfers between devices, exchange(): return lax.ppermute(value, ('rows', 'feat'), pairs)  41.5 us
    ppermute x46, waiting for transfers between devices, exchange(): return lax.ppermute(value, ('rows', 'feat'), pairs)  37.1 us
    pallas_call x21, Pallas kernels, call(): pl.pallas_call(kernel, out_shape=outs, in_specs=specs or [IN_VMEM] * len(...  31.6 us
  transfers between devices with their start and end apart: 46, of which 20 were waited for; matrix products, arithmetic and copies ran while one was open for 0% of the time, Pallas kernels for 15%

profile of v6, /device:TPU:0, one launch (start us, length us, event | category | flops | bytes accessed | tf_op | source)
XLA Modules:
  0.0 111.9 jit_solution(7322673277262797123)
XLA Ops:
  1.3 7.5 %k1.1 = (bf16[4096,1024]{1,0:T(8,128)(2,1)S(1)}, bf16[4096,1024]{1,0:T(8,128)(2,1)S(1)}, f32[1,4096]{1,0:T(1,128)S(1)}, f32[264,128]{1,0:T(8,128)S(1)}) custom-call(s32[1]{0:T(128)S(6)} %copy.6.count, s32[1,4096]{1,0:T(1,128)} %bitcast.1, f32[32,4096]{1,0:T(8,128)} %targets_hbm.1, f32[4096,1024]{1,0:T(8,128)} %features.1), custom_call_target="tpu_custom_call" | custom-call | flops 805306368 | bytes 16777216 | tf_op jit(solution)/shard_map/k1/pallas_call | solution.py:281
  8.8 4.0 %collective-permute-start.2 = (f32[264,128]{1,0:T(8,128)S(1)}, f32[264,128]{1,0:T(8,128)S(1)}, u32[]{:S(2)}, u32[]{:S(2)}) collective-permute-start(f32[264,128]{1,0:T(8,128)S(1)} %get-tuple-element.58), channel_id=1, source_target_pairs={{0,16},{1,65},{2,18},{3,67},{4,20},{5,69},{6,22},{7,71},{8,24},{9,... | collective-permute-start | bytes 405512 | tf_op jit(solution)/shard_map/ppermute | solution.py:301
  13.9 2.0 %collective-permute-done.2 = f32[264,128]{1,0:T(8,128)S(1)} collective-permute-done((f32[264,128]{1,0:T(8,128)S(1)}, f32[264,128]{1,0:T(8,128)S(1)}, u32[]{:S(2)}, u32[]{:S(2)}) %collective-permute-start.2) | collective-permute-done | bytes 135200 | tf_op jit(solution)/shard_map/ppermute | solution.py:301
  15.8 3.2 %collective-permute-done.1 = f32[264,128]{1,0:T(8,128)S(1)} collective-permute-done((f32[264,128]{1,0:T(8,128)S(1)}, f32[264,128]{1,0:T(8,128)S(1)}, u32[]{:S(2)}, u32[]{:S(2)}) %collective-permute-start.1) | collective-permute-done | bytes 135200 | tf_op jit(solution)/shard_map/ppermute | solution.py:301
  19.1 3.3 %collective-permute-start.5 = (f32[264,128]{1,0:T(8,128)S(1)}, f32[264,128]{1,0:T(8,128)S(1)}, u32[]{:S(2)}, u32[]{:S(2)}) collective-permute-start(f32[264,128]{1,0:T(8,128)S(1)} %add_add_fusion.2.p0), channel_id=1, source_target_pairs={{0,64},{1,17},{2,66},{3,19},{4,68},{5,21},{6,70},{7,23},{8,72},{9,... | collective-permute-start | bytes 405512 | tf_op jit(solution)/shard_map/ppermute | solution.py:301
  23.4 2.3 %collective-permute-done.5.p3 = f32[264,128]{1,0:T(8,128)S(1)} collective-permute-done((f32[264,128]{1,0:T(8,128)S(1)}, f32[264,128]{1,0:T(8,128)S(1)}, u32[]{:S(2)}, u32[]{:S(2)}) %collective-permute-start.5) | collective-permute-done | bytes 135200 | tf_op jit(solution)/shard_map/ppermute | solution.py:301
  25.7 2.9 %collective-permute-done.4.p2 = f32[264,128]{1,0:T(8,128)S(1)} collective-permute-done((f32[264,128]{1,0:T(8,128)S(1)}, f32[264,128]{1,0:T(8,128)S(1)}, u32[]{:S(2)}, u32[]{:S(2)}) %collective-permute-start.4) | collective-permute-done | bytes 135200 | tf_op jit(solution)/shard_map/ppermute | solution.py:301
  28.6 1.6 %k2.1 = (f32[32,1024]{1,0:T(8,128)S(1)}, f32[8,128]{1,0:T(8,128)S(1)}, bf16[64,1024]{1,0:T(8,128)(2,1)S(1)}, f32[8,128]{1,0:T(8,128)S(1)}, f32[136,128]{1,0:T(8,128)S(1)}, /*index=5*/f32[136,128]{1,0:T(8,128)S(1)}) custom-call(f32[264,128]{1,0:T(8,128)S(1)} %add_add_fusion.2.p0, f32[264,128]{1,0:T(8,128)S(1)} %collective-permute-done.3.p1, ...), custom_call_target="tpu_custom_call" | custom-call | flops 201326592 | bytes 4194304 | tf_op jit(solution)/shard_map/k2/pallas_call | solution.py:281
  33.6 3.1 %collective-permute-start.11 = (f32[136,128]{1,0:T(8,128)S(1)}, f32[136,128]{1,0:T(8,128)S(1)}, u32[]{:S(2)}, u32[]{:S(2)}) collective-permute-start(f32[136,128]{1,0:T(8,128)S(1)} %add.90), channel_id=1, source_target_pairs={{0,4},{1,5},{2,6},{3,7},{4,0},{5,1},{6,2},{7,3},{8,12},{9,13},{10,... | collective-permute-start | bytes 208904 | tf_op jit(solution)/shard_map/ppermute | solution.py:301
  39.7 2.6 %collective-permute-done.10 = f32[136,128]{1,0:T(8,128)S(1)} collective-permute-done((f32[136,128]{1,0:T(8,128)S(1)}, f32[136,128]{1,0:T(8,128)S(1)}, u32[]{:S(2)}, u32[]{:S(2)}) %collective-permute-start.10) | collective-permute-done | bytes 69664 | tf_op jit(solution)/shard_map/ppermute | solution.py:301
  42.5 2.0 %collective-permute-start.18 = (f32[128,128]{1,0:T(8,128)S(1)}, f32[128,128]{1,0:T(8,128)S(1)}, u32[]{:S(2)}, u32[]{:S(2)}) collective-permute-start(f32[128,128]{1,0:T(8,128)S(1)} %slice_add_fusion.2.near), channel_id=1, source_target_pairs={{0,4},{1,5},{2,6},{3,7},{4,0},{5,1},{6,2},{7,3},{8,12},{9,13},{10,... | collective-permute-start | bytes 196616 | tf_op jit(solution)/shard_map/ppermute | solution.py:301
  46.9 1.6 %collective-permute-done.18.near = f32[128,128]{1,0:T(8,128)S(1)} collective-permute-done((f32[128,128]{1,0:T(8,128)S(1)}, f32[128,128]{1,0:T(8,128)S(1)}, u32[]{:S(2)}, u32[]{:S(2)}) %collective-permute-start.18) | collective-permute-done | bytes 65568 | tf_op jit(solution)/shard_map/ppermute | solution.py:301
  48.5 1.5 %collective-permute-done.16.near = f32[128,128]{1,0:T(8,128)S(1)} collective-permute-done((f32[128,128]{1,0:T(8,128)S(1)}, f32[128,128]{1,0:T(8,128)S(1)}, u32[]{:S(2)}, u32[]{:S(2)}) %collective-permute-start.16) | collective-permute-done | bytes 65568 | tf_op jit(solution)/shard_map/ppermute | solution.py:301
  53.1 1.9 %collective-permute-start.22 = (f32[264,128]{1,0:T(8,128)S(1)}, f32[264,128]{1,0:T(8,128)S(1)}, u32[]{:S(2)}, u32[]{:S(2)}) collective-permute-start(f32[264,128]{1,0:T(8,128)S(1)} %get-tuple-element.80), channel_id=1, source_target_pairs={{0,16},{1,65},{2,18},{3,67},{4,20},{5,69},{6,22},{7,71},{8,24},{9,... | collective-permute-start | bytes 405512 | tf_op jit(solution)/shard_map/ppermute | solution.py:301
  56.7 3.0 %collective-permute-done.22 = f32[264,128]{1,0:T(8,128)S(1)} collective-permute-done((f32[264,128]{1,0:T(8,128)S(1)}, f32[264,128]{1,0:T(8,128)S(1)}, u32[]{:S(2)}, u32[]{:S(2)}) %collective-permute-start.22) | collective-permute-done | bytes 135200 | tf_op jit(solution)/shard_map/ppermute | solution.py:301
  59.7 1.6 %collective-permute-done.21 = f32[264,128]{1,0:T(8,128)S(1)} collective-permute-done((f32[264,128]{1,0:T(8,128)S(1)}, f32[264,128]{1,0:T(8,128)S(1)}, u32[]{:S(2)}, u32[]{:S(2)}) %collective-permute-start.21) | collective-permute-done | bytes 135200 | tf_op jit(solution)/shard_map/ppermute | solution.py:301
  61.3 1.6 %collective-permute-start.25 = (f32[264,128]{1,0:T(8,128)S(1)}, f32[264,128]{1,0:T(8,128)S(1)}, u32[]{:S(2)}, u32[]{:S(2)}) collective-permute-start(f32[264,128]{1,0:T(8,128)S(1)} %add_add_fusion.1.z0), channel_id=1, source_target_pairs={{0,64},{1,17},{2,66},{3,19},{4,68},{5,21},{6,70},{7,23},{8,72},{9,... | collective-permute-start | bytes 405512 | tf_op jit(solution)/shard_map/ppermute | solution.py:301
  62.9 1.4 %collective-permute-start.24 = (f32[264,128]{1,0:T(8,128)S(1)}, f32[264,128]{1,0:T(8,128)S(1)}, u32[]{:S(2)}, u32[]{:S(2)}) collective-permute-start(f32[264,128]{1,0:T(8,128)S(1)} %add_add_fusion.1.z0), channel_id=1, source_target_pairs={{0,96},{1,25},{2,98},{3,27},{4,100},{5,29},{6,102},{7,31},{8,104},... | collective-permute-start | bytes 405512 | tf_op jit(solution)/shard_map/ppermute | solution.py:301
  64.9 3.0 %collective-permute-done.25.z3 = f32[264,128]{1,0:T(8,128)S(1)} collective-permute-done((f32[264,128]{1,0:T(8,128)S(1)}, f32[264,128]{1,0:T(8,128)S(1)}, u32[]{:S(2)}, u32[]{:S(2)}) %collective-permute-start.25) | collective-permute-done | bytes 135200 | tf_op jit(solution)/shard_map/ppermute | solution.py:301
  68.0 1.4 %collective-permute-done.24.z2 = f32[264,128]{1,0:T(8,128)S(1)} collective-permute-done((f32[264,128]{1,0:T(8,128)S(1)}, f32[264,128]{1,0:T(8,128)S(1)}, u32[]{:S(2)}, u32[]{:S(2)}) %collective-permute-start.24) | collective-permute-done | bytes 135200 | tf_op jit(solution)/shard_map/ppermute | solution.py:301
  69.4 1.6 %k4.1 = (f32[32,1024]{1,0:T(8,128)S(1)}, f32[8,128]{1,0:T(8,128)S(1)}, bf16[64,1024]{1,0:T(8,128)(2,1)S(1)}, f32[16,128]{1,0:T(8,128)S(1)}, f32[144,128]{1,0:T(8,128)S(1)}, /*index=5*/f32[144,128]{1,0:T(8,128)S(1)}) custom-call(f32[264,128]{1,0:T(8,128)S(1)} %add_add_fusion.1.z0, f32[264,128]{1,0:T(8,128)S(1)} %collective-permute-done.23.z1, ...), custom_call_target="tpu_custom_call" | custom-call | flops 201326592 | bytes 4194304 | tf_op jit(solution)/shard_map/k4/pallas_call | solution.py:281
  74.3 1.7 %collective-permute-start.31 = (f32[144,128]{1,0:T(8,128)S(1)}, f32[144,128]{1,0:T(8,128)S(1)}, u32[]{:S(2)}, u32[]{:S(2)}) collective-permute-start(f32[144,128]{1,0:T(8,128)S(1)} %add.100), channel_id=1, source_target_pairs={{0,4},{1,5},{2,6},{3,7},{4,0},{5,1},{6,2},{7,3},{8,12},{9,13},{10,... | collective-permute-start | bytes 221192 | tf_op jit(solution)/shard_map/ppermute | solution.py:301
  76.1 1.4 %collective-permute-start.30 = (f32[144,128]{1,0:T(8,128)S(1)}, f32[144,128]{1,0:T(8,128)S(1)}, u32[]{:S(2)}, u32[]{:S(2)}) collective-permute-start(f32[144,128]{1,0:T(8,128)S(1)} %add.101), channel_id=1, source_target_pairs={{0,6},{1,7},{2,4},{3,5},{4,2},{5,3},{6,0},{7,1},{8,14},{9,15},{10,... | collective-permute-start | bytes 221192 | tf_op jit(solution)/shard_map/ppermute | solution.py:301
  82.1 1.9 %collective-permute-start.38 = (f32[128,128]{1,0:T(8,128)S(1)}, f32[128,128]{1,0:T(8,128)S(1)}, u32[]{:S(2)}, u32[]{:S(2)}) collective-permute-start(f32[128,128]{1,0:T(8,128)S(1)} %slice_add_fusion.near), channel_id=1, source_target_pairs={{0,4},{1,5},{2,6},{3,7},{4,0},{5,1},{6,2},{7,3},{8,12},{9,13},{10,... | collective-permute-start | bytes 196616 | tf_op jit(solution)/shard_map/ppermute | solution.py:301
  85.7 1.5 %solve_coef.1 = (f32[32,64]{1,0:T(8,128)S(1)}, f32[32,32]{1,0:T(8,128)S(1)}, f32[32,32]{1,0:T(8,128)S(1)}) custom-call(f32[8,128]{1,0:T(8,128)S(1)} %fusion.3.tile_b, f32[16,128]{1,0:T(8,128)S(1)} %fusion.2.tiles, f32[32,32]{1,0:T(8,128)S(1)} %first_step.1.step), custom_call_target="tpu_custom_call" | custom-call | flops 201326592 | bytes 4194304 | tf_op jit(solution)/shard_map/solve_coef/pallas_call | solution.py:281
  92.8 2.2 %collective-permute-start.42 = (f32[264,128]{1,0:T(8,128)S(1)}, f32[264,128]{1,0:T(8,128)S(1)}, u32[]{:S(2)}, u32[]{:S(2)}) collective-permute-start(f32[264,128]{1,0:T(8,128)S(1)} %mixed_back_kernel.7), channel_id=1, source_target_pairs={{0,16},{1,65},{2,18},{3,67},{4,20},{5,69},{6,22},{7,71},{8,24},{9,... | collective-permute-start | bytes 405512 | tf_op jit(solution)/shard_map/ppermute | solution.py:301
  96.4 3.0 %collective-permute-done.42 = f32[264,128]{1,0:T(8,128)S(1)} collective-permute-done((f32[264,128]{1,0:T(8,128)S(1)}, f32[264,128]{1,0:T(8,128)S(1)}, u32[]{:S(2)}, u32[]{:S(2)}) %collective-permute-start.42) | collective-permute-done | bytes 135200 | tf_op jit(solution)/shard_map/ppermute | solution.py:301
  99.4 1.9 %collective-permute-done.41 = f32[264,128]{1,0:T(8,128)S(1)} collective-permute-done((f32[264,128]{1,0:T(8,128)S(1)}, f32[264,128]{1,0:T(8,128)S(1)}, u32[]{:S(2)}, u32[]{:S(2)}) %collective-permute-start.41) | collective-permute-done | bytes 135200 | tf_op jit(solution)/shard_map/ppermute | solution.py:301
  101.3 2.1 %collective-permute-start.45 = (f32[264,128]{1,0:T(8,128)S(1)}, f32[264,128]{1,0:T(8,128)S(1)}, u32[]{:S(2)}, u32[]{:S(2)}) collective-permute-start(f32[264,128]{1,0:T(8,128)S(1)} %add_add_fusion.z0), channel_id=1, source_target_pairs={{0,64},{1,17},{2,66},{3,19},{4,68},{5,21},{6,70},{7,23},{8,72},{9,... | collective-permute-start | bytes 405512 | tf_op jit(solution)/shard_map/ppermute | solution.py:301
  105.6 2.3 %collective-permute-done.45.z3 = f32[264,128]{1,0:T(8,128)S(1)} collective-permute-done((f32[264,128]{1,0:T(8,128)S(1)}, f32[264,128]{1,0:T(8,128)S(1)}, u32[]{:S(2)}, u32[]{:S(2)}) %collective-permute-start.45) | collective-permute-done | bytes 135200 | tf_op jit(solution)/shard_map/ppermute | solution.py:301
  107.9 1.7 %collective-permute-done.44.z2 = f32[264,128]{1,0:T(8,128)S(1)} collective-permute-done((f32[264,128]{1,0:T(8,128)S(1)}, f32[264,128]{1,0:T(8,128)S(1)}, u32[]{:S(2)}, u32[]{:S(2)}) %collective-permute-start.44) | collective-permute-done | bytes 135200 | tf_op jit(solution)/shard_map/ppermute | solution.py:301
  109.6 2.2 %k6.1 = (f32[32,1024]{1,0:T(8,128)}, f32[32,1024]{1,0:T(8,128)}) custom-call(f32[264,128]{1,0:T(8,128)S(1)} %add_add_fusion.z0, f32[264,128]{1,0:T(8,128)S(1)} %collective-permute-done.43.z1, f32[264,128]{1,0:T(8,128)S(1)} %collective-permute-done.44.z2, f32[264,128]{1,0:T(8,128)S(1)} %collective-permute-done.45.z3, f32[8,128]{1,0:T(8,128)S(1)} %get-tuple-element.82.norm, ...), custom_call_target="tpu_custom_call" | custom-call | tf_op jit(solution)/shard_map/k6/pallas_call | solution.py:281
  (94 shorter events, 35.1 us)
Async XLA Ops:
  8.8 7.0 %collective-permute-start.2 = (f32[264,128]{1,0:T(8,128)S(1)}, f32[264,128]{1,0:T(8,128)S(1)}, u32[]{:S(2)}, u32[]{:S(2)}) collective-permute-start(f32[264,128]{1,0:T(8,128)S(1)} %get-tuple-element.58), channel_id=1, source_target_pairs={{0,16},{1,65},{2,18},{3,67},{4,20},{5,69},{6,22},{7,71},{8,24},{9,... | collective-permute-start | bytes 405512 | tf_op jit(solution)/shard_map/ppermute | solution.py:301
  12.9 6.2 %collective-permute-start.1 = (f32[264,128]{1,0:T(8,128)S(1)}, f32[264,128]{1,0:T(8,128)S(1)}, u32[]{:S(2)}, u32[]{:S(2)}) collective-permute-start(f32[264,128]{1,0:T(8,128)S(1)} %get-tuple-element.58), channel_id=1, source_target_pairs={{0,24},{1,97},{2,26},{3,99},{4,28},{5,101},{6,30},{7,103},{8,16},{... | collective-permute-start | bytes 405512 | tf_op jit(solution)/shard_map/ppermute | solution.py:301
  13.6 5.5 %collective-permute-start = (f32[264,128]{1,0:T(8,128)S(1)}, f32[264,128]{1,0:T(8,128)S(1)}, u32[]{:S(2)}, u32[]{:S(2)}) collective-permute-start(f32[264,128]{1,0:T(8,128)S(1)} %get-tuple-element.58), channel_id=1, source_target_pairs={{0,8},{1,33},{2,10},{3,35},{4,12},{5,37},{6,14},{7,39},{8,0},{9,41... | collective-permute-start | bytes 405512 | tf_op jit(solution)/shard_map/ppermute | solution.py:301
  19.1 6.6 %collective-permute-start.5 = (f32[264,128]{1,0:T(8,128)S(1)}, f32[264,128]{1,0:T(8,128)S(1)}, u32[]{:S(2)}, u32[]{:S(2)}) collective-permute-start(f32[264,128]{1,0:T(8,128)S(1)} %add_add_fusion.2.p0), channel_id=1, source_target_pairs={{0,64},{1,17},{2,66},{3,19},{4,68},{5,21},{6,70},{7,23},{8,72},{9,... | collective-permute-start | bytes 405512 | tf_op jit(solution)/shard_map/ppermute | solution.py:301
  22.4 6.2 %collective-permute-start.4 = (f32[264,128]{1,0:T(8,128)S(1)}, f32[264,128]{1,0:T(8,128)S(1)}, u32[]{:S(2)}, u32[]{:S(2)}) collective-permute-start(f32[264,128]{1,0:T(8,128)S(1)} %add_add_fusion.2.p0), channel_id=1, source_target_pairs={{0,96},{1,25},{2,98},{3,27},{4,100},{5,29},{6,102},{7,31},{8,104},... | collective-permute-start | bytes 405512 | tf_op jit(solution)/shard_map/ppermute | solution.py:301
  23.4 5.2 %collective-permute-start.3 = (f32[264,128]{1,0:T(8,128)S(1)}, f32[264,128]{1,0:T(8,128)S(1)}, u32[]{:S(2)}, u32[]{:S(2)}) collective-permute-start(f32[264,128]{1,0:T(8,128)S(1)} %add_add_fusion.2.p0), channel_id=1, source_target_pairs={{0,32},{1,9},{2,34},{3,11},{4,36},{5,13},{6,38},{7,15},{8,40},{9,1... | collective-permute-start | bytes 405512 | tf_op jit(solution)/shard_map/ppermute | solution.py:301
  31.6 5.1 %collective-permute-start.7 = (f32[136,128]{1,0:T(8,128)S(1)}, f32[136,128]{1,0:T(8,128)S(1)}, u32[]{:S(2)}, u32[]{:S(2)}) collective-permute-start(f32[136,128]{1,0:T(8,128)S(1)} %get-tuple-element.66), channel_id=1, source_target_pairs={{0,1},{1,0},{2,3},{3,2},{4,5},{5,4},{6,7},{7,6},{8,9},{9,8},{10,11... | collective-permute-start | bytes 208904 | tf_op jit(solution)/shard_map/ppermute | solution.py:301
  33.5 4.4 %collective-permute-start.8 = (f32[136,128]{1,0:T(8,128)S(1)}, f32[136,128]{1,0:T(8,128)S(1)}, u32[]{:S(2)}, u32[]{:S(2)}) collective-permute-start(f32[136,128]{1,0:T(8,128)S(1)} %get-tuple-element.69), channel_id=1, source_target_pairs={{0,1},{1,0},{2,3},{3,2},{4,5},{5,4},{6,7},{7,6},{8,9},{9,8},{10,11... | collective-permute-start | bytes 208904 | tf_op jit(solution)/shard_map/ppermute | solution.py:301
  33.6 6.1 %collective-permute-start.11 = (f32[136,128]{1,0:T(8,128)S(1)}, f32[136,128]{1,0:T(8,128)S(1)}, u32[]{:S(2)}, u32[]{:S(2)}) collective-permute-start(f32[136,128]{1,0:T(8,128)S(1)} %add.90), channel_id=1, source_target_pairs={{0,4},{1,5},{2,6},{3,7},{4,0},{5,1},{6,2},{7,3},{8,12},{9,13},{10,... | collective-permute-start | bytes 208904 | tf_op jit(solution)/shard_map/ppermute | solution.py:301
  36.7 5.6 %collective-permute-start.10 = (f32[136,128]{1,0:T(8,128)S(1)}, f32[136,128]{1,0:T(8,128)S(1)}, u32[]{:S(2)}, u32[]{:S(2)}) collective-permute-start(f32[136,128]{1,0:T(8,128)S(1)} %add.91), channel_id=1, source_target_pairs={{0,6},{1,7},{2,4},{3,5},{4,2},{5,3},{6,0},{7,1},{8,14},{9,15},{10,... | collective-permute-start | bytes 208904 | tf_op jit(solution)/shard_map/ppermute | solution.py:301
  38.0 4.4 %collective-permute-start.9 = (f32[136,128]{1,0:T(8,128)S(1)}, f32[136,128]{1,0:T(8,128)S(1)}, u32[]{:S(2)}, u32[]{:S(2)}) collective-permute-start(f32[136,128]{1,0:T(8,128)S(1)} %add.92), channel_id=1, source_target_pairs={{0,2},{1,3},{2,0},{3,1},{4,6},{5,7},{6,4},{7,5},{8,10},{9,11},{10,... | collective-permute-start | bytes 208904 | tf_op jit(solution)/shard_map/ppermute | solution.py:301
  42.5 6.0 %collective-permute-start.18 = (f32[128,128]{1,0:T(8,128)S(1)}, f32[128,128]{1,0:T(8,128)S(1)}, u32[]{:S(2)}, u32[]{:S(2)}) collective-permute-start(f32[128,128]{1,0:T(8,128)S(1)} %slice_add_fusion.2.near), channel_id=1, source_target_pairs={{0,4},{1,5},{2,6},{3,7},{4,0},{5,1},{6,2},{7,3},{8,12},{9,13},{10,... | collective-permute-start | bytes 196616 | tf_op jit(solution)/shard_map/ppermute | solution.py:301
  44.5 5.5 %collective-permute-start.16 = (f32[128,128]{1,0:T(8,128)S(1)}, f32[128,128]{1,0:T(8,128)S(1)}, u32[]{:S(2)}, u32[]{:S(2)}) collective-permute-start(f32[128,128]{1,0:T(8,128)S(1)} %slice_add_fusion.2.near), channel_id=1, source_target_pairs={{0,6},{1,7},{2,4},{3,5},{4,2},{5,3},{6,0},{7,1},{8,14},{9,15},{10,... | collective-permute-start | bytes 196616 | tf_op jit(solution)/shard_map/ppermute | solution.py:301
  45.6 4.3 %collective-permute-start.13 = (f32[128,128]{1,0:T(8,128)S(1)}, f32[128,128]{1,0:T(8,128)S(1)}, u32[]{:S(2)}, u32[]{:S(2)}) collective-permute-start(f32[128,128]{1,0:T(8,128)S(1)} %slice_add_fusion.2.near), channel_id=1, source_target_pairs={{0,2},{1,3},{2,0},{3,1},{4,6},{5,7},{6,4},{7,5},{8,10},{9,11},{10,... | collective-permute-start | bytes 196616 | tf_op jit(solution)/shard_map/ppermute | solution.py:301
  53.1 6.6 %collective-permute-start.22 = (f32[264,128]{1,0:T(8,128)S(1)}, f32[264,128]{1,0:T(8,128)S(1)}, u32[]{:S(2)}, u32[]{:S(2)}) collective-permute-start(f32[264,128]{1,0:T(8,128)S(1)} %get-tuple-element.80), channel_id=1, source_target_pairs={{0,16},{1,65},{2,18},{3,67},{4,20},{5,69},{6,22},{7,71},{8,24},{9,... | collective-permute-start | bytes 405512 | tf_op jit(solution)/shard_map/ppermute | solution.py:301
  55.1 6.2 %collective-permute-start.21 = (f32[264,128]{1,0:T(8,128)S(1)}, f32[264,128]{1,0:T(8,128)S(1)}, u32[]{:S(2)}, u32[]{:S(2)}) collective-permute-start(f32[264,128]{1,0:T(8,128)S(1)} %get-tuple-element.80), channel_id=1, source_target_pairs={{0,24},{1,97},{2,26},{3,99},{4,28},{5,101},{6,30},{7,103},{8,16},{... | collective-permute-start | bytes 405512 | tf_op jit(solution)/shard_map/ppermute | solution.py:301
  56.2 5.1 %collective-permute-start.20 = (f32[264,128]{1,0:T(8,128)S(1)}, f32[264,128]{1,0:T(8,128)S(1)}, u32[]{:S(2)}, u32[]{:S(2)}) collective-permute-start(f32[264,128]{1,0:T(8,128)S(1)} %get-tuple-element.80), channel_id=1, source_target_pairs={{0,8},{1,33},{2,10},{3,35},{4,12},{5,37},{6,14},{7,39},{8,0},{9,41... | collective-permute-start | bytes 405512 | tf_op jit(solution)/shard_map/ppermute | solution.py:301
  61.3 6.6 %collective-permute-start.25 = (f32[264,128]{1,0:T(8,128)S(1)}, f32[264,128]{1,0:T(8,128)S(1)}, u32[]{:S(2)}, u32[]{:S(2)}) collective-permute-start(f32[264,128]{1,0:T(8,128)S(1)} %add_add_fusion.1.z0), channel_id=1, source_target_pairs={{0,64},{1,17},{2,66},{3,19},{4,68},{5,21},{6,70},{7,23},{8,72},{9,... | collective-permute-start | bytes 405512 | tf_op jit(solution)/shard_map/ppermute | solution.py:301
  62.9 6.4 %collective-permute-start.24 = (f32[264,128]{1,0:T(8,128)S(1)}, f32[264,128]{1,0:T(8,128)S(1)}, u32[]{:S(2)}, u32[]{:S(2)}) collective-permute-start(f32[264,128]{1,0:T(8,128)S(1)} %add_add_fusion.1.z0), channel_id=1, source_target_pairs={{0,96},{1,25},{2,98},{3,27},{4,100},{5,29},{6,102},{7,31},{8,104},... | collective-permute-start | bytes 405512 | tf_op jit(solution)/shard_map/ppermute | solution.py:301
  64.4 5.0 %collective-permute-start.23 = (f32[264,128]{1,0:T(8,128)S(1)}, f32[264,128]{1,0:T(8,128)S(1)}, u32[]{:S(2)}, u32[]{:S(2)}) collective-permute-start(f32[264,128]{1,0:T(8,128)S(1)} %add_add_fusion.1.z0), channel_id=1, source_target_pairs={{0,32},{1,9},{2,34},{3,11},{4,36},{5,13},{6,38},{7,15},{8,40},{9,1... | collective-permute-start | bytes 405512 | tf_op jit(solution)/shard_map/ppermute | solution.py:301
  74.3 7.6 %collective-permute-start.31 = (f32[144,128]{1,0:T(8,128)S(1)}, f32[144,128]{1,0:T(8,128)S(1)}, u32[]{:S(2)}, u32[]{:S(2)}) collective-permute-start(f32[144,128]{1,0:T(8,128)S(1)} %add.100), channel_id=1, source_target_pairs={{0,4},{1,5},{2,6},{3,7},{4,0},{5,1},{6,2},{7,3},{8,12},{9,13},{10,... | collective-permute-start | bytes 221192 | tf_op jit(solution)/shard_map/ppermute | solution.py:301
  76.1 6.0 %collective-permute-start.30 = (f32[144,128]{1,0:T(8,128)S(1)}, f32[144,128]{1,0:T(8,128)S(1)}, u32[]{:S(2)}, u32[]{:S(2)}) collective-permute-start(f32[144,128]{1,0:T(8,128)S(1)} %add.101), channel_id=1, source_target_pairs={{0,6},{1,7},{2,4},{3,5},{4,2},{5,3},{6,0},{7,1},{8,14},{9,15},{10,... | collective-permute-start | bytes 221192 | tf_op jit(solution)/shard_map/ppermute | solution.py:301
  77.5 4.4 %collective-permute-start.29 = (f32[144,128]{1,0:T(8,128)S(1)}, f32[144,128]{1,0:T(8,128)S(1)}, u32[]{:S(2)}, u32[]{:S(2)}) collective-permute-start(f32[144,128]{1,0:T(8,128)S(1)} %add.102), channel_id=1, source_target_pairs={{0,2},{1,3},{2,0},{3,1},{4,6},{5,7},{6,4},{7,5},{8,10},{9,11},{10,... | collective-permute-start | bytes 221192 | tf_op jit(solution)/shard_map/ppermute | solution.py:301
  82.1 6.1 %collective-permute-start.38 = (f32[128,128]{1,0:T(8,128)S(1)}, f32[128,128]{1,0:T(8,128)S(1)}, u32[]{:S(2)}, u32[]{:S(2)}) collective-permute-start(f32[128,128]{1,0:T(8,128)S(1)} %slice_add_fusion.near), channel_id=1, source_target_pairs={{0,4},{1,5},{2,6},{3,7},{4,0},{5,1},{6,2},{7,3},{8,12},{9,13},{10,... | collective-permute-start | bytes 196616 | tf_op jit(solution)/shard_map/ppermute | solution.py:301
  84.0 5.5 %collective-permute-start.36 = (f32[128,128]{1,0:T(8,128)S(1)}, f32[128,128]{1,0:T(8,128)S(1)}, u32[]{:S(2)}, u32[]{:S(2)}) collective-permute-start(f32[128,128]{1,0:T(8,128)S(1)} %slice_add_fusion.near), channel_id=1, source_target_pairs={{0,6},{1,7},{2,4},{3,5},{4,2},{5,3},{6,0},{7,1},{8,14},{9,15},{10,... | collective-permute-start | bytes 196616 | tf_op jit(solution)/shard_map/ppermute | solution.py:301
  85.2 4.5 %collective-permute-start.33 = (f32[128,128]{1,0:T(8,128)S(1)}, f32[128,128]{1,0:T(8,128)S(1)}, u32[]{:S(2)}, u32[]{:S(2)}) collective-permute-start(f32[128,128]{1,0:T(8,128)S(1)} %slice_add_fusion.near), channel_id=1, source_target_pairs={{0,2},{1,3},{2,0},{3,1},{4,6},{5,7},{6,4},{7,5},{8,10},{9,11},{10,... | collective-permute-start | bytes 196616 | tf_op jit(solution)/shard_map/ppermute | solution.py:301
  92.8 6.6 %collective-permute-start.42 = (f32[264,128]{1,0:T(8,128)S(1)}, f32[264,128]{1,0:T(8,128)S(1)}, u32[]{:S(2)}, u32[]{:S(2)}) collective-permute-start(f32[264,128]{1,0:T(8,128)S(1)} %mixed_back_kernel.7), channel_id=1, source_target_pairs={{0,16},{1,65},{2,18},{3,67},{4,20},{5,69},{6,22},{7,71},{8,24},{9,... | collective-permute-start | bytes 405512 | tf_op jit(solution)/shard_map/ppermute | solution.py:301
  95.1 6.2 %collective-permute-start.41 = (f32[264,128]{1,0:T(8,128)S(1)}, f32[264,128]{1,0:T(8,128)S(1)}, u32[]{:S(2)}, u32[]{:S(2)}) collective-permute-start(f32[264,128]{1,0:T(8,128)S(1)} %mixed_back_kernel.7), channel_id=1, source_target_pairs={{0,24},{1,97},{2,26},{3,99},{4,28},{5,101},{6,30},{7,103},{8,16},{... | collective-permute-start | bytes 405512 | tf_op jit(solution)/shard_map/ppermute | solution.py:301
  96.0 5.3 %collective-permute-start.40 = (f32[264,128]{1,0:T(8,128)S(1)}, f32[264,128]{1,0:T(8,128)S(1)}, u32[]{:S(2)}, u32[]{:S(2)}) collective-permute-start(f32[264,128]{1,0:T(8,128)S(1)} %mixed_back_kernel.7), channel_id=1, source_target_pairs={{0,8},{1,33},{2,10},{3,35},{4,12},{5,37},{6,14},{7,39},{8,0},{9,41... | collective-permute-start | bytes 405512 | tf_op jit(solution)/shard_map/ppermute | solution.py:301
  101.3 6.6 %collective-permute-start.45 = (f32[264,128]{1,0:T(8,128)S(1)}, f32[264,128]{1,0:T(8,128)S(1)}, u32[]{:S(2)}, u32[]{:S(2)}) collective-permute-start(f32[264,128]{1,0:T(8,128)S(1)} %add_add_fusion.z0), channel_id=1, source_target_pairs={{0,64},{1,17},{2,66},{3,19},{4,68},{5,21},{6,70},{7,23},{8,72},{9,... | collective-permute-start | bytes 405512 | tf_op jit(solution)/shard_map/ppermute | solution.py:301
  103.4 6.2 %collective-permute-start.44 = (f32[264,128]{1,0:T(8,128)S(1)}, f32[264,128]{1,0:T(8,128)S(1)}, u32[]{:S(2)}, u32[]{:S(2)}) collective-permute-start(f32[264,128]{1,0:T(8,128)S(1)} %add_add_fusion.z0), channel_id=1, source_target_pairs={{0,96},{1,25},{2,98},{3,27},{4,100},{5,29},{6,102},{7,31},{8,104},... | collective-permute-start | bytes 405512 | tf_op jit(solution)/shard_map/ppermute | solution.py:301
  104.6 5.0 %collective-permute-start.43 = (f32[264,128]{1,0:T(8,128)S(1)}, f32[264,128]{1,0:T(8,128)S(1)}, u32[]{:S(2)}, u32[]{:S(2)}) collective-permute-start(f32[264,128]{1,0:T(8,128)S(1)} %add_add_fusion.z0), channel_id=1, source_target_pairs={{0,32},{1,9},{2,34},{3,11},{4,36},{5,13},{6,38},{7,15},{8,40},{9,1... | collective-permute-start | bytes 405512 | tf_op jit(solution)/shard_map/ppermute | solution.py:301
  (14 other events, 33.2 us)

commit v7 on v6

--- a/solution.py
+++ b/solution.py
@@ -16,7 +16,7 @@
 HERE = (0, 0)
 CHUNK = 1024
 STREAM = 256
-BUFFERS = 8
+BUFFERS = 6
 prio_power = 0.7
 weight_power = 0.5
 ridge_shift = 0.5
@@ -103,9 +103,10 @@
         pltpu.make_async_copy(features.at[pl.ds(c * STREAM, STREAM)], buf.at[c % BUFFERS], sem.at[c % BUFFERS])
         for c in range(steps)
     ]
-    for copy in small:
-        copy.start()
-    for c in range(BUFFERS):
+    small[0].start()
+    copies[0].start()
+    small[1].start()
+    for c in range(1, BUFFERS):
         copies[c].start()
     live = lax.broadcasted_iota(jnp.int32, (1, slots), 1) < count[0]
     small[0].wait()

time: 112 us -> 112 us (level)
  no operation moved by 1% of the time
where the time goes in v7:
time: 112 us
  starting transfers between devices  41.5 us (37%)
  waiting for transfers between devices  37.1 us (33%)
  Pallas kernels  31.5 us (28%)
  between operations  1.5 us (1%)
    ppermute x46, starting transfers between devices, exchange(): return lax.ppermute(value, ('rows', 'feat'), pairs)  41.5 us
    ppermute x46, waiting for transfers between devices, exchange(): return lax.ppermute(value, ('rows', 'feat'), pairs)  37.1 us
    pallas_call x21, Pallas kernels, call(): pl.pallas_call(kernel, out_shape=outs, in_specs=specs or [IN_VMEM] * len(...  31.5 us
  transfers between devices with their start and end apart: 46, of which 20 were waited for; matrix products, arithmetic and copies ran while one was open for 0% of the time, Pallas kernels for 15%

profile of v7, /device:TPU:0, one launch (start us, length us, event | category | flops | bytes accessed | tf_op | source)
XLA Modules:
  0.0 111.8 jit_solution(17111313093445528727)
XLA Ops:
  1.3 7.5 %k1.1 = (bf16[4096,1024]{1,0:T(8,128)(2,1)S(1)}, bf16[4096,1024]{1,0:T(8,128)(2,1)S(1)}, f32[1,4096]{1,0:T(1,128)S(1)}, f32[264,128]{1,0:T(8,128)S(1)}) custom-call(s32[1]{0:T(128)S(6)} %copy.6.count, s32[1,4096]{1,0:T(1,128)} %bitcast.1, f32[32,4096]{1,0:T(8,128)} %targets_hbm.1, f32[4096,1024]{1,0:T(8,128)} %features.1), custom_call_target="tpu_custom_call" | custom-call | flops 805306368 | bytes 16777216 | tf_op jit(solution)/shard_map/k1/pallas_call | solution.py:282
  8.7 4.0 %collective-permute-start.2 = (f32[264,128]{1,0:T(8,128)S(1)}, f32[264,128]{1,0:T(8,128)S(1)}, u32[]{:S(2)}, u32[]{:S(2)}) collective-permute-start(f32[264,128]{1,0:T(8,128)S(1)} %get-tuple-element.58), channel_id=1, source_target_pairs={{0,16},{1,65},{2,18},{3,67},{4,20},{5,69},{6,22},{7,71},{8,24},{9,... | collective-permute-start | bytes 405512 | tf_op jit(solution)/shard_map/ppermute | solution.py:302
  13.8 2.0 %collective-permute-done.2 = f32[264,128]{1,0:T(8,128)S(1)} collective-permute-done((f32[264,128]{1,0:T(8,128)S(1)}, f32[264,128]{1,0:T(8,128)S(1)}, u32[]{:S(2)}, u32[]{:S(2)}) %collective-permute-start.2) | collective-permute-done | bytes 135200 | tf_op jit(solution)/shard_map/ppermute | solution.py:302
  15.8 3.2 %collective-permute-done.1 = f32[264,128]{1,0:T(8,128)S(1)} collective-permute-done((f32[264,128]{1,0:T(8,128)S(1)}, f32[264,128]{1,0:T(8,128)S(1)}, u32[]{:S(2)}, u32[]{:S(2)}) %collective-permute-start.1) | collective-permute-done | bytes 135200 | tf_op jit(solution)/shard_map/ppermute | solution.py:302
  19.0 3.3 %collective-permute-start.5 = (f32[264,128]{1,0:T(8,128)S(1)}, f32[264,128]{1,0:T(8,128)S(1)}, u32[]{:S(2)}, u32[]{:S(2)}) collective-permute-start(f32[264,128]{1,0:T(8,128)S(1)} %add_add_fusion.2.p0), channel_id=1, source_target_pairs={{0,64},{1,17},{2,66},{3,19},{4,68},{5,21},{6,70},{7,23},{8,72},{9,... | collective-permute-start | bytes 405512 | tf_op jit(solution)/shard_map/ppermute | solution.py:302
  23.4 2.3 %collective-permute-done.5.p3 = f32[264,128]{1,0:T(8,128)S(1)} collective-permute-done((f32[264,128]{1,0:T(8,128)S(1)}, f32[264,128]{1,0:T(8,128)S(1)}, u32[]{:S(2)}, u32[]{:S(2)}) %collective-permute-start.5) | collective-permute-done | bytes 135200 | tf_op jit(solution)/shard_map/ppermute | solution.py:302
  25.6 2.9 %collective-permute-done.4.p2 = f32[264,128]{1,0:T(8,128)S(1)} collective-permute-done((f32[264,128]{1,0:T(8,128)S(1)}, f32[264,128]{1,0:T(8,128)S(1)}, u32[]{:S(2)}, u32[]{:S(2)}) %collective-permute-start.4) | collective-permute-done | bytes 135200 | tf_op jit(solution)/shard_map/ppermute | solution.py:302
  28.5 1.6 %k2.1 = (f32[32,1024]{1,0:T(8,128)S(1)}, f32[8,128]{1,0:T(8,128)S(1)}, bf16[64,1024]{1,0:T(8,128)(2,1)S(1)}, f32[8,128]{1,0:T(8,128)S(1)}, f32[136,128]{1,0:T(8,128)S(1)}, /*index=5*/f32[136,128]{1,0:T(8,128)S(1)}) custom-call(f32[264,128]{1,0:T(8,128)S(1)} %add_add_fusion.2.p0, f32[264,128]{1,0:T(8,128)S(1)} %collective-permute-done.3.p1, ...), custom_call_target="tpu_custom_call" | custom-call | flops 201326592 | bytes 4194304 | tf_op jit(solution)/shard_map/k2/pallas_call | solution.py:282
  33.5 3.1 %collective-permute-start.11 = (f32[136,128]{1,0:T(8,128)S(1)}, f32[136,128]{1,0:T(8,128)S(1)}, u32[]{:S(2)}, u32[]{:S(2)}) collective-permute-start(f32[136,128]{1,0:T(8,128)S(1)} %add.90), channel_id=1, source_target_pairs={{0,4},{1,5},{2,6},{3,7},{4,0},{5,1},{6,2},{7,3},{8,12},{9,13},{10,... | collective-permute-start | bytes 208904 | tf_op jit(solution)/shard_map/ppermute | solution.py:302
  39.6 2.6 %collective-permute-done.10 = f32[136,128]{1,0:T(8,128)S(1)} collective-permute-done((f32[136,128]{1,0:T(8,128)S(1)}, f32[136,128]{1,0:T(8,128)S(1)}, u32[]{:S(2)}, u32[]{:S(2)}) %collective-permute-start.10) | collective-permute-done | bytes 69664 | tf_op jit(solution)/shard_map/ppermute | solution.py:302
  42.4 2.0 %collective-permute-start.18 = (f32[128,128]{1,0:T(8,128)S(1)}, f32[128,128]{1,0:T(8,128)S(1)}, u32[]{:S(2)}, u32[]{:S(2)}) collective-permute-start(f32[128,128]{1,0:T(8,128)S(1)} %slice_add_fusion.2.near), channel_id=1, source_target_pairs={{0,4},{1,5},{2,6},{3,7},{4,0},{5,1},{6,2},{7,3},{8,12},{9,13},{10,... | collective-permute-start | bytes 196616 | tf_op jit(solution)/shard_map/ppermute | solution.py:302
  46.8 1.6 %collective-permute-done.18.near = f32[128,128]{1,0:T(8,128)S(1)} collective-permute-done((f32[128,128]{1,0:T(8,128)S(1)}, f32[128,128]{1,0:T(8,128)S(1)}, u32[]{:S(2)}, u32[]{:S(2)}) %collective-permute-start.18) | collective-permute-done | bytes 65568 | tf_op jit(solution)/shard_map/ppermute | solution.py:302
  48.4 1.5 %collective-permute-done.16.near = f32[128,128]{1,0:T(8,128)S(1)} collective-permute-done((f32[128,128]{1,0:T(8,128)S(1)}, f32[128,128]{1,0:T(8,128)S(1)}, u32[]{:S(2)}, u32[]{:S(2)}) %collective-permute-start.16) | collective-permute-done | bytes 65568 | tf_op jit(solution)/shard_map/ppermute | solution.py:302
  53.0 2.0 %collective-permute-start.22 = (f32[264,128]{1,0:T(8,128)S(1)}, f32[264,128]{1,0:T(8,128)S(1)}, u32[]{:S(2)}, u32[]{:S(2)}) collective-permute-start(f32[264,128]{1,0:T(8,128)S(1)} %get-tuple-element.80), channel_id=1, source_target_pairs={{0,16},{1,65},{2,18},{3,67},{4,20},{5,69},{6,22},{7,71},{8,24},{9,... | collective-permute-start | bytes 405512 | tf_op jit(solution)/shard_map/ppermute | solution.py:302
  56.6 3.0 %collective-permute-done.22 = f32[264,128]{1,0:T(8,128)S(1)} collective-permute-done((f32[264,128]{1,0:T(8,128)S(1)}, f32[264,128]{1,0:T(8,128)S(1)}, u32[]{:S(2)}, u32[]{:S(2)}) %collective-permute-start.22) | collective-permute-done | bytes 135200 | tf_op jit(solution)/shard_map/ppermute | solution.py:302
  59.6 1.6 %collective-permute-done.21 = f32[264,128]{1,0:T(8,128)S(1)} collective-permute-done((f32[264,128]{1,0:T(8,128)S(1)}, f32[264,128]{1,0:T(8,128)S(1)}, u32[]{:S(2)}, u32[]{:S(2)}) %collective-permute-start.21) | collective-permute-done | bytes 135200 | tf_op jit(solution)/shard_map/ppermute | solution.py:302
  61.3 1.6 %collective-permute-start.25 = (f32[264,128]{1,0:T(8,128)S(1)}, f32[264,128]{1,0:T(8,128)S(1)}, u32[]{:S(2)}, u32[]{:S(2)}) collective-permute-start(f32[264,128]{1,0:T(8,128)S(1)} %add_add_fusion.1.z0), channel_id=1, source_target_pairs={{0,64},{1,17},{2,66},{3,19},{4,68},{5,21},{6,70},{7,23},{8,72},{9,... | collective-permute-start | bytes 405512 | tf_op jit(solution)/shard_map/ppermute | solution.py:302
  62.9 1.4 %collective-permute-start.24 = (f32[264,128]{1,0:T(8,128)S(1)}, f32[264,128]{1,0:T(8,128)S(1)}, u32[]{:S(2)}, u32[]{:S(2)}) collective-permute-start(f32[264,128]{1,0:T(8,128)S(1)} %add_add_fusion.1.z0), channel_id=1, source_target_pairs={{0,96},{1,25},{2,98},{3,27},{4,100},{5,29},{6,102},{7,31},{8,104},... | collective-permute-start | bytes 405512 | tf_op jit(solution)/shard_map/ppermute | solution.py:302
  64.8 3.0 %collective-permute-done.25.z3 = f32[264,128]{1,0:T(8,128)S(1)} collective-permute-done((f32[264,128]{1,0:T(8,128)S(1)}, f32[264,128]{1,0:T(8,128)S(1)}, u32[]{:S(2)}, u32[]{:S(2)}) %collective-permute-start.25) | collective-permute-done | bytes 135200 | tf_op jit(solution)/shard_map/ppermute | solution.py:302
  67.9 1.4 %collective-permute-done.24.z2 = f32[264,128]{1,0:T(8,128)S(1)} collective-permute-done((f32[264,128]{1,0:T(8,128)S(1)}, f32[264,128]{1,0:T(8,128)S(1)}, u32[]{:S(2)}, u32[]{:S(2)}) %collective-permute-start.24) | collective-permute-done | bytes 135200 | tf_op jit(solution)/shard_map/ppermute | solution.py:302
  69.3 1.6 %k4.1 = (f32[32,1024]{1,0:T(8,128)S(1)}, f32[8,128]{1,0:T(8,128)S(1)}, bf16[64,1024]{1,0:T(8,128)(2,1)S(1)}, f32[16,128]{1,0:T(8,128)S(1)}, f32[144,128]{1,0:T(8,128)S(1)}, /*index=5*/f32[144,128]{1,0:T(8,128)S(1)}) custom-call(f32[264,128]{1,0:T(8,128)S(1)} %add_add_fusion.1.z0, f32[264,128]{1,0:T(8,128)S(1)} %collective-permute-done.23.z1, ...), custom_call_target="tpu_custom_call" | custom-call | flops 201326592 | bytes 4194304 | tf_op jit(solution)/shard_map/k4/pallas_call | solution.py:282
  74.3 1.7 %collective-permute-start.31 = (f32[144,128]{1,0:T(8,128)S(1)}, f32[144,128]{1,0:T(8,128)S(1)}, u32[]{:S(2)}, u32[]{:S(2)}) collective-permute-start(f32[144,128]{1,0:T(8,128)S(1)} %add.100), channel_id=1, source_target_pairs={{0,4},{1,5},{2,6},{3,7},{4,0},{5,1},{6,2},{7,3},{8,12},{9,13},{10,... | collective-permute-start | bytes 221192 | tf_op jit(solution)/shard_map/ppermute | solution.py:302
  76.0 1.4 %collective-permute-start.30 = (f32[144,128]{1,0:T(8,128)S(1)}, f32[144,128]{1,0:T(8,128)S(1)}, u32[]{:S(2)}, u32[]{:S(2)}) collective-permute-start(f32[144,128]{1,0:T(8,128)S(1)} %add.101), channel_id=1, source_target_pairs={{0,6},{1,7},{2,4},{3,5},{4,2},{5,3},{6,0},{7,1},{8,14},{9,15},{10,... | collective-permute-start | bytes 221192 | tf_op jit(solution)/shard_map/ppermute | solution.py:302
  82.0 1.9 %collective-permute-start.38 = (f32[128,128]{1,0:T(8,128)S(1)}, f32[128,128]{1,0:T(8,128)S(1)}, u32[]{:S(2)}, u32[]{:S(2)}) collective-permute-start(f32[128,128]{1,0:T(8,128)S(1)} %slice_add_fusion.near), channel_id=1, source_target_pairs={{0,4},{1,5},{2,6},{3,7},{4,0},{5,1},{6,2},{7,3},{8,12},{9,13},{10,... | collective-permute-start | bytes 196616 | tf_op jit(solution)/shard_map/ppermute | solution.py:302
  85.6 1.5 %solve_coef.1 = (f32[32,64]{1,0:T(8,128)S(1)}, f32[32,32]{1,0:T(8,128)S(1)}, f32[32,32]{1,0:T(8,128)S(1)}) custom-call(f32[8,128]{1,0:T(8,128)S(1)} %fusion.3.tile_b, f32[16,128]{1,0:T(8,128)S(1)} %fusion.2.tiles, f32[32,32]{1,0:T(8,128)S(1)} %first_step.1.step), custom_call_target="tpu_custom_call" | custom-call | flops 201326592 | bytes 4194304 | tf_op jit(solution)/shard_map/solve_coef/pallas_call | solution.py:282
  92.8 2.2 %collective-permute-start.42 = (f32[264,128]{1,0:T(8,128)S(1)}, f32[264,128]{1,0:T(8,128)S(1)}, u32[]{:S(2)}, u32[]{:S(2)}) collective-permute-start(f32[264,128]{1,0:T(8,128)S(1)} %mixed_back_kernel.7), channel_id=1, source_target_pairs={{0,16},{1,65},{2,18},{3,67},{4,20},{5,69},{6,22},{7,71},{8,24},{9,... | collective-permute-start | bytes 405512 | tf_op jit(solution)/shard_map/ppermute | solution.py:302
  96.3 3.0 %collective-permute-done.42 = f32[264,128]{1,0:T(8,128)S(1)} collective-permute-done((f32[264,128]{1,0:T(8,128)S(1)}, f32[264,128]{1,0:T(8,128)S(1)}, u32[]{:S(2)}, u32[]{:S(2)}) %collective-permute-start.42) | collective-permute-done | bytes 135200 | tf_op jit(solution)/shard_map/ppermute | solution.py:302
  99.3 1.9 %collective-permute-done.41 = f32[264,128]{1,0:T(8,128)S(1)} collective-permute-done((f32[264,128]{1,0:T(8,128)S(1)}, f32[264,128]{1,0:T(8,128)S(1)}, u32[]{:S(2)}, u32[]{:S(2)}) %collective-permute-start.41) | collective-permute-done | bytes 135200 | tf_op jit(solution)/shard_map/ppermute | solution.py:302
  101.3 2.1 %collective-permute-start.45 = (f32[264,128]{1,0:T(8,128)S(1)}, f32[264,128]{1,0:T(8,128)S(1)}, u32[]{:S(2)}, u32[]{:S(2)}) collective-permute-start(f32[264,128]{1,0:T(8,128)S(1)} %add_add_fusion.z0), channel_id=1, source_target_pairs={{0,64},{1,17},{2,66},{3,19},{4,68},{5,21},{6,70},{7,23},{8,72},{9,... | collective-permute-start | bytes 405512 | tf_op jit(solution)/shard_map/ppermute | solution.py:302
  105.5 2.3 %collective-permute-done.45.z3 = f32[264,128]{1,0:T(8,128)S(1)} collective-permute-done((f32[264,128]{1,0:T(8,128)S(1)}, f32[264,128]{1,0:T(8,128)S(1)}, u32[]{:S(2)}, u32[]{:S(2)}) %collective-permute-start.45) | collective-permute-done | bytes 135200 | tf_op jit(solution)/shard_map/ppermute | solution.py:302
  107.9 1.7 %collective-permute-done.44.z2 = f32[264,128]{1,0:T(8,128)S(1)} collective-permute-done((f32[264,128]{1,0:T(8,128)S(1)}, f32[264,128]{1,0:T(8,128)S(1)}, u32[]{:S(2)}, u32[]{:S(2)}) %collective-permute-start.44) | collective-permute-done | bytes 135200 | tf_op jit(solution)/shard_map/ppermute | solution.py:302
  109.5 2.2 %k6.1 = (f32[32,1024]{1,0:T(8,128)}, f32[32,1024]{1,0:T(8,128)}) custom-call(f32[264,128]{1,0:T(8,128)S(1)} %add_add_fusion.z0, f32[264,128]{1,0:T(8,128)S(1)} %collective-permute-done.43.z1, f32[264,128]{1,0:T(8,128)S(1)} %collective-permute-done.44.z2, f32[264,128]{1,0:T(8,128)S(1)} %collective-permute-done.45.z3, f32[8,128]{1,0:T(8,128)S(1)} %get-tuple-element.82.norm, ...), custom_call_target="tpu_custom_call" | custom-call | tf_op jit(solution)/shard_map/k6/pallas_call | solution.py:282
  (94 shorter events, 35.2 us)
Async XLA Ops:
  8.7 7.0 %collective-permute-start.2 = (f32[264,128]{1,0:T(8,128)S(1)}, f32[264,128]{1,0:T(8,128)S(1)}, u32[]{:S(2)}, u32[]{:S(2)}) collective-permute-start(f32[264,128]{1,0:T(8,128)S(1)} %get-tuple-element.58), channel_id=1, source_target_pairs={{0,16},{1,65},{2,18},{3,67},{4,20},{5,69},{6,22},{7,71},{8,24},{9,... | collective-permute-start | bytes 405512 | tf_op jit(solution)/shard_map/ppermute | solution.py:302
  12.8 6.2 %collective-permute-start.1 = (f32[264,128]{1,0:T(8,128)S(1)}, f32[264,128]{1,0:T(8,128)S(1)}, u32[]{:S(2)}, u32[]{:S(2)}) collective-permute-start(f32[264,128]{1,0:T(8,128)S(1)} %get-tuple-element.58), channel_id=1, source_target_pairs={{0,24},{1,97},{2,26},{3,99},{4,28},{5,101},{6,30},{7,103},{8,16},{... | collective-permute-start | bytes 405512 | tf_op jit(solution)/shard_map/ppermute | solution.py:302
  13.5 5.5 %collective-permute-start = (f32[264,128]{1,0:T(8,128)S(1)}, f32[264,128]{1,0:T(8,128)S(1)}, u32[]{:S(2)}, u32[]{:S(2)}) collective-permute-start(f32[264,128]{1,0:T(8,128)S(1)} %get-tuple-element.58), channel_id=1, source_target_pairs={{0,8},{1,33},{2,10},{3,35},{4,12},{5,37},{6,14},{7,39},{8,0},{9,41... | collective-permute-start | bytes 405512 | tf_op jit(solution)/shard_map/ppermute | solution.py:302
  19.0 6.6 %collective-permute-start.5 = (f32[264,128]{1,0:T(8,128)S(1)}, f32[264,128]{1,0:T(8,128)S(1)}, u32[]{:S(2)}, u32[]{:S(2)}) collective-permute-start(f32[264,128]{1,0:T(8,128)S(1)} %add_add_fusion.2.p0), channel_id=1, source_target_pairs={{0,64},{1,17},{2,66},{3,19},{4,68},{5,21},{6,70},{7,23},{8,72},{9,... | collective-permute-start | bytes 405512 | tf_op jit(solution)/shard_map/ppermute | solution.py:302
  22.3 6.2 %collective-permute-start.4 = (f32[264,128]{1,0:T(8,128)S(1)}, f32[264,128]{1,0:T(8,128)S(1)}, u32[]{:S(2)}, u32[]{:S(2)}) collective-permute-start(f32[264,128]{1,0:T(8,128)S(1)} %add_add_fusion.2.p0), channel_id=1, source_target_pairs={{0,96},{1,25},{2,98},{3,27},{4,100},{5,29},{6,102},{7,31},{8,104},... | collective-permute-start | bytes 405512 | tf_op jit(solution)/shard_map/ppermute | solution.py:302
  23.4 5.2 %collective-permute-start.3 = (f32[264,128]{1,0:T(8,128)S(1)}, f32[264,128]{1,0:T(8,128)S(1)}, u32[]{:S(2)}, u32[]{:S(2)}) collective-permute-start(f32[264,128]{1,0:T(8,128)S(1)} %add_add_fusion.2.p0), channel_id=1, source_target_pairs={{0,32},{1,9},{2,34},{3,11},{4,36},{5,13},{6,38},{7,15},{8,40},{9,1... | collective-permute-start | bytes 405512 | tf_op jit(solution)/shard_map/ppermute | solution.py:302
  31.6 5.1 %collective-permute-start.7 = (f32[136,128]{1,0:T(8,128)S(1)}, f32[136,128]{1,0:T(8,128)S(1)}, u32[]{:S(2)}, u32[]{:S(2)}) collective-permute-start(f32[136,128]{1,0:T(8,128)S(1)} %get-tuple-element.66), channel_id=1, source_target_pairs={{0,1},{1,0},{2,3},{3,2},{4,5},{5,4},{6,7},{7,6},{8,9},{9,8},{10,11... | collective-permute-start | bytes 208904 | tf_op jit(solution)/shard_map/ppermute | solution.py:302
  33.5 4.4 %collective-permute-start.8 = (f32[136,128]{1,0:T(8,128)S(1)}, f32[136,128]{1,0:T(8,128)S(1)}, u32[]{:S(2)}, u32[]{:S(2)}) collective-permute-start(f32[136,128]{1,0:T(8,128)S(1)} %get-tuple-element.69), channel_id=1, source_target_pairs={{0,1},{1,0},{2,3},{3,2},{4,5},{5,4},{6,7},{7,6},{8,9},{9,8},{10,11... | collective-permute-start | bytes 208904 | tf_op jit(solution)/shard_map/ppermute | solution.py:302
  33.5 6.1 %collective-permute-start.11 = (f32[136,128]{1,0:T(8,128)S(1)}, f32[136,128]{1,0:T(8,128)S(1)}, u32[]{:S(2)}, u32[]{:S(2)}) collective-permute-start(f32[136,128]{1,0:T(8,128)S(1)} %add.90), channel_id=1, source_target_pairs={{0,4},{1,5},{2,6},{3,7},{4,0},{5,1},{6,2},{7,3},{8,12},{9,13},{10,... | collective-permute-start | bytes 208904 | tf_op jit(solution)/shard_map/ppermute | solution.py:302
  36.6 5.6 %collective-permute-start.10 = (f32[136,128]{1,0:T(8,128)S(1)}, f32[136,128]{1,0:T(8,128)S(1)}, u32[]{:S(2)}, u32[]{:S(2)}) collective-permute-start(f32[136,128]{1,0:T(8,128)S(1)} %add.91), channel_id=1, source_target_pairs={{0,6},{1,7},{2,4},{3,5},{4,2},{5,3},{6,0},{7,1},{8,14},{9,15},{10,... | collective-permute-start | bytes 208904 | tf_op jit(solution)/shard_map/ppermute | solution.py:302
  37.9 4.4 %collective-permute-start.9 = (f32[136,128]{1,0:T(8,128)S(1)}, f32[136,128]{1,0:T(8,128)S(1)}, u32[]{:S(2)}, u32[]{:S(2)}) collective-permute-start(f32[136,128]{1,0:T(8,128)S(1)} %add.92), channel_id=1, source_target_pairs={{0,2},{1,3},{2,0},{3,1},{4,6},{5,7},{6,4},{7,5},{8,10},{9,11},{10,... | collective-permute-start | bytes 208904 | tf_op jit(solution)/shard_map/ppermute | solution.py:302
  42.4 6.0 %collective-permute-start.18 = (f32[128,128]{1,0:T(8,128)S(1)}, f32[128,128]{1,0:T(8,128)S(1)}, u32[]{:S(2)}, u32[]{:S(2)}) collective-permute-start(f32[128,128]{1,0:T(8,128)S(1)} %slice_add_fusion.2.near), channel_id=1, source_target_pairs={{0,4},{1,5},{2,6},{3,7},{4,0},{5,1},{6,2},{7,3},{8,12},{9,13},{10,... | collective-permute-start | bytes 196616 | tf_op jit(solution)/shard_map/ppermute | solution.py:302
  44.4 5.5 %collective-permute-start.16 = (f32[128,128]{1,0:T(8,128)S(1)}, f32[128,128]{1,0:T(8,128)S(1)}, u32[]{:S(2)}, u32[]{:S(2)}) collective-permute-start(f32[128,128]{1,0:T(8,128)S(1)} %slice_add_fusion.2.near), channel_id=1, source_target_pairs={{0,6},{1,7},{2,4},{3,5},{4,2},{5,3},{6,0},{7,1},{8,14},{9,15},{10,... | collective-permute-start | bytes 196616 | tf_op jit(solution)/shard_map/ppermute | solution.py:302
  45.6 4.3 %collective-permute-start.13 = (f32[128,128]{1,0:T(8,128)S(1)}, f32[128,128]{1,0:T(8,128)S(1)}, u32[]{:S(2)}, u32[]{:S(2)}) collective-permute-start(f32[128,128]{1,0:T(8,128)S(1)} %slice_add_fusion.2.near), channel_id=1, source_target_pairs={{0,2},{1,3},{2,0},{3,1},{4,6},{5,7},{6,4},{7,5},{8,10},{9,11},{10,... | collective-permute-start | bytes 196616 | tf_op jit(solution)/shard_map/ppermute | solution.py:302
  53.0 6.6 %collective-permute-start.22 = (f32[264,128]{1,0:T(8,128)S(1)}, f32[264,128]{1,0:T(8,128)S(1)}, u32[]{:S(2)}, u32[]{:S(2)}) collective-permute-start(f32[264,128]{1,0:T(8,128)S(1)} %get-tuple-element.80), channel_id=1, source_target_pairs={{0,16},{1,65},{2,18},{3,67},{4,20},{5,69},{6,22},{7,71},{8,24},{9,... | collective-permute-start | bytes 405512 | tf_op jit(solution)/shard_map/ppermute | solution.py:302
  55.0 6.2 %collective-permute-start.21 = (f32[264,128]{1,0:T(8,128)S(1)}, f32[264,128]{1,0:T(8,128)S(1)}, u32[]{:S(2)}, u32[]{:S(2)}) collective-permute-start(f32[264,128]{1,0:T(8,128)S(1)} %get-tuple-element.80), channel_id=1, source_target_pairs={{0,24},{1,97},{2,26},{3,99},{4,28},{5,101},{6,30},{7,103},{8,16},{... | collective-permute-start | bytes 405512 | tf_op jit(solution)/shard_map/ppermute | solution.py:302
  56.1 5.2 %collective-permute-start.20 = (f32[264,128]{1,0:T(8,128)S(1)}, f32[264,128]{1,0:T(8,128)S(1)}, u32[]{:S(2)}, u32[]{:S(2)}) collective-permute-start(f32[264,128]{1,0:T(8,128)S(1)} %get-tuple-element.80), channel_id=1, source_target_pairs={{0,8},{1,33},{2,10},{3,35},{4,12},{5,37},{6,14},{7,39},{8,0},{9,41... | collective-permute-start | bytes 405512 | tf_op jit(solution)/shard_map/ppermute | solution.py:302
  61.3 6.6 %collective-permute-start.25 = (f32[264,128]{1,0:T(8,128)S(1)}, f32[264,128]{1,0:T(8,128)S(1)}, u32[]{:S(2)}, u32[]{:S(2)}) collective-permute-start(f32[264,128]{1,0:T(8,128)S(1)} %add_add_fusion.1.z0), channel_id=1, source_target_pairs={{0,64},{1,17},{2,66},{3,19},{4,68},{5,21},{6,70},{7,23},{8,72},{9,... | collective-permute-start | bytes 405512 | tf_op jit(solution)/shard_map/ppermute | solution.py:302
  62.9 6.4 %collective-permute-start.24 = (f32[264,128]{1,0:T(8,128)S(1)}, f32[264,128]{1,0:T(8,128)S(1)}, u32[]{:S(2)}, u32[]{:S(2)}) collective-permute-start(f32[264,128]{1,0:T(8,128)S(1)} %add_add_fusion.1.z0), channel_id=1, source_target_pairs={{0,96},{1,25},{2,98},{3,27},{4,100},{5,29},{6,102},{7,31},{8,104},... | collective-permute-start | bytes 405512 | tf_op jit(solution)/shard_map/ppermute | solution.py:302
  64.3 5.0 %collective-permute-start.23 = (f32[264,128]{1,0:T(8,128)S(1)}, f32[264,128]{1,0:T(8,128)S(1)}, u32[]{:S(2)}, u32[]{:S(2)}) collective-permute-start(f32[264,128]{1,0:T(8,128)S(1)} %add_add_fusion.1.z0), channel_id=1, source_target_pairs={{0,32},{1,9},{2,34},{3,11},{4,36},{5,13},{6,38},{7,15},{8,40},{9,1... | collective-permute-start | bytes 405512 | tf_op jit(solution)/shard_map/ppermute | solution.py:302
  74.3 7.6 %collective-permute-start.31 = (f32[144,128]{1,0:T(8,128)S(1)}, f32[144,128]{1,0:T(8,128)S(1)}, u32[]{:S(2)}, u32[]{:S(2)}) collective-permute-start(f32[144,128]{1,0:T(8,128)S(1)} %add.100), channel_id=1, source_target_pairs={{0,4},{1,5},{2,6},{3,7},{4,0},{5,1},{6,2},{7,3},{8,12},{9,13},{10,... | collective-permute-start | bytes 221192 | tf_op jit(solution)/shard_map/ppermute | solution.py:302
  76.0 6.0 %collective-permute-start.30 = (f32[144,128]{1,0:T(8,128)S(1)}, f32[144,128]{1,0:T(8,128)S(1)}, u32[]{:S(2)}, u32[]{:S(2)}) collective-permute-start(f32[144,128]{1,0:T(8,128)S(1)} %add.101), channel_id=1, source_target_pairs={{0,6},{1,7},{2,4},{3,5},{4,2},{5,3},{6,0},{7,1},{8,14},{9,15},{10,... | collective-permute-start | bytes 221192 | tf_op jit(solution)/shard_map/ppermute | solution.py:302
  77.4 4.4 %collective-permute-start.29 = (f32[144,128]{1,0:T(8,128)S(1)}, f32[144,128]{1,0:T(8,128)S(1)}, u32[]{:S(2)}, u32[]{:S(2)}) collective-permute-start(f32[144,128]{1,0:T(8,128)S(1)} %add.102), channel_id=1, source_target_pairs={{0,2},{1,3},{2,0},{3,1},{4,6},{5,7},{6,4},{7,5},{8,10},{9,11},{10,... | collective-permute-start | bytes 221192 | tf_op jit(solution)/shard_map/ppermute | solution.py:302
  82.0 6.1 %collective-permute-start.38 = (f32[128,128]{1,0:T(8,128)S(1)}, f32[128,128]{1,0:T(8,128)S(1)}, u32[]{:S(2)}, u32[]{:S(2)}) collective-permute-start(f32[128,128]{1,0:T(8,128)S(1)} %slice_add_fusion.near), channel_id=1, source_target_pairs={{0,4},{1,5},{2,6},{3,7},{4,0},{5,1},{6,2},{7,3},{8,12},{9,13},{10,... | collective-permute-start | bytes 196616 | tf_op jit(solution)/shard_map/ppermute | solution.py:302
  83.9 5.5 %collective-permute-start.36 = (f32[128,128]{1,0:T(8,128)S(1)}, f32[128,128]{1,0:T(8,128)S(1)}, u32[]{:S(2)}, u32[]{:S(2)}) collective-permute-start(f32[128,128]{1,0:T(8,128)S(1)} %slice_add_fusion.near), channel_id=1, source_target_pairs={{0,6},{1,7},{2,4},{3,5},{4,2},{5,3},{6,0},{7,1},{8,14},{9,15},{10,... | collective-permute-start | bytes 196616 | tf_op jit(solution)/shard_map/ppermute | solution.py:302
  85.2 4.5 %collective-permute-start.33 = (f32[128,128]{1,0:T(8,128)S(1)}, f32[128,128]{1,0:T(8,128)S(1)}, u32[]{:S(2)}, u32[]{:S(2)}) collective-permute-start(f32[128,128]{1,0:T(8,128)S(1)} %slice_add_fusion.near), channel_id=1, source_target_pairs={{0,2},{1,3},{2,0},{3,1},{4,6},{5,7},{6,4},{7,5},{8,10},{9,11},{10,... | collective-permute-start | bytes 196616 | tf_op jit(solution)/shard_map/ppermute | solution.py:302
  92.8 6.6 %collective-permute-start.42 = (f32[264,128]{1,0:T(8,128)S(1)}, f32[264,128]{1,0:T(8,128)S(1)}, u32[]{:S(2)}, u32[]{:S(2)}) collective-permute-start(f32[264,128]{1,0:T(8,128)S(1)} %mixed_back_kernel.7), channel_id=1, source_target_pairs={{0,16},{1,65},{2,18},{3,67},{4,20},{5,69},{6,22},{7,71},{8,24},{9,... | collective-permute-start | bytes 405512 | tf_op jit(solution)/shard_map/ppermute | solution.py:302
  95.0 6.2 %collective-permute-start.41 = (f32[264,128]{1,0:T(8,128)S(1)}, f32[264,128]{1,0:T(8,128)S(1)}, u32[]{:S(2)}, u32[]{:S(2)}) collective-permute-start(f32[264,128]{1,0:T(8,128)S(1)} %mixed_back_kernel.7), channel_id=1, source_target_pairs={{0,24},{1,97},{2,26},{3,99},{4,28},{5,101},{6,30},{7,103},{8,16},{... | collective-permute-start | bytes 405512 | tf_op jit(solution)/shard_map/ppermute | solution.py:302
  95.9 5.3 %collective-permute-start.40 = (f32[264,128]{1,0:T(8,128)S(1)}, f32[264,128]{1,0:T(8,128)S(1)}, u32[]{:S(2)}, u32[]{:S(2)}) collective-permute-start(f32[264,128]{1,0:T(8,128)S(1)} %mixed_back_kernel.7), channel_id=1, source_target_pairs={{0,8},{1,33},{2,10},{3,35},{4,12},{5,37},{6,14},{7,39},{8,0},{9,41... | collective-permute-start | bytes 405512 | tf_op jit(solution)/shard_map/ppermute | solution.py:302
  101.3 6.6 %collective-permute-start.45 = (f32[264,128]{1,0:T(8,128)S(1)}, f32[264,128]{1,0:T(8,128)S(1)}, u32[]{:S(2)}, u32[]{:S(2)}) collective-permute-start(f32[264,128]{1,0:T(8,128)S(1)} %add_add_fusion.z0), channel_id=1, source_target_pairs={{0,64},{1,17},{2,66},{3,19},{4,68},{5,21},{6,70},{7,23},{8,72},{9,... | collective-permute-start | bytes 405512 | tf_op jit(solution)/shard_map/ppermute | solution.py:302
  103.3 6.2 %collective-permute-start.44 = (f32[264,128]{1,0:T(8,128)S(1)}, f32[264,128]{1,0:T(8,128)S(1)}, u32[]{:S(2)}, u32[]{:S(2)}) collective-permute-start(f32[264,128]{1,0:T(8,128)S(1)} %add_add_fusion.z0), channel_id=1, source_target_pairs={{0,96},{1,25},{2,98},{3,27},{4,100},{5,29},{6,102},{7,31},{8,104},... | collective-permute-start | bytes 405512 | tf_op jit(solution)/shard_map/ppermute | solution.py:302
  104.5 5.0 %collective-permute-start.43 = (f32[264,128]{1,0:T(8,128)S(1)}, f32[264,128]{1,0:T(8,128)S(1)}, u32[]{:S(2)}, u32[]{:S(2)}) collective-permute-start(f32[264,128]{1,0:T(8,128)S(1)} %add_add_fusion.z0), channel_id=1, source_target_pairs={{0,32},{1,9},{2,34},{3,11},{4,36},{5,13},{6,38},{7,15},{8,40},{9,1... | collective-permute-start | bytes 405512 | tf_op jit(solution)/shard_map/ppermute | solution.py:302
  (14 other events, 33.2 us)
